TPU v7x, 256 devices: a whole 4x4x8 slice. The times are simulated.
256 devices in a mesh: var: 32 (over z_lo, x, core), tp: 8 (over z_hi, y).
Axes of the slice: x: 4, y: 4, z: 8 (z_hi: 2, z_lo: 4; z = z_hi * 4 + z_lo), core: 2. Of those that a mesh axis runs over, the one named last changes fastest.
Arguments:
- parent_inputs: bfloat16 [4096, 256], P('var'), may hold values from -6 to 6
- gate_parent: bfloat16 [4096, 7168], P('var', 'tp'), may hold values from -0.09375 to 0.09375
- up_parent: bfloat16 [4096, 7168], P('var', 'tp'), may hold values from -0.09375 to 0.09375
- down_parent: bfloat16 [7168, 4096], P('tp', 'var'), may hold values from -0.0625 to 0.0625
- targets: bfloat16 [256, 4096], P('var', 'tp'), may hold values from -6 to 6
- widths: int32 [32], P('var'), may hold values from 1792 to 7168, as said below
- gains: float32 [32, 7168], P('var', 'tp'), may hold values from 0.25 to 2
Outputs:
- down_grad: bfloat16 [32, 7168, 4096], P('var', 'tp')
- gain_grad: float32 [32, 7168], P('var', 'tp')
Inputs may be any that keep to these rules, and one draw needn't show every extreme that they name: `widths`: every draw has a variant of exactly 7168 and one of exactly 1792 kept hidden units.
All inputs are finite; a program needn't handle non-finite values.
Results may differ from a plain program's by a relative error of at most 0.0059.
Values may be sent and summed in bfloat16 or wider, within the bound.
No kernel may reach another device: no remote copies, remote signals or barrier semaphores. Data moves between devices by JAX's collectives and lax.ppermute only.
A program may use at most 128 MiB of HBM per device.

v0:
```python
import jax
import jax.numpy as jnp
from jax import lax
from jax.sharding import PartitionSpec as P


def local(parent_inputs, gate_parent, up_parent, down_parent, targets, widths, gains):
    contract_rows = (((0,), (0,)), ((), ()))
    rows = parent_inputs.shape[1]
    local_ff = gate_parent.shape[1]
    feats = lax.all_gather(parent_inputs, "var", axis=0, tiled=True)
    gate_piece = lax.all_gather(gate_parent, "var", axis=0, tiled=True)
    up_piece = lax.all_gather(up_parent, "var", axis=0, tiled=True)
    gate_sum = lax.dot_general(feats, gate_piece, contract_rows, preferred_element_type=jnp.float32)
    up_sum = lax.dot_general(feats, up_piece, contract_rows, preferred_element_type=jnp.float32)
    raw = jax.nn.silu(gate_sum) * up_sum
    column = lax.axis_index("tp") * local_ff + lax.broadcasted_iota(jnp.int32, (1, local_ff), 1)
    kept = (column < widths[0]).astype(jnp.float32)
    hidden = (raw * gains * kept).astype(jnp.bfloat16)
    down_whole = lax.all_gather(down_parent, "var", axis=1, tiled=True)
    partial_value = jnp.dot(hidden, down_whole, preferred_element_type=jnp.float32)
    target_part = lax.all_gather(targets, "var", axis=0, tiled=True)
    output = lax.psum(partial_value, "tp")
    target_whole = lax.all_gather(target_part, "tp", axis=1, tiled=True)
    residual = (output - target_whole.astype(jnp.float32)).astype(jnp.bfloat16)
    scale = 1.0 / rows**0.5
    grad_down = lax.dot_general(hidden, residual, contract_rows, preferred_element_type=jnp.float32)
    grad_down = (grad_down * scale).astype(jnp.bfloat16)[None]
    back = lax.dot_general(
        residual, down_whole, (((1,), (1,)), ((), ())), preferred_element_type=jnp.float32
    )
    grad_gain = kept * jnp.sum(raw * back, axis=0, keepdims=True) * scale
    return (grad_down, grad_gain)


def solution(mesh):
    return jax.shard_map(
        local,
        mesh=mesh,
        in_specs=(
            P("var", None),
            P("var", "tp"),
            P("var", "tp"),
            P("tp", "var"),
            P("var", "tp"),
            P("var"),
            P("var", "tp"),
        ),
        out_specs=(P("var", "tp", None), P("var", "tp")),
        check_vma=False,
    )
```

profile of v0, /device:TPU:2, one launch (start us, length us, event | category | flops | bytes accessed | tf_op | source)
XLA Modules:
  0.0 588.8 jit_solution(13577693330374438191)
XLA Ops:
  7.2 0.0 all-gather.6.cloned.1.call-start
  7.2 0.7 all-gather.6.cloned.1.call-update
  7.9 0.0 all-gather.8.cloned.1.call-start
  7.9 0.7 all-gather.8.cloned.1.call-update
  8.6 0.0 all-gather.10.cloned.1.call-start
  8.7 0.7 all-gather.10.cloned.1.call-update
  9.4 0.0 all-gather.12.cloned.1.call-start
  9.4 0.5 all-gather.12.cloned.1.call-update
  10.0 0.0 all-gather.14.cloned.1.call-start
  10.0 43.6 %all_gather.22 = bf16[256,512]{1,0:T(8,128)(2,1)} all-gather(bf16[8,512]{1,0:T(8,128)(2,1)} %param.11), channel_id=1, replica_groups=mesh['var'=32,'tp'=8] {'var'}, dimensions={0}, use_global_device_ids=true | all-gather | bytes 270336 | tf_op jit(solution)/shard_map/all_gather | solution.py:22
  53.6 0.0 all-gather.14.cloned.1.call-update
  53.6 0.0 all-reduce.2.cloned.1.call-start
  54.3 0.7 reduce
  55.0 17.7 %all-gather.6.cloned.1.call-done = bf16[4096,256]{1,0:T(8,128)(2,1)} async-done(((bf16[128,256]{1,0:T(8,128)(2,1)}), bf16[4096,256]{1,0:T(8,128)(2,1)}) %all-gather.6.cloned.1.call-update) | async-done | bytes 2097168 | tf_op jit(solution)/shard_map/all_gather | solution.py:11
  72.8 0.0 copy-start
  72.8 68.9 %all-gather.8.cloned.1.call-done = bf16[4096,896]{1,0:T(8,128)(2,1)} async-done(((bf16[128,896]{1,0:T(8,128)(2,1)}), bf16[4096,896]{1,0:T(8,128)(2,1)}) %all-gather.8.cloned.1.call-update) | async-done | bytes 7340048 | tf_op jit(solution)/shard_map/all_gather | solution.py:12
  141.7 7.0 %fusion.5 = f32[256,896]{1,0:T(8,128)} fusion(bf16[4096,256]{1,0:T(8,128)(2,1)} %all-gather.6.cloned.1.call-done, bf16[4096,896]{1,0:T(8,128)(2,1)} %all-gather.8.cloned.1.call-done), kind=kOutput, calls=%fused_computation.12 | convolution fusion | flops 1879048192 | bytes 10354688 | tf_op jit(solution)/shard_map/dot_general | solution.py:14
  148.7 61.7 %all-gather.10.cloned.1.call-done = bf16[4096,896]{1,0:T(8,128)(2,1)} async-done(((bf16[128,896]{1,0:T(8,128)(2,1)}), bf16[4096,896]{1,0:T(8,128)(2,1)}) %all-gather.10.cloned.1.call-update) | async-done | bytes 7340048 | tf_op jit(solution)/shard_map/all_gather | solution.py:13
  210.4 0.0 copy-done
  210.4 5.7 convolution_multiply_fusion.1
  216.1 77.7 %all-gather.12.cloned.1.call-done = bf16[896,4096]{1,0:T(8,128)(2,1)} async-done(((bf16[896,128]{1,0:T(8,128)(2,1)}), bf16[896,4096]{1,0:T(8,128)(2,1)}) %all-gather.12.cloned.1.call-update) | async-done | bytes 7340048 | tf_op jit(solution)/shard_map/all_gather | solution.py:20
  293.8 7.4 %fusion.2 = f32[256,4096]{1,0:T(8,128)} fusion(bf16[896,4096]{1,0:T(8,128)(2,1)} %all-gather.12.cloned.1.call-done, f32[256,896]{1,0:T(8,128)S(1)} %convolution_multiply_fusion.1, f32[896]{0:T(1024)S(1)} %fusion.3, f32[896]{0:T(1024)S(1)} %reduce), kind=kOutput, calls=%fused_computation.7 | convolution fusion | flops 1879736320 | bytes 12459008 | tf_op jit(solution)/shard_map/dot_general | solution.py:21
  301.2 0.0 all-reduce.2.cloned.1.call-update
  301.2 70.7 %all-gather.14.cloned.1.call-done = bf16[256,4096]{1,0:T(8,128)(2,1)} async-done(((bf16[256,512]{1,0:T(8,128)(2,1)}), bf16[256,4096]{1,0:T(8,128)(2,1)}) %all-gather.14.cloned.1.call-update) | async-done | bytes 2097168 | tf_op jit(solution)/shard_map/all_gather | solution.py:24
  371.9 0.0 copy-start.2
  371.9 196.7 %all-reduce.2.cloned.1.call-done = f32[256,4096]{1,0:T(8,128)} async-done(((f32[256,4096]{1,0:T(8,128)}), f32[256,4096]{1,0:T(8,128)}) %all-reduce.2.cloned.1.call-update) | async-done | bytes 4194320 | tf_op jit(solution)/shard_map/psum | solution.py:23
  568.7 0.0 copy-start.1
  568.7 7.4 %fusion.1 = f32[896]{0:T(1024)S(1)} fusion(f32[256,896]{1,0:T(8,128)S(1)} %convolution_multiply_fusion.1, bf16[896,4096]{1,0:T(8,128)(2,1)} %all-gather.12.cloned.1.call-done, f32[256,4096]{1,0:T(8,128)} %all-reduce.2.cloned.1.call-done, bf16[256,4096]{1,0:T(8,128)(2,1)} %all-gather.14.cloned.1.call-done), kind=kOutput, calls=%fused_computation.5 | convolution fusion | flops 1882651776 | bytes 14552576 | tf_op jit(solution)/shard_map/dot_general | solution.py:29
  576.1 0.6 fusion.4
  576.7 0.0 copy-done.2
  576.7 0.0 copy-done.1
  576.7 5.2 fusion
  (1 shorter events, 0.0 us)
Async XLA Ops:
  7.2 65.6 %all-gather.6.cloned.1.call-start = ((), (), s32[]{:S(2)}) async-start(), calls=%async_computation | async-start | bytes 2162688 | tf_op jit(solution)/shard_map/all_gather | solution.py:11
  7.9 133.8 %all-gather.8.cloned.1.call-start = ((), (), s32[]{:S(2)}) async-start(), calls=%async_computation.1 | async-start | bytes 7569408 | tf_op jit(solution)/shard_map/all_gather | solution.py:12
  8.6 201.8 %all-gather.10.cloned.1.call-start = ((), (), s32[]{:S(2)}) async-start(), calls=%async_computation.2 | async-start | bytes 7569408 | tf_op jit(solution)/shard_map/all_gather | solution.py:13
  9.4 284.4 %all-gather.12.cloned.1.call-start = ((), (), s32[]{:S(2)}) async-start(), calls=%async_computation.3 | async-start | bytes 7569408 | tf_op jit(solution)/shard_map/all_gather | solution.py:20
  10.0 362.0 %all-gather.14.cloned.1.call-start = ((), (), s32[]{:S(2)}) async-start(), calls=%async_computation.5 | async-start | bytes 2359296 | tf_op jit(solution)/shard_map/all_gather | solution.py:24
  53.6 515.1 %all-reduce.2.cloned.1.call-start = ((), (), s32[]{:S(2)}) async-start(), calls=%async_computation.4 | async-start | bytes 8388608 | tf_op jit(solution)/shard_map/psum | solution.py:23
  72.8 137.6 %copy-start = (bf16[4096,256]{1,0:T(8,128)(2,1)S(1)}, bf16[4096,256]{1,0:T(8,128)(2,1)}, u32[]{:S(2)}) copy-start(bf16[4096,256]{1,0:T(8,128)(2,1)} %all-gather.6.cloned.1.call-done) | copy-start | bytes 6291460
  371.9 204.8 %copy-start.2 = (bf16[256,4096]{1,0:T(8,128)(2,1)S(1)}, bf16[256,4096]{1,0:T(8,128)(2,1)}, u32[]{:S(2)}) copy-start(bf16[256,4096]{1,0:T(8,128)(2,1)} %all-gather.14.cloned.1.call-done) | copy-start | bytes 6291460
  568.7 8.1 %copy-start.1 = (f32[256,4096]{1,0:T(8,128)S(1)}, f32[256,4096]{1,0:T(8,128)}, u32[]{:S(2)}) copy-start(f32[256,4096]{1,0:T(8,128)} %all-reduce.2.cloned.1.call-done) | copy-start | bytes 12582916
Sparse Core Ops, SparseCore 0:
  9.9 62.8 all-gather.5
  74.6 66.9 all-gather.7
  143.5 66.8 all-gather.9
  212.0 81.7 all-gather.11
  296.1 75.8 all-gather.13
  375.0 193.6 all-reduce.1
where the time goes:
time: 590 us; the launch traced here: 589 us
  waiting for transfers between devices  496 us (84%)
  blocking collectives  43.6 us (7%)
  matrix products  32.8 us (6%)
  between operations  14.8 us (3%)
    psum x1, waiting for transfers between devices, local(): output = lax.psum(partial_value, 'tp')  197 us
    all_gather x1, waiting for transfers between devices, local(): down_whole = lax.all_gather(down_parent, 'var', axis=1, tiled=True)  77.7 us
    all_gather x1, waiting for transfers between devices, local(): target_whole = lax.all_gather(target_part, 'tp', axis=1, tiled=True)  70.7 us
    all_gather x1, waiting for transfers between devices, local(): gate_piece = lax.all_gather(gate_parent, 'var', axis=0, tiled=True)  68.9 us
    all_gather x1, waiting for transfers between devices, local(): up_piece = lax.all_gather(up_parent, 'var', axis=0, tiled=True)  61.7 us
    all_gather x1, blocking collectives, local(): target_part = lax.all_gather(targets, 'var', axis=0, tiled=True)  43.6 us
    all_gather x1, waiting for transfers between devices, local(): feats = lax.all_gather(parent_inputs, 'var', axis=0, tiled=True)  17.7 us
  transfers between devices with their start and end apart: 6, of which 6 were waited for; matrix products, arithmetic and copies ran while one was open for 4% of the time, Pallas kernels for 0%

commit v1 on v0

v1 whole, which is shorter than its diff:
```python
import functools

import jax
import jax.numpy as jnp
from jax import lax
from jax.experimental import pallas as pl
from jax.experimental.pallas import tpu as pltpu
from jax.sharding import Mesh, PartitionSpec as P

SHAPE = (4, 4, 2, 2, 4)
AXES = ("zl", "x", "core", "zh", "y")
VAR = ("zl", "x", "core")
SIZE = dict(zip(AXES, SHAPE))
MIB = 1024 * 1024


def swap(value, axis, mask=1):
    return lax.ppermute(value, axis, [(i, i ^ mask) for i in range(SIZE[axis])])


def pick(stacked, places, axis=0):
    return jnp.stack([lax.dynamic_index_in_dim(stacked, p, axis, keepdims=False) for p in places], axis)


def gather4(value, axis):
    me = lax.axis_index(axis)
    near = jnp.stack([value] + [swap(value, axis, k) for k in (1, 2, 3)])
    return pick(near, [me ^ a for a in range(4)])


def gather_pair(value):
    other = swap(value, "core")
    first = lax.axis_index("core") == 0
    return jnp.stack([jnp.where(first, value, other), jnp.where(first, other, value)])


def gather_tp(value):
    far = swap(value, "zh")
    return [value] + [swap(value, "y", k) for k in (1, 2, 3)] + [far] + [swap(far, "y", k) for k in (1, 2, 3)]


def output_kernel(raw_ref, gain_ref, down_ref, target_ref, res_ref, hidden, total):
    step = pl.program_id(0)
    variants = gain_ref.shape[1]
    rows = raw_ref.shape[1]
    raw = raw_ref[0]
    for v in range(variants):
        hidden[v * rows : (v + 1) * rows, :] = (raw * gain_ref[0, v : v + 1, :]).astype(jnp.bfloat16)
    term = jnp.dot(hidden[...], down_ref[0], preferred_element_type=jnp.float32)

    @pl.when(step == 0)
    def _():
        total[...] = term

    @pl.when(step > 0)
    def _():
        total[...] += term

    @pl.when(step == pl.num_programs(0) - 1)
    def _():
        whole = total[...].reshape(variants, rows, total.shape[1])
        res_ref[...] = (whole - target_ref[...].astype(jnp.float32)[None]).astype(jnp.bfloat16)


def output_call(raw8, gain8, down8, target):
    pieces, rows, width = raw8.shape
    variants = gain8.shape[1]
    feats = down8.shape[2]
    return pl.pallas_call(
        output_kernel,
        grid=(pieces,),
        in_specs=[
            pl.BlockSpec((1, rows, width), lambda s: (s, 0, 0)),
            pl.BlockSpec((1, variants, width), lambda s: (s, 0, 0)),
            pl.BlockSpec((1, width, feats), lambda s: (s, 0, 0)),
            pl.BlockSpec((rows, feats), lambda s: (0, 0)),
        ],
        out_specs=pl.BlockSpec((variants, rows, feats), lambda s: (0, 0, 0)),
        out_shape=jax.ShapeDtypeStruct((variants, rows, feats), jnp.bfloat16),
        scratch_shapes=[
            pltpu.VMEM((variants * rows, width), jnp.bfloat16),
            pltpu.VMEM((variants * rows, feats), jnp.float32),
        ],
        compiler_params=pltpu.CompilerParams(vmem_limit_bytes=24 * MIB),
        cost_estimate=pl.CostEstimate(
            flops=2 * variants * rows * pieces * width * feats, bytes_accessed=4 * MIB, transcendentals=0
        ),
        name="output",
    )(raw8, gain8, down8, target)


def back_kernel(res_ref, raw_ref, down_ref, out_ref):
    variants, rows, feats = res_ref.shape
    width = raw_ref.shape[2]
    raw = raw_ref[0]
    some = 8
    for at in range(0, variants, some):
        res = res_ref[at : at + some].reshape(some * rows, feats)
        back = lax.dot_general(
            res, down_ref[0], (((1,), (1,)), ((), ())), preferred_element_type=jnp.float32
        )
        out_ref[0, at : at + some, :] = jnp.sum(back.reshape(some, rows, width) * raw[None], axis=1)


def back_call(res, raw8, down8):
    pieces, rows, width = raw8.shape
    variants, _, feats = res.shape
    return pl.pallas_call(
        back_kernel,
        grid=(pieces,),
        in_specs=[
            pl.BlockSpec((variants, rows, feats), lambda s: (0, 0, 0)),
            pl.BlockSpec((1, rows, width), lambda s: (s, 0, 0)),
            pl.BlockSpec((1, width, feats), lambda s: (s, 0, 0)),
        ],
        out_specs=pl.BlockSpec((1, variants, width), lambda s: (s, 0, 0)),
        out_shape=jax.ShapeDtypeStruct((pieces, variants, width), jnp.float32),
        compiler_params=pltpu.CompilerParams(vmem_limit_bytes=24 * MIB),
        cost_estimate=pl.CostEstimate(
            flops=2 * variants * rows * pieces * width * feats, bytes_accessed=4 * MIB, transcendentals=0
        ),
        name="back",
    )(res, raw8, down8)


def grad_kernel(scale, raw_ref, gain_ref, *refs):
    res_refs, out_ref, hidden_t, block = refs[:8], refs[8], refs[9], refs[10]
    rows = raw_ref.shape[1]
    some, feats = res_refs[0].shape[0], res_refs[0].shape[2]

    @pl.when(pl.program_id(0) == 0)
    def _():
        for p in range(8):
            hidden = (raw_ref[p] * gain_ref[...]).astype(jnp.bfloat16)
            block[p * rows : (p + 1) * rows, : hidden.shape[1]] = hidden
        hidden_t[...] = block[:, : hidden_t.shape[0]].T

    for p in range(8):
        for q in range(some):
            block[p * rows : (p + 1) * rows, q * feats : (q + 1) * feats] = res_refs[p][q]
    grad = jnp.dot(hidden_t[...], block[:, : some * feats], preferred_element_type=jnp.float32)
    out_ref[0] = (grad * scale).astype(jnp.bfloat16)


def grad_call(raw8, gain, res8, scale):
    pieces, rows, width = raw8.shape
    blocks, _, feats = res8[0].shape
    some = 4
    return pl.pallas_call(
        functools.partial(grad_kernel, scale),
        grid=(blocks // some,),
        in_specs=[
            pl.BlockSpec((pieces, rows, width), lambda s: (0, 0, 0)),
            pl.BlockSpec((1, width), lambda s: (0, 0)),
        ]
        + [pl.BlockSpec((some, rows, feats), lambda s: (s, 0, 0))] * 8,
        out_specs=pl.BlockSpec((1, width, some * feats), lambda s: (0, 0, s)),
        out_shape=jax.ShapeDtypeStruct((1, width, blocks * feats), jnp.bfloat16),
        scratch_shapes=[
            pltpu.VMEM((width, pieces * rows), jnp.bfloat16),
            pltpu.VMEM((pieces * rows, max(width, some * feats)), jnp.bfloat16),
        ],
        compiler_params=pltpu.CompilerParams(vmem_limit_bytes=24 * MIB),
        cost_estimate=pl.CostEstimate(
            flops=2 * pieces * rows * width * blocks * feats, bytes_accessed=10 * MIB, transcendentals=0
        ),
        name="grad",
    )(raw8, gain, *res8)


def target_part(targets):
    me = {a: lax.axis_index(a) for a in AXES}
    feats = targets.shape[1] // 4
    got = []
    for t in range(4):
        pairs = []
        for source in range(256):
            rest, y = divmod(source, 4)
            rest, zh = divmod(rest, 2)
            rest, core = divmod(rest, 2)
            zl, x = divmod(rest, 4)
            column = zl ^ t
            dest = zh * 2 + y // 2
            dest = dest * 4 + (y % 2) * 2 + column // 2
            dest = dest * 2 + column % 2
            dest = dest * 2 + core
            dest = dest * 4 + x
            pairs.append((source, dest))
        part = lax.dynamic_slice_in_dim(targets, (me["zl"] ^ t) * feats, feats, 1)
        got.append(lax.ppermute(part, AXES, pairs))
    column = (me["x"] % 2) * 2 + me["core"]
    return pick(jnp.stack(got), [column ^ a for a in range(4)]).reshape(-1, feats)


def local(inputs, gate, up, down, targets, widths, gains):
    me = {a: lax.axis_index(a) for a in AXES}
    first = me["core"] == 0
    rows = inputs.shape[1]
    width = gate.shape[1]
    scale = 1.0 / rows**0.5
    contract_rows = (((0,), (0,)), ((), ()))

    mine = jnp.where(first, gate, up)
    theirs = swap(jnp.where(first, up, gate), "core")
    inputs_other = swap(inputs, "core")

    column = (me["zh"] * 4 + me["y"]) * width + lax.broadcasted_iota(jnp.int32, (1, width), 1)
    kept = (column < widths[0]).astype(jnp.float32)
    gain = gains * kept
    all_gains = gather4(gather4(gather_pair(gain[0]), "x"), "zl").reshape(32, width)
    gain8 = jnp.stack(gather_tp(all_gains))
    down8 = jnp.stack(gather_tp(down))
    target = target_part(targets)

    part = lax.dot_general(inputs, mine, contract_rows, preferred_element_type=jnp.float32)
    part = part + lax.dot_general(inputs_other, theirs, contract_rows, preferred_element_type=jnp.float32)
    part = lax.all_to_all(part.reshape(16, rows // 16, width), ("x", "y"), 0, 0, tiled=True)
    part = jnp.sum(part.reshape(4, 4, 8, 2, width), axis=0)
    part = lax.all_to_all(part.transpose(1, 0, 2, 3), ("zh", "zl"), 0, 0, tiled=True)
    part = jnp.sum(part.reshape(2, 4, 4, 2, width), axis=1)
    other = swap(part, "core")
    raw = jax.nn.silu(jnp.where(first, part, other)) * jnp.where(first, other, part)
    raw = pick(raw, [me["zh"] ^ a for a in range(2)])
    raw = pick(raw, [me["y"] ^ k for k in range(4)], 1)
    raw = gather4(gather4(raw, "zl"), "x")
    raw8 = raw.transpose(2, 3, 0, 1, 4, 5).reshape(8, rows // 8, width)

    res = output_call(raw8, gain8, down8, target)
    res_own = lax.all_to_all(res, VAR, 0, 0, tiled=True)
    res8 = gather_tp(res_own)

    raw_tp = raw8.reshape(2, 4, rows // 8, width)
    raw_own = jnp.stack([raw_tp[:, 0]] + [swap(raw_tp[:, k], "y", k) for k in (1, 2, 3)], 1)
    raw_own = jnp.concatenate([raw_own[0], swap(raw_own[1], "zh")])

    grad_down = grad_call(raw_own, gain, res8, scale)

    sums = back_call(res, raw8, down8).reshape(2, 4, 32, width)
    sums = sums[:, 0] + swap(sums[:, 1], "y", 1) + swap(sums[:, 2], "y", 2) + swap(sums[:, 3], "y", 3)
    sums = sums[0] + swap(sums[1], "zh")
    sums = jnp.sum(lax.all_to_all(sums, VAR, 0, 0, tiled=True), axis=0, keepdims=True)
    return grad_down, kept * sums * scale


def solution(mesh):
    fine = Mesh(mesh.devices.reshape(SHAPE), AXES)
    tp = ("zh", "y")
    return jax.shard_map(
        local,
        mesh=fine,
        in_specs=(P(VAR, None), P(VAR, tp), P(VAR, tp), P(tp, VAR), P(VAR, tp), P(VAR), P(VAR, tp)),
        out_specs=(P(VAR, tp, None), P(VAR, tp)),
        check_vma=False,
    )
```

time: 590 us -> 266 us (0.45)
  waiting for transfers between devices: 496 us -> 89.7 us
  starting transfers between devices: 0.23 us -> 121 us
  blocking collectives: 43.6 us -> 0 us
  matrix products: 32.8 us -> 4.64 us
  local copies, waits for them, and re-layouts: 0.01 us -> 19.9 us
  Pallas kernels: 0 us -> 18.9 us
  between operations: 14.8 us -> 1.98 us
  other arithmetic: 1.3 us -> 8.43 us
    all_gather x5 -> x0, waiting for transfers between devices: 297 us -> none  [the longest x1 77.7 us: local(): down_whole = lax.all_gather(down_parent, 'var', axis=1, tiled=True)]
    psum x1 -> x0, waiting for transfers between devices: 197 us -> none  [local(): output = lax.psum(partial_value, 'tp')]
    ppermute x0 -> x49, starting transfers between devices: none -> 91.3 us  [the longest x45 72.9 us: swap(): return lax.ppermute(value, axis, [(i, i ^ mask) for i in range(SIZE[axis])])]
    ppermute x0 -> x49, waiting for transfers between devices: none -> 80.5 us  [the longest x45 80.5 us: swap(): return lax.ppermute(value, axis, [(i, i ^ mask) for i in range(SIZE[axis])])]
    all_gather x1 -> x0, blocking collectives: 43.6 us -> none  [local(): target_part = lax.all_gather(targets, 'var', axis=0, tiled=True)]
    all_to_all x0 -> x4, starting transfers between devices: none -> 29.4 us  [the longest x1 11.9 us: local(): lax.all_to_all(sums, VAR, 0, 0, tiled=True)]
    dot_general x5 -> x2, matrix products: 32.8 us -> 4.64 us  [the longest x1 2.43 us: local(): lax.dot_general(inputs_other, theirs, contract_rows, preferred_element_ty...]
    pallas_call x0 -> x3, Pallas kernels: none -> 18.9 us  [the longest x1 6.54 us: output_call(): pl.pallas_call(output_kernel, grid=(pieces,), in_specs=[pl.BlockSpec((1,...]
  transfers between devices with their start and end apart: 6 -> 53, of which waited for: 6 -> 26; matrix products, arithmetic and copies ran while one was open for 4% -> 8% of each run, Pallas kernels for 0% -> 0%
where the time goes in v1:
time: 266 us; the launch traced here: 264 us
  starting transfers between devices  121 us (45%)
  waiting for transfers between devices  89.7 us (34%)
  local copies, waits for them, and re-layouts  19.9 us (7%)
  Pallas kernels  18.9 us (7%)
  other arithmetic  8.43 us (3%)
  matrix products  4.64 us (2%)
    ppermute x45, waiting for transfers between devices, swap(): return lax.ppermute(value, axis, [(i, i ^ mask) for i in range(SIZE[axis])])  80.5 us
    ppermute x45, starting transfers between devices, swap(): return lax.ppermute(value, axis, [(i, i ^ mask) for i in range(SIZE[axis])])  72.9 us
    ppermute x4, starting transfers between devices, target_part(): got.append(lax.ppermute(part, AXES, pairs))  18.4 us
    all_to_all x1, starting transfers between devices, local(): lax.all_to_all(sums, VAR, 0, 0, tiled=True)  11.9 us
    unnamed x30, local copies, waits for them, and re-layouts  7.95 us
    all_to_all x1, waiting for transfers between devices, local(): lax.all_to_all(part.transpose(1, 0, 2, 3), ('zh', 'zl'), 0, 0, tiled=True)  7.94 us
    all_to_all x1, starting transfers between devices, local(): res_own = lax.all_to_all(res, VAR, 0, 0, tiled=True)  6.9 us
    pallas_call x1, Pallas kernels, output_call(): pl.pallas_call(output_kernel, grid=(pieces,), in_specs=[pl.BlockSpec((1,...  6.54 us
  transfers between devices with their start and end apart: 53, of which 26 were waited for; matrix products, arithmetic and copies ran while one was open for 8% of the time, Pallas kernels for 0%

profile of v1, /device:TPU:2, one launch (start us, length us, event | category | flops | bytes accessed | tf_op | source)
XLA Modules:
  0.0 264.3 jit_solution(6375268194569424511)
XLA Ops:
  1.5 3.4 %collective-permute-start.34 = (bf16[8,128]{1,0:T(8,128)(2,1)S(1)}, bf16[8,128]{1,0:T(8,128)(2,1)S(1)}, u32[]{:S(2)}, u32[]{:S(2)}) collective-permute-start(bf16[8,128]{1,0:T(8,128)(2,1)S(1)} %get-tuple-element.39), channel_id=1, source_target_pairs={{0,0},{1,32},{2,64},{3,96},{4,128},{5,160},{6,192},{7,224},{8,4},{... | collective-permute-start | bytes 6152 | tf_op jit(solution)/shard_map/ppermute | solution.py:190
  4.9 9.3 %collective-permute-start.35 = (bf16[8,128]{1,0:T(8,128)(2,1)S(1)}, bf16[8,128]{1,0:T(8,128)(2,1)S(1)}, u32[]{:S(2)}, u32[]{:S(2)}) collective-permute-start(bf16[8,128]{1,0:T(8,128)(2,1)S(1)} %get-tuple-element.40), channel_id=1, source_target_pairs={{0,8},{1,40},{2,72},{3,104},{4,136},{5,168},{6,200},{7,232},{8,12}... | collective-permute-start | bytes 6152 | tf_op jit(solution)/shard_map/ppermute | solution.py:190
  14.3 2.7 %collective-permute-start.37 = (bf16[8,128]{1,0:T(8,128)(2,1)S(1)}, bf16[8,128]{1,0:T(8,128)(2,1)S(1)}, u32[]{:S(2)}, u32[]{:S(2)}) collective-permute-start(bf16[8,128]{1,0:T(8,128)(2,1)S(1)} %get-tuple-element.41), channel_id=1, source_target_pairs={{0,24},{1,56},{2,88},{3,120},{4,152},{5,184},{6,216},{7,248},{8,28... | collective-permute-start | bytes 6152 | tf_op jit(solution)/shard_map/ppermute | solution.py:190
  17.0 2.9 %collective-permute-start.36 = (bf16[8,128]{1,0:T(8,128)(2,1)S(1)}, bf16[8,128]{1,0:T(8,128)(2,1)S(1)}, u32[]{:S(2)}, u32[]{:S(2)}) collective-permute-start(bf16[8,128]{1,0:T(8,128)(2,1)S(1)} %get-tuple-element.42), channel_id=1, source_target_pairs={{0,16},{1,48},{2,80},{3,112},{4,144},{5,176},{6,208},{7,240},{8,20... | collective-permute-start | bytes 6152 | tf_op jit(solution)/shard_map/ppermute | solution.py:190
  19.9 3.0 %collective-permute-start.1 = (bf16[128,256]{1,0:T(8,128)(2,1)}, bf16[128,256]{1,0:T(8,128)(2,1)S(1)}, u32[]{:S(2)}, u32[]{:S(2)}) collective-permute-start(bf16[128,256]{1,0:T(8,128)(2,1)} %param.7), channel_id=1, source_target_pairs={{0,8},{8,0},{1,9},{9,1},{2,10},{10,2},{3,11},{11,3},{4,12},{12,4},... | collective-permute-start | bytes 196616 | tf_op jit(solution)/shard_map/ppermute | solution.py:18
  24.5 2.2 fusion.3
  27.5 2.4 collective-permute-start.28
  31.6 2.5 collective-permute-start.14
  37.9 4.1 %collective-permute-start.18 = (f32[4,2,896]{2,1,0:T(2,128)S(1)}, f32[4,2,896]{2,1,0:T(2,128)S(1)}, u32[]{:S(2)}, u32[]{:S(2)}) collective-permute-start(f32[4,2,896]{2,1,0:T(2,128)S(1)} %pad_maximum_fusion.9), channel_id=1, source_target_pairs={{0,128},{64,192},{128,0},{192,64},{1,129},{65,193},{129,1},{193,65... | collective-permute-start | bytes 86024 | tf_op jit(solution)/shard_map/ppermute | solution.py:18
  43.9 2.1 collective-permute-start.27
  49.4 5.6 %collective-permute-done.20 = f32[32,896]{1,0:T(8,128)S(1)} collective-permute-done((f32[32,896]{1,0:T(8,128)S(1)}, f32[32,896]{1,0:T(8,128)S(1)}, u32[]{:S(2)}, u32[]{:S(2)}) %collective-permute-start.20) | collective-permute-done | bytes 114720 | tf_op jit(solution)/shard_map/ppermute | solution.py:18
  55.0 6.4 %collective-permute-done.21 = f32[32,896]{1,0:T(8,128)S(1)} collective-permute-done((f32[32,896]{1,0:T(8,128)S(1)}, f32[32,896]{1,0:T(8,128)S(1)}, u32[]{:S(2)}, u32[]{:S(2)}) %collective-permute-start.21) | collective-permute-done | bytes 114720 | tf_op jit(solution)/shard_map/ppermute | solution.py:18
  61.4 6.0 %collective-permute-done.22 = f32[32,896]{1,0:T(8,128)S(1)} collective-permute-done((f32[32,896]{1,0:T(8,128)S(1)}, f32[32,896]{1,0:T(8,128)S(1)}, u32[]{:S(2)}, u32[]{:S(2)}) %collective-permute-start.22) | collective-permute-done | bytes 114720 | tf_op jit(solution)/shard_map/ppermute | solution.py:18
  67.3 3.3 %collective-permute-start.23 = (f32[32,896]{1,0:T(8,128)}, f32[32,896]{1,0:T(8,128)S(1)}, u32[]{:S(2)}, u32[]{:S(2)}) collective-permute-start(f32[32,896]{1,0:T(8,128)} %copy-done.6), channel_id=1, source_target_pairs={{0,4},{4,0},{1,5},{5,1},{2,6},{6,2},{3,7},{7,3},{8,12},{12,8},{9,1... | collective-permute-start | bytes 344072 | tf_op jit(solution)/shard_map/ppermute | solution.py:18
  70.6 6.8 %collective-permute-done.23 = f32[32,896]{1,0:T(8,128)S(1)} collective-permute-done((f32[32,896]{1,0:T(8,128)}, f32[32,896]{1,0:T(8,128)S(1)}, u32[]{:S(2)}, u32[]{:S(2)}) %collective-permute-start.23) | collective-permute-done | bytes 114720 | tf_op jit(solution)/shard_map/ppermute | solution.py:18
  79.2 1.8 collective-permute-start.26
  81.0 2.4 convolution_add_fusion
  83.4 6.3 %all-to-all-start = ((f32[16,16,896]{2,1,0:T(8,128)}), f32[16,16,896]{2,1,0:T(8,128)}, u32[]{:S(2)}, u32[]{:S(2)}) async-start(f32[16,16,896]{2,1,0:T(8,128)} %bitcast.139), calls=%async_computation | async-start | bytes 1835008 | tf_op jit(solution)/shard_map/all_to_all | solution.py:217
  89.7 3.1 %collective-permute-start.25 = (f32[32,896]{1,0:T(8,128)S(1)}, f32[32,896]{1,0:T(8,128)S(1)}, u32[]{:S(2)}, u32[]{:S(2)}) collective-permute-start(f32[32,896]{1,0:T(8,128)S(1)} %collective-permute-done.23), channel_id=1, source_target_pairs={{0,2},{1,3},{2,0},{3,1},{4,6},{5,7},{6,4},{7,5},{8,10},{9,11},{10,... | collective-permute-start | bytes 344072 | tf_op jit(solution)/shard_map/ppermute | solution.py:18
  96.1 2.9 %collective-permute-start.32 = (bf16[896,128]{1,0:T(8,128)(2,1)S(1)}, bf16[896,128]{1,0:T(8,128)(2,1)}, u32[]{:S(2)}, u32[]{:S(2)}) collective-permute-start(bf16[896,128]{1,0:T(8,128)(2,1)S(1)} %collective-permute-done.30), channel_id=1, source_target_pairs={{0,2},{1,3},{2,0},{3,1},{4,6},{5,7},{6,4},{7,5},{8,10},{9,11},{10,... | collective-permute-start | bytes 688136 | tf_op jit(solution)/shard_map/ppermute | solution.py:18
  100.0 7.5 %collective-permute-done.24 = f32[32,896]{1,0:T(8,128)S(1)} collective-permute-done((f32[32,896]{1,0:T(8,128)S(1)}, f32[32,896]{1,0:T(8,128)S(1)}, u32[]{:S(2)}, u32[]{:S(2)}) %collective-permute-start.24) | collective-permute-done | bytes 114720 | tf_op jit(solution)/shard_map/ppermute | solution.py:18
  108.5 2.6 reshape.52
  113.5 4.3 %all-to-all-start.1 = ((f32[8,4,2,896]{3,2,1,0:T(2,128)}), f32[8,4,2,896]{3,2,1,0:T(2,128)S(1)}, u32[]{:S(2)}, u32[]{:S(2)}) async-start(f32[8,4,2,896]{3,2,1,0:T(2,128)} %copy.36), calls=%async_computation.1 | async-start | bytes 458752 | tf_op jit(solution)/shard_map/all_to_all | solution.py:219
  120.0 7.9 %all-to-all-done.1 = f32[8,4,2,896]{3,2,1,0:T(2,128)S(1)} async-done(((f32[8,4,2,896]{3,2,1,0:T(2,128)}), f32[8,4,2,896]{3,2,1,0:T(2,128)S(1)}, u32[]{:S(2)}, u32[]{:S(2)}) %all-to-all-start.1) | async-done | bytes 229408 | tf_op jit(solution)/shard_map/all_to_all | solution.py:219
  130.7 3.3 %collective-permute-start.5 = (f32[2,4,2,896]{3,2,1,0:T(2,128)S(1)}, f32[2,4,2,896]{3,2,1,0:T(2,128)S(1)}, u32[]{:S(2)}, u32[]{:S(2)}) collective-permute-start(f32[2,4,2,896]{3,2,1,0:T(2,128)S(1)} %pad_maximum_fusion.7), channel_id=1, source_target_pairs={{0,192},{64,128},{128,64},{192,0},{1,193},{65,129},{129,65},{193,1... | collective-permute-start | bytes 172040 | tf_op jit(solution)/shard_map/ppermute | solution.py:18
  134.0 2.3 collective-permute-done.4
  137.3 2.4 collective-permute-start.7
  142.6 4.9 %collective-permute-done.7 = f32[4,2,4,2,896]{4,3,0,2,1:T(2,128)S(1)} collective-permute-done((f32[4,2,4,2,896]{4,3,0,2,1:T(2,128)S(1)}, f32[4,2,4,2,896]{4,3,0,2,1:T(2,128)S(1)}, u32[]{:S(2)}, u32[]{:S(2)}) %collective-permute-start.7) | collective-permute-done | bytes 229408 | tf_op jit(solution)/shard_map/ppermute | solution.py:18
  147.5 3.2 %collective-permute-done.6 = f32[4,2,4,2,896]{4,3,0,2,1:T(2,128)S(1)} collective-permute-done((f32[4,2,4,2,896]{4,3,0,2,1:T(2,128)S(1)}, f32[4,2,4,2,896]{4,3,0,2,1:T(2,128)S(1)}, u32[]{:S(2)}, u32[]{:S(2)}) %collective-permute-start.6) | collective-permute-done | bytes 229408 | tf_op jit(solution)/shard_map/ppermute | solution.py:18
  152.5 1.8 reshape.54.raw_ref
  154.4 2.8 %reshape.58 = f32[2,4,32,896]{3,2,1,0:T(8,128)} reshape(f32[2,4,4,4,2,896]{5,4,3,2,1,0:T(2,128)} %maximum_bitcast_fusion) | data formatting | bytes 1835008 | tf_op jit(solution)/shard_map/reshape;reshape | solution.py:232
  158.3 6.5 %output.1.res_ref = bf16[32,32,128]{2,1,0:T(8,128)(2,1)} custom-call(f32[8,32,896]{2,1,0:T(8,128)S(1)} %reshape.54.raw_ref, f32[8,32,896]{2,1,0:T(8,128)S(1)} %copy-done.3, bf16[8,896,128]{2,1,0:T(8,128)(2,1)S(1)} %bitcast_dynamic-update-slice_fusion.down_ref, bf16[32,128]{1,0:T(8,128)(2,1)S(1)} %maximum_bitcast_fusion.1.target_ref), custom_call_target="tpu_custom_call" | custom-call | flops 1879048192 | bytes 4194304 | tf_op jit(solution)/shard_map/output/pallas_call | solution.py:69
  166.3 6.3 %back.1 = f32[8,32,896]{2,1,0:T(8,128)S(1)} custom-call(bf16[32,32,128]{2,1,0:T(8,128)(2,1)} %output.1.res_ref, f32[8,32,896]{2,1,0:T(8,128)S(1)} %reshape.54.raw_ref, bf16[8,896,128]{2,1,0:T(8,128)(2,1)S(1)} %copy-done.1), custom_call_target="tpu_custom_call" | custom-call | flops 1879048192 | bytes 4194304 | tf_op jit(solution)/shard_map/back/pallas_call | solution.py:108
  172.6 6.9 %all-to-all-start.2 = ((bf16[32,32,128]{2,1,0:T(8,128)(2,1)}), bf16[32,32,128]{2,1,0:T(8,128)(2,1)S(1)}, u32[]{:S(2)}, u32[]{:S(2)}) async-start(bf16[32,32,128]{2,1,0:T(8,128)(2,1)} %output.1.res_ref), calls=%async_computation.2 | async-start | bytes 524288 | tf_op jit(solution)/shard_map/all_to_all | solution.py:229
  180.6 2.3 collective-permute-start.46
  188.1 1.8 collective-permute-start.11
  190.0 4.5 %collective-permute-done.46 = f32[2,32,896]{2,1,0:T(8,128)S(1)} collective-permute-done((f32[2,32,896]{2,1,0:T(8,128)S(1)}, f32[2,32,896]{2,1,0:T(8,128)S(1)}, u32[]{:S(2)}, u32[]{:S(2)}) %collective-permute-start.46) | collective-permute-done | bytes 229408 | tf_op jit(solution)/shard_map/ppermute | solution.py:18
  194.4 8.1 %collective-permute-done.47 = f32[2,32,896]{2,1,0:T(8,128)S(1)} collective-permute-done((f32[2,32,896]{2,1,0:T(8,128)S(1)}, f32[2,32,896]{2,1,0:T(8,128)S(1)}, u32[]{:S(2)}, u32[]{:S(2)}) %collective-permute-start.47) | collective-permute-done | bytes 229408 | tf_op jit(solution)/shard_map/ppermute | solution.py:18
  202.6 2.3 collective-permute-start.48
  206.2 2.7 %collective-permute-start.12 = (f32[4,32,896]{2,1,0:T(8,128)S(1)}, f32[4,32,896]{2,1,0:T(8,128)S(1)}, u32[]{:S(2)}, u32[]{:S(2)}) collective-permute-start(f32[4,32,896]{2,1,0:T(8,128)S(1)} %get-tuple-element.8), channel_id=1, source_target_pairs={{0,4},{4,0},{1,5},{5,1},{2,6},{6,2},{3,7},{7,3},{8,12},{12,8},{9,1... | collective-permute-start | bytes 1376264 | tf_op jit(solution)/shard_map/ppermute | solution.py:18
  208.9 3.3 %collective-permute-start.41 = (bf16[32,32,128]{2,1,0:T(8,128)(2,1)S(1)}, bf16[32,32,128]{2,1,0:T(8,128)(2,1)S(1)}, u32[]{:S(2)}, u32[]{:S(2)}) collective-permute-start(bf16[32,32,128]{2,1,0:T(8,128)(2,1)S(1)} %all-to-all-done.2.refs_0_), channel_id=1, source_target_pairs={{0,4},{4,0},{1,5},{5,1},{2,6},{6,2},{3,7},{7,3},{8,12},{12,8},{9,1... | collective-permute-start | bytes 786440 | tf_op jit(solution)/shard_map/ppermute | solution.py:18
  215.2 11.9 %all-to-all-start.3 = ((f32[32,1,896]{2,1,0:T(1,128)}), f32[32,1,896]{2,1,0:T(1,128)}, u32[]{:S(2)}, u32[]{:S(2)}) async-start(f32[32,1,896]{2,1,0:T(1,128)} %all_to_all.18), calls=%async_computation.3 | async-start | bytes 229376 | tf_op jit(solution)/shard_map/all_to_all | solution.py:241
  227.2 8.2 %collective-permute-start.39 = (bf16[32,32,128]{2,1,0:T(8,128)(2,1)S(1)}, bf16[32,32,128]{2,1,0:T(8,128)(2,1)S(1)}, u32[]{:S(2)}, u32[]{:S(2)}) collective-permute-start(bf16[32,32,128]{2,1,0:T(8,128)(2,1)S(1)} %all-to-all-done.2.refs_0_), channel_id=1, source_target_pairs={{0,2},{1,3},{2,0},{3,1},{4,6},{5,7},{6,4},{7,5},{8,10},{9,11},{10,... | collective-permute-start | bytes 786440 | tf_op jit(solution)/shard_map/ppermute | solution.py:18
  235.4 5.8 %collective-permute-done.41.refs_4_ = bf16[32,32,128]{2,1,0:T(8,128)(2,1)S(1)} collective-permute-done((bf16[32,32,128]{2,1,0:T(8,128)(2,1)S(1)}, bf16[32,32,128]{2,1,0:T(8,128)(2,1)S(1)}, u32[]{:S(2)}, u32[]{:S(2)}) %collective-permute-start.41) | collective-permute-done | bytes 262176 | tf_op jit(solution)/shard_map/ppermute | solution.py:18
  242.6 2.7 %collective-permute-start.42 = (bf16[32,32,128]{2,1,0:T(8,128)(2,1)S(1)}, bf16[32,32,128]{2,1,0:T(8,128)(2,1)S(1)}, u32[]{:S(2)}, u32[]{:S(2)}) collective-permute-start(bf16[32,32,128]{2,1,0:T(8,128)(2,1)S(1)} %collective-permute-done.41.refs_4_), channel_id=1, source_target_pairs={{0,1},{1,0},{2,3},{3,2},{4,5},{5,4},{6,7},{7,6},{8,9},{9,8},{10,11... | collective-permute-start | bytes 786440 | tf_op jit(solution)/shard_map/ppermute | solution.py:18
  248.2 6.2 %collective-permute-done.44.refs_7_ = bf16[32,32,128]{2,1,0:T(8,128)(2,1)S(1)} collective-permute-done((bf16[32,32,128]{2,1,0:T(8,128)(2,1)S(1)}, bf16[32,32,128]{2,1,0:T(8,128)(2,1)S(1)}, u32[]{:S(2)}, u32[]{:S(2)}) %collective-permute-start.44) | collective-permute-done | bytes 262176 | tf_op jit(solution)/shard_map/ppermute | solution.py:18
  254.4 3.8 %collective-permute-done.42.refs_5_ = bf16[32,32,128]{2,1,0:T(8,128)(2,1)S(1)} collective-permute-done((bf16[32,32,128]{2,1,0:T(8,128)(2,1)S(1)}, bf16[32,32,128]{2,1,0:T(8,128)(2,1)S(1)}, u32[]{:S(2)}, u32[]{:S(2)}) %collective-permute-start.42) | collective-permute-done | bytes 262176 | tf_op jit(solution)/shard_map/ppermute | solution.py:18
  258.2 6.1 %grad.1 = bf16[1,896,4096]{2,1,0:T(8,128)(2,1)} custom-call(f32[8,32,896]{2,1,0:T(8,128)S(1)} %pad_maximum_fusion.2.raw_ref, f32[1,896]{1,0:T(1,128)S(1)} %get-tuple-element.3.gain_ref, bf16[32,32,128]{2,1,0:T(8,128)(2,1)S(1)} %all-to-all-done.2.refs_0_, bf16[32,32,128]{2,1,0:T(8,128)(2,1)S(1)} %collective-permute-done.38.refs_1_, ...), custom_call_target="tpu_custom_call" | custom-call | flops 1879048192 | bytes 10485760 | tf_op jit(solution)/shard_map/grad/pallas_call | solution.py:149
  (143 shorter events, 50.6 us)
Async XLA Ops:
  1.5 26.0 %collective-permute-start.34 = (bf16[8,128]{1,0:T(8,128)(2,1)S(1)}, bf16[8,128]{1,0:T(8,128)(2,1)S(1)}, u32[]{:S(2)}, u32[]{:S(2)}) collective-permute-start(bf16[8,128]{1,0:T(8,128)(2,1)S(1)} %get-tuple-element.39), channel_id=1, source_target_pairs={{0,0},{1,32},{2,64},{3,96},{4,128},{5,160},{6,192},{7,224},{8,4},{... | collective-permute-start | bytes 6152 | tf_op jit(solution)/shard_map/ppermute | solution.py:190
  4.9 25.0 %collective-permute-start.35 = (bf16[8,128]{1,0:T(8,128)(2,1)S(1)}, bf16[8,128]{1,0:T(8,128)(2,1)S(1)}, u32[]{:S(2)}, u32[]{:S(2)}) collective-permute-start(bf16[8,128]{1,0:T(8,128)(2,1)S(1)} %get-tuple-element.40), channel_id=1, source_target_pairs={{0,8},{1,40},{2,72},{3,104},{4,136},{5,168},{6,200},{7,232},{8,12}... | collective-permute-start | bytes 6152 | tf_op jit(solution)/shard_map/ppermute | solution.py:190
  14.3 15.7 %collective-permute-start.37 = (bf16[8,128]{1,0:T(8,128)(2,1)S(1)}, bf16[8,128]{1,0:T(8,128)(2,1)S(1)}, u32[]{:S(2)}, u32[]{:S(2)}) collective-permute-start(bf16[8,128]{1,0:T(8,128)(2,1)S(1)} %get-tuple-element.41), channel_id=1, source_target_pairs={{0,24},{1,56},{2,88},{3,120},{4,152},{5,184},{6,216},{7,248},{8,28... | collective-permute-start | bytes 6152 | tf_op jit(solution)/shard_map/ppermute | solution.py:190
  17.0 13.0 %collective-permute-start.36 = (bf16[8,128]{1,0:T(8,128)(2,1)S(1)}, bf16[8,128]{1,0:T(8,128)(2,1)S(1)}, u32[]{:S(2)}, u32[]{:S(2)}) collective-permute-start(bf16[8,128]{1,0:T(8,128)(2,1)S(1)} %get-tuple-element.42), channel_id=1, source_target_pairs={{0,16},{1,48},{2,80},{3,112},{4,144},{5,176},{6,208},{7,240},{8,20... | collective-permute-start | bytes 6152 | tf_op jit(solution)/shard_map/ppermute | solution.py:190
  19.9 57.6 %collective-permute-start.1 = (bf16[128,256]{1,0:T(8,128)(2,1)}, bf16[128,256]{1,0:T(8,128)(2,1)S(1)}, u32[]{:S(2)}, u32[]{:S(2)}) collective-permute-start(bf16[128,256]{1,0:T(8,128)(2,1)} %param.7), channel_id=1, source_target_pairs={{0,8},{8,0},{1,9},{9,1},{2,10},{10,2},{3,11},{11,3},{4,12},{12,4},... | collective-permute-start | bytes 196616 | tf_op jit(solution)/shard_map/ppermute | solution.py:18
  27.5 66.2 %collective-permute-start.28 = (bf16[896,128]{1,0:T(8,128)(2,1)S(1)}, bf16[896,128]{1,0:T(8,128)(2,1)}, u32[]{:S(2)}, u32[]{:S(2)}) collective-permute-start(bf16[896,128]{1,0:T(8,128)(2,1)S(1)} %copy-done.5), channel_id=1, source_target_pairs={{0,2},{1,3},{2,0},{3,1},{4,6},{5,7},{6,4},{7,5},{8,10},{9,11},{10,... | collective-permute-start | bytes 688136 | tf_op jit(solution)/shard_map/ppermute | solution.py:18
  31.2 5.2 %collective-permute-start.15 = (f32[2,896]{1,0:T(2,128)S(1)}, f32[2,896]{1,0:T(2,128)S(1)}, u32[]{:S(2)}, u32[]{:S(2)}) collective-permute-start(f32[2,896]{1,0:T(2,128)S(1)} %get-tuple-element.46), channel_id=1, source_target_pairs={{0,32},{16,48},{32,0},{48,16},{1,33},{17,49},{33,1},{49,17},{2,34}... | collective-permute-start | bytes 21512 | tf_op jit(solution)/shard_map/ppermute | solution.py:18
  31.6 4.7 %collective-permute-start.14 = (f32[2,896]{1,0:T(2,128)S(1)}, f32[2,896]{1,0:T(2,128)S(1)}, u32[]{:S(2)}, u32[]{:S(2)}) collective-permute-start(f32[2,896]{1,0:T(2,128)S(1)} %get-tuple-element.46), channel_id=1, source_target_pairs={{0,16},{16,0},{32,48},{48,32},{1,17},{17,1},{33,49},{49,33},{2,18}... | collective-permute-start | bytes 21512 | tf_op jit(solution)/shard_map/ppermute | solution.py:18
  37.9 6.0 %collective-permute-start.18 = (f32[4,2,896]{2,1,0:T(2,128)S(1)}, f32[4,2,896]{2,1,0:T(2,128)S(1)}, u32[]{:S(2)}, u32[]{:S(2)}) collective-permute-start(f32[4,2,896]{2,1,0:T(2,128)S(1)} %pad_maximum_fusion.9), channel_id=1, source_target_pairs={{0,128},{64,192},{128,0},{192,64},{1,129},{65,193},{129,1},{193,65... | collective-permute-start | bytes 86024 | tf_op jit(solution)/shard_map/ppermute | solution.py:18
  42.9 6.0 %collective-permute-start.19 = (f32[4,2,896]{2,1,0:T(2,128)S(1)}, f32[4,2,896]{2,1,0:T(2,128)S(1)}, u32[]{:S(2)}, u32[]{:S(2)}) collective-permute-start(f32[4,2,896]{2,1,0:T(2,128)S(1)} %pad_maximum_fusion.9), channel_id=1, source_target_pairs={{0,192},{64,128},{128,64},{192,0},{1,193},{65,129},{129,65},{193,1... | collective-permute-start | bytes 86024 | tf_op jit(solution)/shard_map/ppermute | solution.py:18
  43.9 45.8 %collective-permute-start.27 = (bf16[896,128]{1,0:T(8,128)(2,1)S(1)}, bf16[896,128]{1,0:T(8,128)(2,1)}, u32[]{:S(2)}, u32[]{:S(2)}) collective-permute-start(bf16[896,128]{1,0:T(8,128)(2,1)S(1)} %copy-done.5), channel_id=1, source_target_pairs={{0,1},{1,0},{2,3},{3,2},{4,5},{5,4},{6,7},{7,6},{8,9},{9,8},{10,11... | collective-permute-start | bytes 688136 | tf_op jit(solution)/shard_map/ppermute | solution.py:18
  46.1 48.3 %collective-permute-start.30 = (bf16[896,128]{1,0:T(8,128)(2,1)S(1)}, bf16[896,128]{1,0:T(8,128)(2,1)S(1)}, u32[]{:S(2)}, u32[]{:S(2)}) collective-permute-start(bf16[896,128]{1,0:T(8,128)(2,1)S(1)} %copy-done.5), channel_id=1, source_target_pairs={{0,4},{4,0},{1,5},{5,1},{2,6},{6,2},{3,7},{7,3},{8,12},{12,8},{9,1... | collective-permute-start | bytes 688136 | tf_op jit(solution)/shard_map/ppermute | solution.py:18
  49.2 5.7 %collective-permute-start.20 = (f32[32,896]{1,0:T(8,128)S(1)}, f32[32,896]{1,0:T(8,128)S(1)}, u32[]{:S(2)}, u32[]{:S(2)}) collective-permute-start(f32[32,896]{1,0:T(8,128)S(1)} %reshape.55), channel_id=1, source_target_pairs={{0,1},{1,0},{2,3},{3,2},{4,5},{5,4},{6,7},{7,6},{8,9},{9,8},{10,11... | collective-permute-start | bytes 344072 | tf_op jit(solution)/shard_map/ppermute | solution.py:18
  55.0 6.4 %collective-permute-start.21 = (f32[32,896]{1,0:T(8,128)S(1)}, f32[32,896]{1,0:T(8,128)S(1)}, u32[]{:S(2)}, u32[]{:S(2)}) collective-permute-start(f32[32,896]{1,0:T(8,128)S(1)} %reshape.55), channel_id=1, source_target_pairs={{0,2},{1,3},{2,0},{3,1},{4,6},{5,7},{6,4},{7,5},{8,10},{9,11},{10,... | collective-permute-start | bytes 344072 | tf_op jit(solution)/shard_map/ppermute | solution.py:18
  61.3 6.0 %collective-permute-start.22 = (f32[32,896]{1,0:T(8,128)S(1)}, f32[32,896]{1,0:T(8,128)S(1)}, u32[]{:S(2)}, u32[]{:S(2)}) collective-permute-start(f32[32,896]{1,0:T(8,128)S(1)} %reshape.55), channel_id=1, source_target_pairs={{0,3},{1,2},{2,1},{3,0},{4,7},{5,6},{6,5},{7,4},{8,11},{9,10},{10,... | collective-permute-start | bytes 344072 | tf_op jit(solution)/shard_map/ppermute | solution.py:18
  67.3 10.1 %collective-permute-start.23 = (f32[32,896]{1,0:T(8,128)}, f32[32,896]{1,0:T(8,128)S(1)}, u32[]{:S(2)}, u32[]{:S(2)}) collective-permute-start(f32[32,896]{1,0:T(8,128)} %copy-done.6), channel_id=1, source_target_pairs={{0,4},{4,0},{1,5},{5,1},{2,6},{6,2},{3,7},{7,3},{8,12},{12,8},{9,1... | collective-permute-start | bytes 344072 | tf_op jit(solution)/shard_map/ppermute | solution.py:18
  77.5 18.6 %collective-permute-start.29 = (bf16[896,128]{1,0:T(8,128)(2,1)S(1)}, bf16[896,128]{1,0:T(8,128)(2,1)}, u32[]{:S(2)}, u32[]{:S(2)}) collective-permute-start(bf16[896,128]{1,0:T(8,128)(2,1)S(1)} %copy-done.5), channel_id=1, source_target_pairs={{0,3},{1,2},{2,1},{3,0},{4,7},{5,6},{6,5},{7,4},{8,11},{9,10},{10,... | collective-permute-start | bytes 688136 | tf_op jit(solution)/shard_map/ppermute | solution.py:18
  79.2 38.6 %collective-permute-start.26 = (f32[32,896]{1,0:T(8,128)S(1)}, f32[32,896]{1,0:T(8,128)}, u32[]{:S(2)}, u32[]{:S(2)}) collective-permute-start(f32[32,896]{1,0:T(8,128)S(1)} %collective-permute-done.23), channel_id=1, source_target_pairs={{0,3},{1,2},{2,1},{3,0},{4,7},{5,6},{6,5},{7,4},{8,11},{9,10},{10,... | collective-permute-start | bytes 344072 | tf_op jit(solution)/shard_map/ppermute | solution.py:18
  83.4 25.1 %all-to-all-start = ((f32[16,16,896]{2,1,0:T(8,128)}), f32[16,16,896]{2,1,0:T(8,128)}, u32[]{:S(2)}, u32[]{:S(2)}) async-start(f32[16,16,896]{2,1,0:T(8,128)} %bitcast.139), calls=%async_computation | async-start | bytes 1835008 | tf_op jit(solution)/shard_map/all_to_all | solution.py:217
  89.7 18.8 %collective-permute-start.25 = (f32[32,896]{1,0:T(8,128)S(1)}, f32[32,896]{1,0:T(8,128)S(1)}, u32[]{:S(2)}, u32[]{:S(2)}) collective-permute-start(f32[32,896]{1,0:T(8,128)S(1)} %collective-permute-done.23), channel_id=1, source_target_pairs={{0,2},{1,3},{2,0},{3,1},{4,6},{5,7},{6,4},{7,5},{8,10},{9,11},{10,... | collective-permute-start | bytes 344072 | tf_op jit(solution)/shard_map/ppermute | solution.py:18
  93.7 13.7 %collective-permute-start.24 = (f32[32,896]{1,0:T(8,128)S(1)}, f32[32,896]{1,0:T(8,128)S(1)}, u32[]{:S(2)}, u32[]{:S(2)}) collective-permute-start(f32[32,896]{1,0:T(8,128)S(1)} %collective-permute-done.23), channel_id=1, source_target_pairs={{0,1},{1,0},{2,3},{3,2},{4,5},{5,4},{6,7},{7,6},{8,9},{9,8},{10,11... | collective-permute-start | bytes 344072 | tf_op jit(solution)/shard_map/ppermute | solution.py:18
  94.4 47.1 %collective-permute-start.33 = (bf16[896,128]{1,0:T(8,128)(2,1)S(1)}, bf16[896,128]{1,0:T(8,128)(2,1)}, u32[]{:S(2)}, u32[]{:S(2)}) collective-permute-start(bf16[896,128]{1,0:T(8,128)(2,1)S(1)} %collective-permute-done.30), channel_id=1, source_target_pairs={{0,3},{1,2},{2,1},{3,0},{4,7},{5,6},{6,5},{7,4},{8,11},{9,10},{10,... | collective-permute-start | bytes 688136 | tf_op jit(solution)/shard_map/ppermute | solution.py:18
  96.1 32.0 %collective-permute-start.32 = (bf16[896,128]{1,0:T(8,128)(2,1)S(1)}, bf16[896,128]{1,0:T(8,128)(2,1)}, u32[]{:S(2)}, u32[]{:S(2)}) collective-permute-start(bf16[896,128]{1,0:T(8,128)(2,1)S(1)} %collective-permute-done.30), channel_id=1, source_target_pairs={{0,2},{1,3},{2,0},{3,1},{4,6},{5,7},{6,4},{7,5},{8,10},{9,11},{10,... | collective-permute-start | bytes 688136 | tf_op jit(solution)/shard_map/ppermute | solution.py:18
  107.5 11.2 %collective-permute-start.31 = (bf16[896,128]{1,0:T(8,128)(2,1)S(1)}, bf16[896,128]{1,0:T(8,128)(2,1)}, u32[]{:S(2)}, u32[]{:S(2)}) collective-permute-start(bf16[896,128]{1,0:T(8,128)(2,1)S(1)} %collective-permute-done.30), channel_id=1, source_target_pairs={{0,1},{1,0},{2,3},{3,2},{4,5},{5,4},{6,7},{7,6},{8,9},{9,8},{10,11... | collective-permute-start | bytes 688136 | tf_op jit(solution)/shard_map/ppermute | solution.py:18
  113.5 14.4 %all-to-all-start.1 = ((f32[8,4,2,896]{3,2,1,0:T(2,128)}), f32[8,4,2,896]{3,2,1,0:T(2,128)S(1)}, u32[]{:S(2)}, u32[]{:S(2)}) async-start(f32[8,4,2,896]{3,2,1,0:T(2,128)} %copy.36), calls=%async_computation.1 | async-start | bytes 458752 | tf_op jit(solution)/shard_map/all_to_all | solution.py:219
  129.5 6.8 %collective-permute-start.4 = (f32[2,4,2,896]{3,2,1,0:T(2,128)S(1)}, f32[2,4,2,896]{3,2,1,0:T(2,128)S(1)}, u32[]{:S(2)}, u32[]{:S(2)}) collective-permute-start(f32[2,4,2,896]{3,2,1,0:T(2,128)S(1)} %pad_maximum_fusion.7), channel_id=1, source_target_pairs={{0,128},{64,192},{128,0},{192,64},{1,129},{65,193},{129,1},{193,65... | collective-permute-start | bytes 172040 | tf_op jit(solution)/shard_map/ppermute | solution.py:18
  130.2 6.2 %collective-permute-start.3 = (f32[2,4,2,896]{3,2,1,0:T(2,128)S(1)}, f32[2,4,2,896]{3,2,1,0:T(2,128)S(1)}, u32[]{:S(2)}, u32[]{:S(2)}) collective-permute-start(f32[2,4,2,896]{3,2,1,0:T(2,128)S(1)} %pad_maximum_fusion.7), channel_id=1, source_target_pairs={{0,64},{64,0},{128,192},{192,128},{1,65},{65,1},{129,193},{193,129... | collective-permute-start | bytes 172040 | tf_op jit(solution)/shard_map/ppermute | solution.py:18
  130.7 6.3 %collective-permute-start.5 = (f32[2,4,2,896]{3,2,1,0:T(2,128)S(1)}, f32[2,4,2,896]{3,2,1,0:T(2,128)S(1)}, u32[]{:S(2)}, u32[]{:S(2)}) collective-permute-start(f32[2,4,2,896]{3,2,1,0:T(2,128)S(1)} %pad_maximum_fusion.7), channel_id=1, source_target_pairs={{0,192},{64,128},{128,64},{192,0},{1,193},{65,129},{129,65},{193,1... | collective-permute-start | bytes 172040 | tf_op jit(solution)/shard_map/ppermute | solution.py:18
  137.3 10.1 %collective-permute-start.7 = (f32[4,2,4,2,896]{4,3,0,2,1:T(2,128)S(1)}, f32[4,2,4,2,896]{4,3,0,2,1:T(2,128)S(1)}, u32[]{:S(2)}, u32[]{:S(2)}) collective-permute-start(f32[4,2,4,2,896]{4,3,0,2,1:T(2,128)S(1)} %pad_maximum_fusion.4), channel_id=1, source_target_pairs={{0,32},{16,48},{32,0},{48,16},{1,33},{17,49},{33,1},{49,17},{2,34}... | collective-permute-start | bytes 688136 | tf_op jit(solution)/shard_map/ppermute | solution.py:18
  139.7 10.9 %collective-permute-start.6 = (f32[4,2,4,2,896]{4,3,0,2,1:T(2,128)S(1)}, f32[4,2,4,2,896]{4,3,0,2,1:T(2,128)S(1)}, u32[]{:S(2)}, u32[]{:S(2)}) collective-permute-start(f32[4,2,4,2,896]{4,3,0,2,1:T(2,128)S(1)} %pad_maximum_fusion.4), channel_id=1, source_target_pairs={{0,16},{16,0},{32,48},{48,32},{1,17},{17,1},{33,49},{49,33},{2,18}... | collective-permute-start | bytes 688136 | tf_op jit(solution)/shard_map/ppermute | solution.py:18
  141.0 9.7 %collective-permute-start.8 = (f32[4,2,4,2,896]{4,3,0,2,1:T(2,128)S(1)}, f32[4,2,4,2,896]{4,3,0,2,1:T(2,128)S(1)}, u32[]{:S(2)}, u32[]{:S(2)}) collective-permute-start(f32[4,2,4,2,896]{4,3,0,2,1:T(2,128)S(1)} %pad_maximum_fusion.4), channel_id=1, source_target_pairs={{0,48},{16,32},{32,16},{48,0},{1,49},{17,33},{33,17},{49,1},{2,50}... | collective-permute-start | bytes 688136 | tf_op jit(solution)/shard_map/ppermute | solution.py:18
  172.6 36.3 %all-to-all-start.2 = ((bf16[32,32,128]{2,1,0:T(8,128)(2,1)}), bf16[32,32,128]{2,1,0:T(8,128)(2,1)S(1)}, u32[]{:S(2)}, u32[]{:S(2)}) async-start(bf16[32,32,128]{2,1,0:T(8,128)(2,1)} %output.1.res_ref), calls=%async_computation.2 | async-start | bytes 524288 | tf_op jit(solution)/shard_map/all_to_all | solution.py:229
  179.6 8.5 %collective-permute-start.45 = (f32[2,32,896]{2,1,0:T(8,128)S(1)}, f32[2,32,896]{2,1,0:T(8,128)S(1)}, u32[]{:S(2)}, u32[]{:S(2)}) collective-permute-start(f32[2,32,896]{2,1,0:T(8,128)S(1)} %get-tuple-element.4), channel_id=1, source_target_pairs={{0,1},{1,0},{2,3},{3,2},{4,5},{5,4},{6,7},{7,6},{8,9},{9,8},{10,11... | collective-permute-start | bytes 688136 | tf_op jit(solution)/shard_map/ppermute | solution.py:18
  180.6 13.8 %collective-permute-start.46 = (f32[2,32,896]{2,1,0:T(8,128)S(1)}, f32[2,32,896]{2,1,0:T(8,128)S(1)}, u32[]{:S(2)}, u32[]{:S(2)}) collective-permute-start(f32[2,32,896]{2,1,0:T(8,128)S(1)} %get-tuple-element.5), channel_id=1, source_target_pairs={{0,2},{1,3},{2,0},{3,1},{4,6},{5,7},{6,4},{7,5},{8,10},{9,11},{10,... | collective-permute-start | bytes 688136 | tf_op jit(solution)/shard_map/ppermute | solution.py:18
  183.0 19.6 %collective-permute-start.47 = (f32[2,32,896]{2,1,0:T(8,128)S(1)}, f32[2,32,896]{2,1,0:T(8,128)S(1)}, u32[]{:S(2)}, u32[]{:S(2)}) collective-permute-start(f32[2,32,896]{2,1,0:T(8,128)S(1)} %get-tuple-element.6), channel_id=1, source_target_pairs={{0,3},{1,2},{2,1},{3,0},{4,7},{5,6},{6,5},{7,4},{8,11},{9,10},{10,... | collective-permute-start | bytes 688136 | tf_op jit(solution)/shard_map/ppermute | solution.py:18
  184.4 20.5 %collective-permute-start.10 = (f32[2,32,896]{2,1,0:T(8,128)S(1)}, f32[2,32,896]{2,1,0:T(8,128)S(1)}, u32[]{:S(2)}, u32[]{:S(2)}) collective-permute-start(f32[2,32,896]{2,1,0:T(8,128)S(1)} %get-tuple-element.10), channel_id=1, source_target_pairs={{0,2},{1,3},{2,0},{3,1},{4,6},{5,7},{6,4},{7,5},{8,10},{9,11},{10,... | collective-permute-start | bytes 688136 | tf_op jit(solution)/shard_map/ppermute | solution.py:18
  185.5 19.5 %collective-permute-start.9 = (f32[2,32,896]{2,1,0:T(8,128)S(1)}, f32[2,32,896]{2,1,0:T(8,128)S(1)}, u32[]{:S(2)}, u32[]{:S(2)}) collective-permute-start(f32[2,32,896]{2,1,0:T(8,128)S(1)} %get-tuple-element.11), channel_id=1, source_target_pairs={{0,1},{1,0},{2,3},{3,2},{4,5},{5,4},{6,7},{7,6},{8,9},{9,8},{10,11... | collective-permute-start | bytes 688136 | tf_op jit(solution)/shard_map/ppermute | solution.py:18
  188.1 17.9 %collective-permute-start.11 = (f32[2,32,896]{2,1,0:T(8,128)S(1)}, f32[2,32,896]{2,1,0:T(8,128)S(1)}, u32[]{:S(2)}, u32[]{:S(2)}) collective-permute-start(f32[2,32,896]{2,1,0:T(8,128)S(1)} %get-tuple-element.12), channel_id=1, source_target_pairs={{0,3},{1,2},{2,1},{3,0},{4,7},{5,6},{6,5},{7,4},{8,11},{9,10},{10,... | collective-permute-start | bytes 688136 | tf_op jit(solution)/shard_map/ppermute | solution.py:18
  202.6 11.0 %collective-permute-start.48 = (f32[32,896]{1,0:T(8,128)S(1)}, f32[32,896]{1,0:T(8,128)}, u32[]{:S(2)}, u32[]{:S(2)}) collective-permute-start(f32[32,896]{1,0:T(8,128)S(1)} %slice_bitcast_fusion.9), channel_id=1, source_target_pairs={{0,4},{4,0},{1,5},{5,1},{2,6},{6,2},{3,7},{7,3},{8,12},{12,8},{9,1... | collective-permute-start | bytes 344072 | tf_op jit(solution)/shard_map/ppermute | solution.py:18
  206.2 36.4 %collective-permute-start.12 = (f32[4,32,896]{2,1,0:T(8,128)S(1)}, f32[4,32,896]{2,1,0:T(8,128)S(1)}, u32[]{:S(2)}, u32[]{:S(2)}) collective-permute-start(f32[4,32,896]{2,1,0:T(8,128)S(1)} %get-tuple-element.8), channel_id=1, source_target_pairs={{0,4},{4,0},{1,5},{5,1},{2,6},{6,2},{3,7},{7,3},{8,12},{12,8},{9,1... | collective-permute-start | bytes 1376264 | tf_op jit(solution)/shard_map/ppermute | solution.py:18
  208.9 32.3 %collective-permute-start.41 = (bf16[32,32,128]{2,1,0:T(8,128)(2,1)S(1)}, bf16[32,32,128]{2,1,0:T(8,128)(2,1)S(1)}, u32[]{:S(2)}, u32[]{:S(2)}) collective-permute-start(bf16[32,32,128]{2,1,0:T(8,128)(2,1)S(1)} %all-to-all-done.2.refs_0_), channel_id=1, source_target_pairs={{0,4},{4,0},{1,5},{5,1},{2,6},{6,2},{3,7},{7,3},{8,12},{12,8},{9,1... | collective-permute-start | bytes 786440 | tf_op jit(solution)/shard_map/ppermute | solution.py:18
  212.2 30.4 %collective-permute-start.40 = (bf16[32,32,128]{2,1,0:T(8,128)(2,1)S(1)}, bf16[32,32,128]{2,1,0:T(8,128)(2,1)S(1)}, u32[]{:S(2)}, u32[]{:S(2)}) collective-permute-start(bf16[32,32,128]{2,1,0:T(8,128)(2,1)S(1)} %all-to-all-done.2.refs_0_), channel_id=1, source_target_pairs={{0,3},{1,2},{2,1},{3,0},{4,7},{5,6},{6,5},{7,4},{8,11},{9,10},{10,... | collective-permute-start | bytes 786440 | tf_op jit(solution)/shard_map/ppermute | solution.py:18
  215.2 31.3 %all-to-all-start.3 = ((f32[32,1,896]{2,1,0:T(1,128)}), f32[32,1,896]{2,1,0:T(1,128)}, u32[]{:S(2)}, u32[]{:S(2)}) async-start(f32[32,1,896]{2,1,0:T(1,128)} %all_to_all.18), calls=%async_computation.3 | async-start | bytes 229376 | tf_op jit(solution)/shard_map/all_to_all | solution.py:241
  227.2 21.0 %collective-permute-start.39 = (bf16[32,32,128]{2,1,0:T(8,128)(2,1)S(1)}, bf16[32,32,128]{2,1,0:T(8,128)(2,1)S(1)}, u32[]{:S(2)}, u32[]{:S(2)}) collective-permute-start(bf16[32,32,128]{2,1,0:T(8,128)(2,1)S(1)} %all-to-all-done.2.refs_0_), channel_id=1, source_target_pairs={{0,2},{1,3},{2,0},{3,1},{4,6},{5,7},{6,4},{7,5},{8,10},{9,11},{10,... | collective-permute-start | bytes 786440 | tf_op jit(solution)/shard_map/ppermute | solution.py:18
  235.4 12.8 %collective-permute-start.38 = (bf16[32,32,128]{2,1,0:T(8,128)(2,1)S(1)}, bf16[32,32,128]{2,1,0:T(8,128)(2,1)S(1)}, u32[]{:S(2)}, u32[]{:S(2)}) collective-permute-start(bf16[32,32,128]{2,1,0:T(8,128)(2,1)S(1)} %all-to-all-done.2.refs_0_), channel_id=1, source_target_pairs={{0,1},{1,0},{2,3},{3,2},{4,5},{5,4},{6,7},{7,6},{8,9},{9,8},{10,11... | collective-permute-start | bytes 786440 | tf_op jit(solution)/shard_map/ppermute | solution.py:18
  241.2 13.2 %collective-permute-start.44 = (bf16[32,32,128]{2,1,0:T(8,128)(2,1)S(1)}, bf16[32,32,128]{2,1,0:T(8,128)(2,1)S(1)}, u32[]{:S(2)}, u32[]{:S(2)}) collective-permute-start(bf16[32,32,128]{2,1,0:T(8,128)(2,1)S(1)} %collective-permute-done.41.refs_4_), channel_id=1, source_target_pairs={{0,3},{1,2},{2,1},{3,0},{4,7},{5,6},{6,5},{7,4},{8,11},{9,10},{10,... | collective-permute-start | bytes 786440 | tf_op jit(solution)/shard_map/ppermute | solution.py:18
  242.6 11.8 %collective-permute-start.43 = (bf16[32,32,128]{2,1,0:T(8,128)(2,1)S(1)}, bf16[32,32,128]{2,1,0:T(8,128)(2,1)S(1)}, u32[]{:S(2)}, u32[]{:S(2)}) collective-permute-start(bf16[32,32,128]{2,1,0:T(8,128)(2,1)S(1)} %collective-permute-done.41.refs_4_), channel_id=1, source_target_pairs={{0,2},{1,3},{2,0},{3,1},{4,6},{5,7},{6,4},{7,5},{8,10},{9,11},{10,... | collective-permute-start | bytes 786440 | tf_op jit(solution)/shard_map/ppermute | solution.py:18
  242.6 15.6 %collective-permute-start.42 = (bf16[32,32,128]{2,1,0:T(8,128)(2,1)S(1)}, bf16[32,32,128]{2,1,0:T(8,128)(2,1)S(1)}, u32[]{:S(2)}, u32[]{:S(2)}) collective-permute-start(bf16[32,32,128]{2,1,0:T(8,128)(2,1)S(1)} %collective-permute-done.41.refs_4_), channel_id=1, source_target_pairs={{0,1},{1,0},{2,3},{3,2},{4,5},{5,4},{6,7},{7,6},{8,9},{9,8},{10,11... | collective-permute-start | bytes 786440 | tf_op jit(solution)/shard_map/ppermute | solution.py:18
  (13 other events, 130.5 us)

commit v2 on v0

v2 whole, which is shorter than its diff:
```python
import functools

import jax
import jax.numpy as jnp
from jax import lax
from jax.experimental import pallas as pl
from jax.experimental.pallas import tpu as pltpu
from jax.sharding import Mesh, PartitionSpec as P

SHAPE = (4, 4, 2, 2, 4)
AXES = ("zl", "x", "core", "zh", "y")
VAR = ("zl", "x", "core")
SIZE = dict(zip(AXES, SHAPE))
MIB = 1024 * 1024
F32, BF16 = jnp.float32, jnp.bfloat16


def swap(value, axis, mask=1):
    return lax.ppermute(value, axis, [(i, i ^ mask) for i in range(SIZE[axis])])


def near4(value, axis):
    return [value] + [swap(value, axis, k) for k in (1, 2, 3)]


def after(value, other):
    return lax.optimization_barrier((value, other))[0]


def params(mib=56):
    return pltpu.CompilerParams(vmem_limit_bytes=mib * MIB)


SMEM = pl.BlockSpec(memory_space=pltpu.SMEM)
VMEM = pl.BlockSpec(memory_space=pltpu.VMEM)
HBM = pl.BlockSpec(memory_space=pl.ANY)


def part_kernel(where_ref, x_ref, x_other_ref, gate_ref, up_ref, theirs_ref, gain_ref, target_ref, out_ref):
    core = where_ref[2]
    lanes = gate_ref.shape[1] // 128
    mine = jnp.where(core == 0, gate_ref[...], up_ref[...])
    x = jnp.concatenate([x_ref[...], x_other_ref[...]]).T
    part = jnp.dot(x, jnp.concatenate([mine, theirs_ref[...]]), preferred_element_type=F32)
    target = target_ref[...].astype(F32)
    for slot in range(16):
        for e in range(2):
            for lane in range(lanes):
                at = slot * 16 + e * 8
                out_ref[slot, e * lanes + lane] = part[at : at + 8, lane * 128 : lane * 128 + 128]
        for half in range(2):
            at = ((slot // 4) % 2) * 256 + half * 128
            out_ref[slot, 2 * lanes + half] = target[:, at : at + 128]
        out_ref[slot, 2 * lanes + 2] = jnp.zeros((8, 128), F32)
        for lane in range(lanes):
            out_ref[slot, 2 * lanes + 2, lane : lane + 1, :] = gain_ref[:, lane * 128 : lane * 128 + 128]


def part_call(where, x, x_other, gate, up, theirs, gain, targets):
    lanes = gate.shape[1] // 128
    return pl.pallas_call(
        part_kernel,
        in_specs=[SMEM] + [VMEM] * 7,
        out_specs=VMEM,
        out_shape=jax.ShapeDtypeStruct((16, 2 * lanes + 3, 8, 128), F32),
        compiler_params=params(),
        name="part",
    )(where, x, x_other, gate, up, theirs, gain, targets)


def sum_kernel(where_ref, part_ref, out_ref, gain_ref, target_ref):
    lanes = out_ref.shape[1]
    for y in range(4):
        for e in range(2):
            for lane in range(lanes):
                t = e * lanes + lane
                total = (part_ref[y, t] + part_ref[4 + y, t]) + (part_ref[8 + y, t] + part_ref[12 + y, t])
                out_ref[:, lane, y * 2 + e, :] = total
    for s in range(16):
        gain_ref[s] = part_ref[s, 2 * lanes + 2]
    x, y = where_ref[0], where_ref[3]
    for high in range(2):
        for half in range(2):
            target_ref[high * 2 + half] = part_ref[y * 4 + high * 2 + x // 2, 2 * lanes + half]


def sum_call(where, part):
    lanes = (part.shape[1] - 3) // 2
    return pl.pallas_call(
        sum_kernel,
        in_specs=[SMEM, VMEM],
        out_specs=[VMEM] * 3,
        out_shape=[
            jax.ShapeDtypeStruct((8, lanes, 8, 128), F32),
            jax.ShapeDtypeStruct((16, 8, 128), F32),
            jax.ShapeDtypeStruct((4, 8, 128), F32),
        ],
        compiler_params=params(),
        name="sum_x",
    )(where, part)


def raw_kernel(where_ref, mine_ref, other_ref, out_ref):
    first = where_ref[2] == 0
    for zh in range(2):
        for lane in range(out_ref.shape[2]):
            mine = (mine_ref[zh * 4, lane] + mine_ref[zh * 4 + 1, lane]) + (mine_ref[zh * 4 + 2, lane] + mine_ref[zh * 4 + 3, lane])
            other = (other_ref[zh * 4, lane] + other_ref[zh * 4 + 1, lane]) + (other_ref[zh * 4 + 2, lane] + other_ref[zh * 4 + 3, lane])
            gate = jnp.where(first, mine, other)
            raw = jax.nn.silu(gate) * jnp.where(first, other, mine)
            for copy in range(4):
                out_ref[copy, zh, lane] = raw


def raw_call(where, mine, other):
    lanes = mine.shape[1]
    return pl.pallas_call(
        raw_kernel,
        in_specs=[SMEM, VMEM, VMEM],
        out_specs=VMEM,
        out_shape=jax.ShapeDtypeStruct((4, 2, lanes, 8, 128), F32),
        compiler_params=params(),
        name="raw",
    )(where, mine, other)


def output_kernel(where_ref, *refs):
    raw_refs, small_refs, mine_refs, theirs_refs = (refs[i : i + 4] for i in (0, 4, 8, 12))
    res_ref, own_refs = refs[16], refs[17:21]
    raw_all, small_all, down_all, hidden, total, raw_sem, small_sem, mine_sem, theirs_sem = refs[21:]
    x, zl, core, y, zh = (where_ref[i] for i in range(5))
    lanes = raw_all.shape[2]
    copies = []
    for k in range(4):
        copies.append([
            pltpu.make_async_copy(raw_refs[k], raw_all.at[pl.ds((x ^ k) * 4, 4)], raw_sem.at[k]),
            pltpu.make_async_copy(small_refs[k], small_all.at[zl ^ k], small_sem.at[k]),
            pltpu.make_async_copy(mine_refs[k], down_all.at[core, k], mine_sem.at[k]),
            pltpu.make_async_copy(theirs_refs[k], down_all.at[1 - core, k], theirs_sem.at[k]),
        ])
    for kind in range(2):
        for k in range(4):
            copies[k][kind].start()
    for k in range(4):
        copies[k][2].start()
        copies[k][3].start()
    for kind in range(2):
        for k in range(4):
            copies[k][kind].wait()
    for k in range(4):
        copies[k][2].wait()
        copies[k][3].wait()
        for a in range(2):
            unit = zh ^ a
            for e in range(2):
                for lane in range(lanes):
                    cols = slice(lane * 128, lane * 128 + 128)
                    raw = raw_all[:, unit, lane, (y ^ k) * 2 + e, :]
                    own_refs[k][a, e, :, cols] = raw
                    for v in range(16):
                        gain = small_all[v // 4, a, (v % 4) * 4 + (y ^ k), lane : lane + 1, :]
                        at = v * 32 + e * 16
                        hidden[at : at + 16, cols] = (raw * gain).astype(BF16)
            down = jnp.concatenate([down_all[0, k, a], down_all[1, k, a]], axis=1)
            term = jnp.dot(hidden[...], down, preferred_element_type=F32)
            if k == 0 and a == 0:
                total[...] = term
            else:
                total[...] += term
    source = (zl // 2) ^ zh
    for e in range(2):
        tile = 16 + 4 * jnp.where(core == e, 0, 1) + 2 * (zl % 2)
        for v in range(16):
            at = v * 32 + e * 16
            for half in range(2):
                cols = slice(half * 128, half * 128 + 128)
                target = small_all[:, source, tile + half, pl.ds(zh * 4, 4), :].reshape(16, 128)
                res_ref[v, e * 16 : e * 16 + 16, cols] = (total[at : at + 16, cols] - target).astype(BF16)


def output_call(where, raws, smalls, mine, theirs):
    lanes = raws[0].shape[2]
    width = lanes * 128
    return pl.pallas_call(
        output_kernel,
        in_specs=[SMEM] + [HBM] * 16,
        out_specs=[VMEM] * 5,
        out_shape=[jax.ShapeDtypeStruct((16, 32, 256), BF16)]
        + [jax.ShapeDtypeStruct((2, 2, 16, width), F32)] * 4,
        scratch_shapes=[
            pltpu.VMEM((16, 2, lanes, 8, 128), F32),
            pltpu.VMEM((4,) + smalls[0].shape, F32),
            pltpu.VMEM((2, 4) + mine[0].shape, BF16),
            pltpu.VMEM((512, width), BF16),
            pltpu.VMEM((512, 256), F32),
        ]
        + [pltpu.SemaphoreType.DMA((4,))] * 4,
        compiler_params=params(),
        cost_estimate=pl.CostEstimate(flops=2 * 512 * 8 * width * 256, bytes_accessed=6 * MIB, transcendentals=0),
        name="output",
    )(where, *raws, *smalls, *mine, *theirs)


def back_kernel(where_ref, *refs):
    res_ref, own_refs, mine_refs, theirs_refs, out_refs = refs[0], refs[1:5], refs[5:9], refs[9:13], refs[13:]
    first = where_ref[2] == 0
    for k in range(4):
        for a in range(2):
            mine, theirs = mine_refs[k][a], theirs_refs[k][a]
            down = jnp.concatenate([jnp.where(first, mine, theirs), jnp.where(first, theirs, mine)], axis=1)
            raw = jnp.concatenate([own_refs[k][a, 0], own_refs[k][a, 1]])
            for at in range(0, 16, 8):
                res = res_ref[at : at + 8].reshape(256, 256)
                back = lax.dot_general(res, down, (((1,), (1,)), ((), ())), preferred_element_type=F32)
                out_refs[k][a, at : at + 8, :] = jnp.sum(back.reshape(8, 32, -1) * raw[None], axis=1)


def back_call(where, res, owns, mine, theirs):
    width = owns[0].shape[3]
    return pl.pallas_call(
        back_kernel,
        in_specs=[SMEM] + [VMEM] * 13,
        out_specs=[VMEM] * 4,
        out_shape=[jax.ShapeDtypeStruct((2, 16, width), F32)] * 4,
        compiler_params=params(),
        cost_estimate=pl.CostEstimate(flops=2 * 512 * 8 * width * 256, bytes_accessed=6 * MIB, transcendentals=0),
        name="back",
    )(where, res, *owns, *mine, *theirs)


def pick_kernel(where_ref, *refs):
    for k in range(4):
        refs[4][k] = refs[k][1, where_ref[2]]


def pick_call(where, owns):
    shape = owns[0].shape
    return pl.pallas_call(
        pick_kernel,
        in_specs=[SMEM] + [VMEM] * 4,
        out_specs=VMEM,
        out_shape=jax.ShapeDtypeStruct((4,) + shape[2:], F32),
        compiler_params=params(),
        name="pick",
    )(where, *owns)


def grad_kernel(scale, where_ref, gain_ref, *refs):
    own_refs, far_ref, far_other_ref, res_refs = refs[:4], refs[4], refs[5], refs[6:14]
    out_ref, hidden_t, block = refs[14:]
    core = where_ref[2]
    some, rows, feats = res_refs[0].shape
    width = gain_ref.shape[1]

    @pl.when(pl.program_id(0) == 0)
    def _():
        for k in range(4):
            for e in range(2):
                far = jnp.where(core == e, far_ref[k], far_other_ref[k])
                for a, raw in enumerate((own_refs[k][0, e], far)):
                    at = (a * 4 + k) * rows + e * 16
                    block[at : at + 16, :width] = (raw * gain_ref[...]).astype(BF16)
        hidden_t[...] = block[:, :width].T

    for p in range(8):
        for q in range(some):
            block[p * rows : (p + 1) * rows, q * feats : (q + 1) * feats] = res_refs[p][q]
    grad = jnp.dot(hidden_t[...], block[:, : some * feats], preferred_element_type=F32)
    out_ref[0] = (grad * scale).astype(BF16)


def grad_call(where, gain, owns, far, far_other, res8, scale):
    width = gain.shape[1]
    blocks, rows, feats = res8[0].shape
    some = 2
    whole = lambda shape: pl.BlockSpec(shape, lambda s, w: (0,) * len(shape))
    return pl.pallas_call(
        functools.partial(grad_kernel, scale),
        grid_spec=pltpu.PrefetchScalarGridSpec(
            num_scalar_prefetch=1,
            grid=(blocks // some,),
            in_specs=[whole(gain.shape)]
            + [pl.BlockSpec((1,) + owns[0].shape[1:], lambda s, w: (0, 0, 0, 0))] * 4
            + [whole(far.shape)] * 2
            + [pl.BlockSpec((some, rows, feats), lambda s, w: (s, 0, 0))] * 8,
            out_specs=pl.BlockSpec((1, width, some * feats), lambda s, w: (0, 0, s)),
            scratch_shapes=[
                pltpu.VMEM((width, 8 * rows), BF16),
                pltpu.VMEM((8 * rows, max(width, some * feats)), BF16),
            ],
        ),
        out_shape=jax.ShapeDtypeStruct((1, width, blocks * feats), BF16),
        compiler_params=params(),
        cost_estimate=pl.CostEstimate(
            flops=2 * 8 * rows * width * blocks * feats, bytes_accessed=10 * MIB, transcendentals=0
        ),
        name="grad",
    )(where, gain, *owns, far, far_other, *res8)


def local(inputs, gate, up, down, targets, widths, gains):
    me = {a: lax.axis_index(a) for a in AXES}
    where = jnp.stack([me["x"], me["zl"], me["core"], me["y"], me["zh"]]).astype(jnp.int32)
    first = me["core"] == 0
    rows = inputs.shape[1]
    width = gate.shape[1]
    scale = 1.0 / rows**0.5

    column = (me["zh"] * 4 + me["y"]) * width + lax.broadcasted_iota(jnp.int32, (1, width), 1)
    kept = (column < widths[0]).astype(F32)
    gain = gains * kept

    theirs = swap(jnp.where(first, up, gate), "core")
    inputs_other = swap(inputs, "core")
    part = part_call(where, inputs, inputs_other, gate, up, theirs, gain, targets)
    down_pair = after(down, part)
    part = lax.all_to_all(part, ("x", "y"), 0, 0, tiled=True)
    part, gain_xy, target_xy = sum_call(where, part)
    part = lax.all_to_all(part, ("zh", "zl"), 0, 0, tiled=True)
    raw = raw_call(where, part, swap(part, "core"))
    raws = near4(lax.all_to_all(raw, "zl", 0, 0, tiled=True), "x")

    small = jnp.concatenate([gain_xy, target_xy, swap(target_xy, "core")])
    smalls = near4(jnp.stack([small, swap(small, "zh")]), "zl")

    down_pair = jnp.stack([down_pair, swap(down_pair, "zh")])
    mine = near4(down_pair, "y")
    theirs = [swap(d, "core") for d in mine]

    res, *owns = output_call(where, raws, smalls, mine, theirs)
    res_own = lax.all_to_all(res, ("zl", "x"), 0, 0, tiled=True)
    res8 = near4(res_own, "y") + near4(swap(res_own, "zh"), "y")

    got = [owns[0]] + [swap(owns[k], "y", k) for k in (1, 2, 3)]
    far = swap(pick_call(where, got), "zh")
    grad_down = grad_call(where, gain, got, far, swap(far, "core"), res8, scale)

    sums = back_call(where, after(res, res_own), owns, mine, theirs)
    sums = sums[0] + swap(sums[1], "y", 1) + swap(sums[2], "y", 2) + swap(sums[3], "y", 3)
    sums = sums[0] + swap(sums[1], "zh")
    sums = jnp.sum(lax.all_to_all(sums, ("zl", "x"), 0, 0, tiled=True), axis=0, keepdims=True)
    return grad_down, kept * sums * scale


def solution(mesh):
    fine = Mesh(mesh.devices.reshape(SHAPE), AXES)
    tp = ("zh", "y")
    return jax.shard_map(
        local,
        mesh=fine,
        in_specs=(P(VAR, None), P(VAR, tp), P(VAR, tp), P(tp, VAR), P(VAR, tp), P(VAR), P(VAR, tp)),
        out_specs=(P(VAR, tp, None), P(VAR, tp)),
        check_vma=False,
    )
```

time: 590 us -> 204 us (0.35)
  waiting for transfers between devices: 496 us -> 56.7 us
  starting transfers between devices: 0.23 us -> 82.2 us
  matrix products: 32.8 us -> 0 us
  Pallas kernels: 0 us -> 32.6 us
  blocking collectives: 43.6 us -> 17.5 us
  between operations: 14.8 us -> 1.68 us
  local copies, waits for them, and re-layouts: 0.01 us -> 6.8 us
    all_gather x5 -> x0, waiting for transfers between devices: 297 us -> none  [the longest x1 77.7 us: local(): down_whole = lax.all_gather(down_parent, 'var', axis=1, tiled=True)]
    psum x1 -> x0, waiting for transfers between devices: 197 us -> none  [local(): output = lax.psum(partial_value, 'tp')]
    ppermute x0 -> x35, starting transfers between devices: none -> 56.1 us  [swap(): return lax.ppermute(value, axis, [(i, i ^ mask) for i in range(SIZE[axis])])]
    all_gather x1 -> x0, blocking collectives: 43.6 us -> none  [local(): target_part = lax.all_gather(targets, 'var', axis=0, tiled=True)]
    dot_general x5 -> x0, matrix products: 32.8 us -> none  [the longest x1 7.45 us: local(): lax.dot_general(residual, down_whole, (((1,), (1,)), ((), ())), preferred...]
    pallas_call x0 -> x7, Pallas kernels: none -> 32.6 us  [the longest x1 9.41 us: output_call(): pl.pallas_call(output_kernel, in_specs=[SMEM] + [HBM] * 16, out_specs=[VM...]
    ppermute x0 -> x35, waiting for transfers between devices: none -> 32.3 us  [swap(): return lax.ppermute(value, axis, [(i, i ^ mask) for i in range(SIZE[axis])])]
    all_to_all x0 -> x4, starting transfers between devices: none -> 26.2 us  [the longest x1 8.6 us: local(): part = lax.all_to_all(part, ('zh', 'zl'), 0, 0, tiled=True)]
  transfers between devices with their start and end apart: 6 -> 39, of which waited for: 6 -> 12; matrix products, arithmetic and copies ran while one was open for 4% -> 2% of each run, Pallas kernels for 0% -> 6%
where the time goes in v2:
time: 204 us; the launch traced here: 201 us
  starting transfers between devices  82.2 us (40%)
  waiting for transfers between devices  56.7 us (28%)
  Pallas kernels  32.6 us (16%)
  blocking collectives  17.5 us (9%)
  local copies, waits for them, and re-layouts  6.8 us (3%)
  other arithmetic  3.9 us (2%)
    ppermute x35, starting transfers between devices, swap(): return lax.ppermute(value, axis, [(i, i ^ mask) for i in range(SIZE[axis])])  56.1 us
    ppermute x35, waiting for transfers between devices, swap(): return lax.ppermute(value, axis, [(i, i ^ mask) for i in range(SIZE[axis])])  32.3 us
    all_to_all x1, blocking collectives, local(): lax.all_to_all(sums, ('zl', 'x'), 0, 0, tiled=True)  17.5 us
    all_to_all x1, waiting for transfers between devices, local(): raws = near4(lax.all_to_all(raw, 'zl', 0, 0, tiled=True), 'x')  9.76 us
    pallas_call x1, Pallas kernels, output_call(): pl.pallas_call(output_kernel, in_specs=[SMEM] + [HBM] * 16, out_specs=[VM...  9.41 us
    pallas_call x1, Pallas kernels, grad_call(): pl.pallas_call(functools.partial(grad_kernel, scale), grid_spec=pltpu.Pre...  9.1 us
    all_to_all x1, waiting for transfers between devices, local(): part = lax.all_to_all(part, ('x', 'y'), 0, 0, tiled=True)  8.75 us
    all_to_all x1, starting transfers between devices, local(): part = lax.all_to_all(part, ('zh', 'zl'), 0, 0, tiled=True)  8.6 us
  transfers between devices with their start and end apart: 39, of which 12 were waited for; matrix products, arithmetic and copies ran while one was open for 2% of the time, Pallas kernels for 6%

profile of v2, /device:TPU:2, one launch (start us, length us, event | category | flops | bytes accessed | tf_op | source)
XLA Modules:
  0.0 201.4 jit_solution(6311274553217192069)
XLA Ops:
  0.6 1.0 broadcast_select_fusion
  2.9 1.3 compare_select_fusion.1.gain_ref
  5.4 0.7 copy-done.19
  6.1 2.6 %part.1 = f32[16,17,8,128]{3,2,1,0:T(8,128)} custom-call(s32[5]{0:T(128)} %stack.41.where_ref, bf16[128,256]{1,0:T(8,128)(2,1)} %x_ref.1, bf16[128,256]{1,0:T(8,128)(2,1)} %copy-done.22, bf16[128,896]{1,0:T(8,128)(2,1)} %gate_ref.1, bf16[128,896]{1,0:T(8,128)(2,1)} %up_ref.1, bf16[128,896]{1,0:T(8,128)(2,1)} %copy-done.19, ...), custom_call_target="tpu_custom_call" | custom-call | tf_op jit(solution)/shard_map/part/pallas_call | solution.py:61
  8.7 7.6 %all-to-all-start = ((f32[16,17,8,128]{3,2,1,0:T(8,128)}), f32[16,17,8,128]{3,2,1,0:T(8,128)S(1)}, u32[]{:S(2)}, u32[]{:S(2)}) async-start(f32[16,17,8,128]{3,2,1,0:T(8,128)} %part.1), calls=%async_computation | async-start | bytes 2228224 | tf_op jit(solution)/shard_map/all_to_all | solution.py:317
  16.3 7.3 %collective-permute-start.11 = (bf16[896,128]{1,0:T(8,128)(2,1)S(1)}, bf16[896,128]{1,0:T(8,128)(2,1)S(1)}, u32[]{:S(2)}, u32[]{:S(2)}) collective-permute-start(bf16[896,128]{1,0:T(8,128)(2,1)S(1)} %copy-done.14), channel_id=1, source_target_pairs={{0,4},{4,0},{1,5},{5,1},{2,6},{6,2},{3,7},{7,3},{8,12},{12,8},{9,1... | collective-permute-start | bytes 688136 | tf_op jit(solution)/shard_map/ppermute | solution.py:19
  23.6 8.7 %all-to-all-done.part_ref = f32[16,17,8,128]{3,2,1,0:T(8,128)S(1)} async-done(((f32[16,17,8,128]{3,2,1,0:T(8,128)}), f32[16,17,8,128]{3,2,1,0:T(8,128)S(1)}, u32[]{:S(2)}, u32[]{:S(2)}) %all-to-all-start) | async-done | bytes 1114144 | tf_op jit(solution)/shard_map/all_to_all | solution.py:317
  32.3 1.0 copy-done
  33.3 2.1 %sum_x.1 = (f32[8,7,8,128]{3,2,1,0:T(8,128)}, f32[16,8,128]{2,1,0:T(8,128)}, f32[4,8,128]{2,1,0:T(8,128)}) custom-call(s32[5]{0:T(128)} %stack.41.where_ref, f32[16,17,8,128]{3,2,1,0:T(8,128)} %copy-done), custom_call_target="tpu_custom_call" | custom-call | tf_op jit(solution)/shard_map/sum_x/pallas_call | solution.py:89
  35.4 8.6 %all-to-all-start.1 = ((f32[8,7,8,128]{3,2,1,0:T(8,128)}), f32[8,7,8,128]{3,2,1,0:T(8,128)S(1)}, u32[]{:S(2)}, u32[]{:S(2)}) async-start(f32[8,7,8,128]{3,2,1,0:T(8,128)} %get-tuple-element.16), calls=%async_computation.1 | async-start | bytes 458752 | tf_op jit(solution)/shard_map/all_to_all | solution.py:319
  44.1 1.5 collective-permute-start.14
  45.6 1.2 collective-permute-start.13
  46.8 1.5 collective-permute-start.12
  48.3 5.9 %all-to-all-done.1.mine_ref = f32[8,7,8,128]{3,2,1,0:T(8,128)S(1)} async-done(((f32[8,7,8,128]{3,2,1,0:T(8,128)}), f32[8,7,8,128]{3,2,1,0:T(8,128)S(1)}, u32[]{:S(2)}, u32[]{:S(2)}) %all-to-all-start.1) | async-done | bytes 229408 | tf_op jit(solution)/shard_map/all_to_all | solution.py:319
  54.2 11.6 %collective-permute-done.14.refs_11_.refs_8_ = bf16[2,896,128]{2,1,0:T(8,128)(2,1)S(1)} collective-permute-done((bf16[2,896,128]{2,1,0:T(8,128)(2,1)S(1)}, bf16[2,896,128]{2,1,0:T(8,128)(2,1)S(1)}, u32[]{:S(2)}, u32[]{:S(2)}) %collective-permute-start.14) | collective-permute-done | bytes 458784 | tf_op jit(solution)/shard_map/ppermute | solution.py:19
  66.9 5.7 %collective-permute-start.7 = (f32[24,8,128]{2,1,0:T(8,128)S(1)}, f32[24,8,128]{2,1,0:T(8,128)S(1)}, u32[]{:S(2)}, u32[]{:S(2)}) collective-permute-start(f32[24,8,128]{2,1,0:T(8,128)S(1)} %constant_dynamic-update-slice_fusion), channel_id=1, source_target_pairs={{0,4},{4,0},{1,5},{5,1},{2,6},{6,2},{3,7},{7,3},{8,12},{12,8},{9,1... | collective-permute-start | bytes 294920 | tf_op jit(solution)/shard_map/ppermute | solution.py:19
  72.6 1.8 raw.1
  74.4 3.4 %all-to-all-start.2 = ((f32[4,2,7,8,128]{4,3,2,1,0:T(8,128)}), f32[4,2,7,8,128]{4,3,2,1,0:T(8,128)S(1)}, u32[]{:S(2)}, u32[]{:S(2)}) async-start(f32[4,2,7,8,128]{4,3,2,1,0:T(8,128)} %raw.1), calls=%async_computation.2 | async-start | bytes 458752 | tf_op jit(solution)/shard_map/all_to_all | solution.py:321
  77.9 3.9 %collective-permute-start.10 = (f32[2,24,8,128]{3,2,1,0:T(8,128)S(1)}, f32[2,24,8,128]{3,2,1,0:T(8,128)S(1)}, u32[]{:S(2)}, u32[]{:S(2)}) collective-permute-start(f32[2,24,8,128]{3,2,1,0:T(8,128)S(1)} %pad_maximum_fusion.1.refs_4_), channel_id=1, source_target_pairs={{0,192},{64,128},{128,64},{192,0},{1,193},{65,129},{129,65},{193,1... | collective-permute-start | bytes 589832 | tf_op jit(solution)/shard_map/ppermute | solution.py:19
  81.7 9.8 %all-to-all-done.2.refs_0_ = f32[4,2,7,8,128]{4,3,2,1,0:T(8,128)S(1)} async-done(((f32[4,2,7,8,128]{4,3,2,1,0:T(8,128)}), f32[4,2,7,8,128]{4,3,2,1,0:T(8,128)S(1)}, u32[]{:S(2)}, u32[]{:S(2)}) %all-to-all-start.2) | async-done | bytes 229408 | tf_op jit(solution)/shard_map/all_to_all | solution.py:321
  91.5 1.2 collective-permute-start.5
  92.7 2.6 %collective-permute-start.4 = (f32[4,2,7,8,128]{4,3,2,1,0:T(8,128)S(1)}, f32[4,2,7,8,128]{4,3,2,1,0:T(8,128)S(1)}, u32[]{:S(2)}, u32[]{:S(2)}) collective-permute-start(f32[4,2,7,8,128]{4,3,2,1,0:T(8,128)S(1)} %all-to-all-done.2.refs_0_), channel_id=1, source_target_pairs={{0,32},{16,48},{32,0},{48,16},{1,33},{17,49},{33,1},{49,17},{2,34}... | collective-permute-start | bytes 688136 | tf_op jit(solution)/shard_map/ppermute | solution.py:19
  95.6 3.7 %collective-permute-start.8 = (f32[2,24,8,128]{3,2,1,0:T(8,128)S(1)}, f32[2,24,8,128]{3,2,1,0:T(8,128)S(1)}, u32[]{:S(2)}, u32[]{:S(2)}) collective-permute-start(f32[2,24,8,128]{3,2,1,0:T(8,128)S(1)} %pad_maximum_fusion.1.refs_4_), channel_id=1, source_target_pairs={{0,64},{64,0},{128,192},{192,128},{1,65},{65,1},{129,193},{193,129... | collective-permute-start | bytes 589832 | tf_op jit(solution)/shard_map/ppermute | solution.py:19
  99.3 5.1 %collective-permute-done.9.refs_6_ = f32[2,24,8,128]{3,2,1,0:T(8,128)S(1)} collective-permute-done((f32[2,24,8,128]{3,2,1,0:T(8,128)S(1)}, f32[2,24,8,128]{3,2,1,0:T(8,128)S(1)}, u32[]{:S(2)}, u32[]{:S(2)}) %collective-permute-start.9) | collective-permute-done | bytes 196640 | tf_op jit(solution)/shard_map/ppermute | solution.py:19
  105.4 0.7 copy-done.30
  106.1 9.4 %output.1 = (bf16[16,32,256]{2,1,0:T(8,128)(2,1)}, f32[2,2,16,896]{3,2,1,0:T(8,128)}, f32[2,2,16,896]{3,2,1,0:T(8,128)}, f32[2,2,16,896]{3,2,1,0:T(8,128)}, f32[2,2,16,896]{3,2,1,0:T(8,128)}) custom-call(s32[5]{0:T(128)} %stack.41.where_ref, f32[4,2,7,8,128]{4,3,2,1,0:T(8,128)} %copy-done.15, f32[4,2,7,8,128]{4,3,2,1,0:T(8,128)} %copy-done.30, ...), custom_call_target="tpu_custom_call" | custom-call | flops 1879048192 | bytes 6291456 | tf_op jit(solution)/shard_map/output/pallas_call | solution.py:184
  115.5 6.6 %all-to-all-start.3 = ((bf16[16,32,256]{2,1,0:T(8,128)(2,1)}), bf16[16,32,256]{2,1,0:T(8,128)(2,1)S(1)}, u32[]{:S(2)}, u32[]{:S(2)}) async-start(bf16[16,32,256]{2,1,0:T(8,128)(2,1)} %get-tuple-element.25.refs_0_), calls=%async_computation.3 | async-start | bytes 524288 | tf_op jit(solution)/shard_map/all_to_all | solution.py:331
  122.6 2.5 %collective-permute-start.20 = (f32[2,2,16,896]{3,2,1,0:T(8,128)}, f32[2,2,16,896]{3,2,1,0:T(8,128)S(1)}, u32[]{:S(2)}, u32[]{:S(2)}) collective-permute-start(f32[2,2,16,896]{3,2,1,0:T(8,128)} %get-tuple-element.22.refs_3_), channel_id=1, source_target_pairs={{0,2},{1,3},{2,0},{3,1},{4,6},{5,7},{6,4},{7,5},{8,10},{9,11},{10,... | collective-permute-start | bytes 688136 | tf_op jit(solution)/shard_map/ppermute | solution.py:19
  125.2 1.6 collective-permute-start.21
  126.7 1.5 collective-permute-done.19.refs_1_
  128.3 3.6 %collective-permute-done.20.refs_2_ = f32[2,2,16,896]{3,2,1,0:T(8,128)S(1)} collective-permute-done((f32[2,2,16,896]{3,2,1,0:T(8,128)}, f32[2,2,16,896]{3,2,1,0:T(8,128)S(1)}, u32[]{:S(2)}, u32[]{:S(2)}) %collective-permute-start.20) | collective-permute-done | bytes 229408 | tf_op jit(solution)/shard_map/ppermute | solution.py:19
  131.9 2.4 %collective-permute-done.21.refs_3_ = f32[2,2,16,896]{3,2,1,0:T(8,128)S(1)} collective-permute-done((f32[2,2,16,896]{3,2,1,0:T(8,128)}, f32[2,2,16,896]{3,2,1,0:T(8,128)S(1)}, u32[]{:S(2)}, u32[]{:S(2)}) %collective-permute-start.21) | collective-permute-done | bytes 229408 | tf_op jit(solution)/shard_map/ppermute | solution.py:19
  135.0 2.0 pick.1
  137.0 4.2 %collective-permute-start.22 = (f32[4,16,896]{2,1,0:T(8,128)}, f32[4,16,896]{2,1,0:T(8,128)S(1)}, u32[]{:S(2)}, u32[]{:S(2)}) collective-permute-start(f32[4,16,896]{2,1,0:T(8,128)} %pick.1), channel_id=1, source_target_pairs={{0,4},{4,0},{1,5},{5,1},{2,6},{6,2},{3,7},{7,3},{8,12},{12,8},{9,1... | collective-permute-start | bytes 688136 | tf_op jit(solution)/shard_map/ppermute | solution.py:19
  141.2 5.6 %back.1 = (f32[2,16,896]{2,1,0:T(8,128)}, f32[2,16,896]{2,1,0:T(8,128)}, f32[2,16,896]{2,1,0:T(8,128)}, f32[2,16,896]{2,1,0:T(8,128)}) custom-call(s32[5]{0:T(128)} %stack.41.where_ref, bf16[16,32,256]{2,1,0:T(8,128)(2,1)} %get-tuple-element.25.refs_0_, f32[2,2,16,896]{3,2,1,0:T(8,128)} %get-tuple-element.20.refs_0_.refs_1_, ...), custom_call_target="tpu_custom_call" | custom-call | flops 1879048192 | bytes 6291456 | tf_op jit(solution)/shard_map/back/pallas_call | solution.py:220
  146.8 3.0 %collective-permute-start.32 = (f32[2,16,896]{2,1,0:T(8,128)}, f32[2,16,896]{2,1,0:T(8,128)S(1)}, u32[]{:S(2)}, u32[]{:S(2)}) collective-permute-start(f32[2,16,896]{2,1,0:T(8,128)} %get-tuple-element.28), channel_id=1, source_target_pairs={{0,2},{1,3},{2,0},{3,1},{4,6},{5,7},{6,4},{7,5},{8,10},{9,11},{10,... | collective-permute-start | bytes 344072 | tf_op jit(solution)/shard_map/ppermute | solution.py:19
  149.9 1.6 collective-permute-start.33
  151.5 4.8 %collective-permute-start.27 = (bf16[16,32,256]{2,1,0:T(8,128)(2,1)S(1)}, bf16[16,32,256]{2,1,0:T(8,128)(2,1)S(1)}, u32[]{:S(2)}, u32[]{:S(2)}) collective-permute-start(bf16[16,32,256]{2,1,0:T(8,128)(2,1)S(1)} %all-to-all-done.3.refs_6_), channel_id=1, source_target_pairs={{0,4},{4,0},{1,5},{5,1},{2,6},{6,2},{3,7},{7,3},{8,12},{12,8},{9,1... | collective-permute-start | bytes 786440 | tf_op jit(solution)/shard_map/ppermute | solution.py:19
  156.4 1.6 collective-permute-start.26
  158.0 0.9 add_add_fusion
  158.9 1.5 collective-permute-start.34
  160.4 6.9 %collective-permute-done.34 = f32[16,896]{1,0:T(8,128)S(1)} collective-permute-done((f32[16,896]{1,0:T(8,128)S(1)}, f32[16,896]{1,0:T(8,128)S(1)}, u32[]{:S(2)}, u32[]{:S(2)}) %collective-permute-start.34) | collective-permute-done | bytes 57376 | tf_op jit(solution)/shard_map/ppermute | solution.py:19
  167.3 1.7 collective-permute-start.30
  169.1 2.3 %collective-permute-start.29 = (bf16[16,32,256]{2,1,0:T(8,128)(2,1)S(1)}, bf16[16,32,256]{2,1,0:T(8,128)(2,1)S(1)}, u32[]{:S(2)}, u32[]{:S(2)}) collective-permute-start(bf16[16,32,256]{2,1,0:T(8,128)(2,1)S(1)} %collective-permute-done.27.refs_10_), channel_id=1, source_target_pairs={{0,2},{1,3},{2,0},{3,1},{4,6},{5,7},{6,4},{7,5},{8,10},{9,11},{10,... | collective-permute-start | bytes 786440 | tf_op jit(solution)/shard_map/ppermute | solution.py:19
  171.4 0.9 collective-permute-done.26.refs_9_
  172.4 17.5 %all_to_all.29 = f32[16,1,896]{2,1,0:T(1,128)S(1)} all-to-all(f32[16,1,896]{2,1,0:T(1,128)S(1)} %copy.9), channel_id=1, replica_groups=mesh['zl'=4,'x'=4,'core'=2,'zh'=2,'y'=4] {'zl','x'}, dimensions={0} | all-to-all | bytes 114688 | tf_op jit(solution)/shard_map/all_to_all | solution.py:341
  191.6 0.7 copy-done.13
  192.3 9.1 %grad.1 = bf16[1,896,4096]{2,1,0:T(8,128)(2,1)} custom-call(s32[5]{0:T(128)} %stack.41.where_ref, f32[1,896]{1,0:T(1,128)} %compare_select_fusion.1.gain_ref, f32[2,2,16,896]{3,2,1,0:T(8,128)} %get-tuple-element.20.refs_0_.refs_1_, f32[2,2,16,896]{3,2,1,0:T(8,128)} %copy-done.3, f32[2,2,16,896]{3,2,1,0:T(8,128)} %copy-done.4, f32[2,2,16,896]{3,2,1,0:T(8,128)} %copy-done.5, ...), custom_call_target="tpu_custom_call" | custom-call | flops 1879048192 | bytes 10485760 | tf_op jit(solution)/shard_map/grad/pallas_call | solution.py:277
  (120 shorter events, 7.2 us)
Async XLA Ops:
  1.6 3.2 %collective-permute-start.1 = (bf16[128,896]{1,0:T(8,128)(2,1)S(1)}, bf16[128,896]{1,0:T(8,128)(2,1)S(1)}, u32[]{:S(2)}, u32[]{:S(2)}) collective-permute-start(bf16[128,896]{1,0:T(8,128)(2,1)S(1)} %broadcast_select_fusion), channel_id=1, source_target_pairs={{0,8},{8,0},{1,9},{9,1},{2,10},{10,2},{3,11},{11,3},{4,12},{12,4},... | collective-permute-start | bytes 688136 | tf_op jit(solution)/shard_map/ppermute | solution.py:19
  1.7 3.1 %collective-permute-start = (bf16[128,256]{1,0:T(8,128)(2,1)}, bf16[128,256]{1,0:T(8,128)(2,1)S(1)}, u32[]{:S(2)}, u32[]{:S(2)}) collective-permute-start(bf16[128,256]{1,0:T(8,128)(2,1)} %x_ref.1), channel_id=1, source_target_pairs={{0,8},{8,0},{1,9},{9,1},{2,10},{10,2},{3,11},{11,3},{4,12},{12,4},... | collective-permute-start | bytes 196616 | tf_op jit(solution)/shard_map/ppermute | solution.py:19
  8.7 23.6 %all-to-all-start = ((f32[16,17,8,128]{3,2,1,0:T(8,128)}), f32[16,17,8,128]{3,2,1,0:T(8,128)S(1)}, u32[]{:S(2)}, u32[]{:S(2)}) async-start(f32[16,17,8,128]{3,2,1,0:T(8,128)} %part.1), calls=%async_computation | async-start | bytes 2228224 | tf_op jit(solution)/shard_map/all_to_all | solution.py:317
  16.3 27.7 %collective-permute-start.11 = (bf16[896,128]{1,0:T(8,128)(2,1)S(1)}, bf16[896,128]{1,0:T(8,128)(2,1)S(1)}, u32[]{:S(2)}, u32[]{:S(2)}) collective-permute-start(bf16[896,128]{1,0:T(8,128)(2,1)S(1)} %copy-done.14), channel_id=1, source_target_pairs={{0,4},{4,0},{1,5},{5,1},{2,6},{6,2},{3,7},{7,3},{8,12},{12,8},{9,1... | collective-permute-start | bytes 688136 | tf_op jit(solution)/shard_map/ppermute | solution.py:19
  35.4 18.7 %all-to-all-start.1 = ((f32[8,7,8,128]{3,2,1,0:T(8,128)}), f32[8,7,8,128]{3,2,1,0:T(8,128)S(1)}, u32[]{:S(2)}, u32[]{:S(2)}) async-start(f32[8,7,8,128]{3,2,1,0:T(8,128)} %get-tuple-element.16), calls=%async_computation.1 | async-start | bytes 458752 | tf_op jit(solution)/shard_map/all_to_all | solution.py:319
  44.1 60.5 %copy-start.6 = (bf16[2,896,128]{2,1,0:T(8,128)(2,1)}, bf16[2,896,128]{2,1,0:T(8,128)(2,1)S(1)}, u32[]{:S(2)}) copy-start(bf16[2,896,128]{2,1,0:T(8,128)(2,1)S(1)} %pad_maximum_fusion.refs_8_.refs_5_) | copy-start | bytes 1376260
  44.1 21.7 %collective-permute-start.14 = (bf16[2,896,128]{2,1,0:T(8,128)(2,1)S(1)}, bf16[2,896,128]{2,1,0:T(8,128)(2,1)S(1)}, u32[]{:S(2)}, u32[]{:S(2)}) collective-permute-start(bf16[2,896,128]{2,1,0:T(8,128)(2,1)S(1)} %pad_maximum_fusion.refs_8_.refs_5_), channel_id=1, source_target_pairs={{0,3},{1,2},{2,1},{3,0},{4,7},{5,6},{6,5},{7,4},{8,11},{9,10},{10,... | collective-permute-start | bytes 1376264 | tf_op jit(solution)/shard_map/ppermute | solution.py:19
  45.6 20.2 %collective-permute-start.13 = (bf16[2,896,128]{2,1,0:T(8,128)(2,1)S(1)}, bf16[2,896,128]{2,1,0:T(8,128)(2,1)S(1)}, u32[]{:S(2)}, u32[]{:S(2)}) collective-permute-start(bf16[2,896,128]{2,1,0:T(8,128)(2,1)S(1)} %pad_maximum_fusion.refs_8_.refs_5_), channel_id=1, source_target_pairs={{0,2},{1,3},{2,0},{3,1},{4,6},{5,7},{6,4},{7,5},{8,10},{9,11},{10,... | collective-permute-start | bytes 1376264 | tf_op jit(solution)/shard_map/ppermute | solution.py:19
  46.8 19.6 %collective-permute-start.12 = (bf16[2,896,128]{2,1,0:T(8,128)(2,1)S(1)}, bf16[2,896,128]{2,1,0:T(8,128)(2,1)S(1)}, u32[]{:S(2)}, u32[]{:S(2)}) collective-permute-start(bf16[2,896,128]{2,1,0:T(8,128)(2,1)S(1)} %pad_maximum_fusion.refs_8_.refs_5_), channel_id=1, source_target_pairs={{0,1},{1,0},{2,3},{3,2},{4,5},{5,4},{6,7},{7,6},{8,9},{9,8},{10,11... | collective-permute-start | bytes 1376264 | tf_op jit(solution)/shard_map/ppermute | solution.py:19
  48.3 18.1 %collective-permute-start.6 = (f32[4,8,128]{2,1,0:T(8,128)S(1)}, f32[4,8,128]{2,1,0:T(8,128)S(1)}, u32[]{:S(2)}, u32[]{:S(2)}) collective-permute-start(f32[4,8,128]{2,1,0:T(8,128)S(1)} %copy-done.23), channel_id=1, source_target_pairs={{0,8},{8,0},{1,9},{9,1},{2,10},{10,2},{3,11},{11,3},{4,12},{12,4},... | collective-permute-start | bytes 49160 | tf_op jit(solution)/shard_map/ppermute | solution.py:19
  54.1 12.8 %collective-permute-start.2 = (f32[8,7,8,128]{3,2,1,0:T(8,128)S(1)}, f32[8,7,8,128]{3,2,1,0:T(8,128)S(1)}, u32[]{:S(2)}, u32[]{:S(2)}) collective-permute-start(f32[8,7,8,128]{3,2,1,0:T(8,128)S(1)} %all-to-all-done.1.mine_ref), channel_id=1, source_target_pairs={{0,8},{8,0},{1,9},{9,1},{2,10},{10,2},{3,11},{11,3},{4,12},{12,4},... | collective-permute-start | bytes 688136 | tf_op jit(solution)/shard_map/ppermute | solution.py:19
  65.8 38.8 %copy-start.24 = (bf16[2,896,128]{2,1,0:T(8,128)(2,1)}, bf16[2,896,128]{2,1,0:T(8,128)(2,1)S(1)}, u32[]{:S(2)}) copy-start(bf16[2,896,128]{2,1,0:T(8,128)(2,1)S(1)} %collective-permute-done.14.refs_11_.refs_8_) | copy-start | bytes 1376260
  65.8 16.0 %collective-permute-start.15 = (bf16[2,896,128]{2,1,0:T(8,128)(2,1)S(1)}, bf16[2,896,128]{2,1,0:T(8,128)(2,1)S(1)}, u32[]{:S(2)}, u32[]{:S(2)}) collective-permute-start(bf16[2,896,128]{2,1,0:T(8,128)(2,1)S(1)} %pad_maximum_fusion.refs_8_.refs_5_), channel_id=1, source_target_pairs={{0,8},{8,0},{1,9},{9,1},{2,10},{10,2},{3,11},{11,3},{4,12},{12,4},... | collective-permute-start | bytes 1376264 | tf_op jit(solution)/shard_map/ppermute | solution.py:19
  65.8 38.8 %copy-start.25 = (bf16[2,896,128]{2,1,0:T(8,128)(2,1)}, bf16[2,896,128]{2,1,0:T(8,128)(2,1)S(1)}, u32[]{:S(2)}) copy-start(bf16[2,896,128]{2,1,0:T(8,128)(2,1)S(1)} %collective-permute-done.13.refs_10_.refs_7_) | copy-start | bytes 1376260
  65.8 26.9 %collective-permute-start.18 = (bf16[2,896,128]{2,1,0:T(8,128)(2,1)S(1)}, bf16[2,896,128]{2,1,0:T(8,128)(2,1)}, u32[]{:S(2)}, u32[]{:S(2)}) collective-permute-start(bf16[2,896,128]{2,1,0:T(8,128)(2,1)S(1)} %collective-permute-done.14.refs_11_.refs_8_), channel_id=1, source_target_pairs={{0,8},{8,0},{1,9},{9,1},{2,10},{10,2},{3,11},{11,3},{4,12},{12,4},... | collective-permute-start | bytes 1376264 | tf_op jit(solution)/shard_map/ppermute | solution.py:19
  66.4 38.2 %copy-start.26 = (bf16[2,896,128]{2,1,0:T(8,128)(2,1)}, bf16[2,896,128]{2,1,0:T(8,128)(2,1)S(1)}, u32[]{:S(2)}) copy-start(bf16[2,896,128]{2,1,0:T(8,128)(2,1)S(1)} %collective-permute-done.12.refs_9_.refs_6_) | copy-start | bytes 1376260
  66.4 29.0 %collective-permute-start.17 = (bf16[2,896,128]{2,1,0:T(8,128)(2,1)S(1)}, bf16[2,896,128]{2,1,0:T(8,128)(2,1)}, u32[]{:S(2)}, u32[]{:S(2)}) collective-permute-start(bf16[2,896,128]{2,1,0:T(8,128)(2,1)S(1)} %collective-permute-done.13.refs_10_.refs_7_), channel_id=1, source_target_pairs={{0,8},{8,0},{1,9},{9,1},{2,10},{10,2},{3,11},{11,3},{4,12},{12,4},... | collective-permute-start | bytes 1376264 | tf_op jit(solution)/shard_map/ppermute | solution.py:19
  66.4 29.2 %collective-permute-start.16 = (bf16[2,896,128]{2,1,0:T(8,128)(2,1)S(1)}, bf16[2,896,128]{2,1,0:T(8,128)(2,1)}, u32[]{:S(2)}, u32[]{:S(2)}) collective-permute-start(bf16[2,896,128]{2,1,0:T(8,128)(2,1)S(1)} %collective-permute-done.12.refs_9_.refs_6_), channel_id=1, source_target_pairs={{0,8},{8,0},{1,9},{9,1},{2,10},{10,2},{3,11},{11,3},{4,12},{12,4},... | collective-permute-start | bytes 1376264 | tf_op jit(solution)/shard_map/ppermute | solution.py:19
  66.9 10.9 %collective-permute-start.7 = (f32[24,8,128]{2,1,0:T(8,128)S(1)}, f32[24,8,128]{2,1,0:T(8,128)S(1)}, u32[]{:S(2)}, u32[]{:S(2)}) collective-permute-start(f32[24,8,128]{2,1,0:T(8,128)S(1)} %constant_dynamic-update-slice_fusion), channel_id=1, source_target_pairs={{0,4},{4,0},{1,5},{5,1},{2,6},{6,2},{3,7},{7,3},{8,12},{12,8},{9,1... | collective-permute-start | bytes 294920 | tf_op jit(solution)/shard_map/ppermute | solution.py:19
  74.4 17.1 %all-to-all-start.2 = ((f32[4,2,7,8,128]{4,3,2,1,0:T(8,128)}), f32[4,2,7,8,128]{4,3,2,1,0:T(8,128)S(1)}, u32[]{:S(2)}, u32[]{:S(2)}) async-start(f32[4,2,7,8,128]{4,3,2,1,0:T(8,128)} %raw.1), calls=%async_computation.2 | async-start | bytes 458752 | tf_op jit(solution)/shard_map/all_to_all | solution.py:321
  77.8 26.8 %copy-start.20 = (f32[2,24,8,128]{3,2,1,0:T(8,128)}, f32[2,24,8,128]{3,2,1,0:T(8,128)S(1)}, u32[]{:S(2)}) copy-start(f32[2,24,8,128]{3,2,1,0:T(8,128)S(1)} %pad_maximum_fusion.1.refs_4_) | copy-start | bytes 589828
  77.9 17.7 %collective-permute-start.10 = (f32[2,24,8,128]{3,2,1,0:T(8,128)S(1)}, f32[2,24,8,128]{3,2,1,0:T(8,128)S(1)}, u32[]{:S(2)}, u32[]{:S(2)}) collective-permute-start(f32[2,24,8,128]{3,2,1,0:T(8,128)S(1)} %pad_maximum_fusion.1.refs_4_), channel_id=1, source_target_pairs={{0,192},{64,128},{128,64},{192,0},{1,193},{65,129},{129,65},{193,1... | collective-permute-start | bytes 589832 | tf_op jit(solution)/shard_map/ppermute | solution.py:19
  81.7 22.9 %copy-start.27 = (bf16[2,896,128]{2,1,0:T(8,128)(2,1)}, bf16[2,896,128]{2,1,0:T(8,128)(2,1)S(1)}, u32[]{:S(2)}) copy-start(bf16[2,896,128]{2,1,0:T(8,128)(2,1)S(1)} %collective-permute-done.15.refs_12_.refs_9_) | copy-start | bytes 1376260
  91.5 13.0 %collective-permute-start.5 = (f32[4,2,7,8,128]{4,3,2,1,0:T(8,128)S(1)}, f32[4,2,7,8,128]{4,3,2,1,0:T(8,128)S(1)}, u32[]{:S(2)}, u32[]{:S(2)}) collective-permute-start(f32[4,2,7,8,128]{4,3,2,1,0:T(8,128)S(1)} %all-to-all-done.2.refs_0_), channel_id=1, source_target_pairs={{0,48},{16,32},{32,16},{48,0},{1,49},{17,33},{33,17},{49,1},{2,50}... | collective-permute-start | bytes 688136 | tf_op jit(solution)/shard_map/ppermute | solution.py:19
  92.7 11.8 %collective-permute-start.4 = (f32[4,2,7,8,128]{4,3,2,1,0:T(8,128)S(1)}, f32[4,2,7,8,128]{4,3,2,1,0:T(8,128)S(1)}, u32[]{:S(2)}, u32[]{:S(2)}) collective-permute-start(f32[4,2,7,8,128]{4,3,2,1,0:T(8,128)S(1)} %all-to-all-done.2.refs_0_), channel_id=1, source_target_pairs={{0,32},{16,48},{32,0},{48,16},{1,33},{17,49},{33,1},{49,17},{2,34}... | collective-permute-start | bytes 688136 | tf_op jit(solution)/shard_map/ppermute | solution.py:19
  95.3 9.2 %collective-permute-start.3 = (f32[4,2,7,8,128]{4,3,2,1,0:T(8,128)S(1)}, f32[4,2,7,8,128]{4,3,2,1,0:T(8,128)S(1)}, u32[]{:S(2)}, u32[]{:S(2)}) collective-permute-start(f32[4,2,7,8,128]{4,3,2,1,0:T(8,128)S(1)} %all-to-all-done.2.refs_0_), channel_id=1, source_target_pairs={{0,16},{16,0},{32,48},{48,32},{1,17},{17,1},{33,49},{49,33},{2,18}... | collective-permute-start | bytes 688136 | tf_op jit(solution)/shard_map/ppermute | solution.py:19
  95.6 8.8 %collective-permute-start.9 = (f32[2,24,8,128]{3,2,1,0:T(8,128)S(1)}, f32[2,24,8,128]{3,2,1,0:T(8,128)S(1)}, u32[]{:S(2)}, u32[]{:S(2)}) collective-permute-start(f32[2,24,8,128]{3,2,1,0:T(8,128)S(1)} %pad_maximum_fusion.1.refs_4_), channel_id=1, source_target_pairs={{0,128},{64,192},{128,0},{192,64},{1,129},{65,193},{129,1},{193,65... | collective-permute-start | bytes 589832 | tf_op jit(solution)/shard_map/ppermute | solution.py:19
  95.6 8.9 %collective-permute-start.8 = (f32[2,24,8,128]{3,2,1,0:T(8,128)S(1)}, f32[2,24,8,128]{3,2,1,0:T(8,128)S(1)}, u32[]{:S(2)}, u32[]{:S(2)}) collective-permute-start(f32[2,24,8,128]{3,2,1,0:T(8,128)S(1)} %pad_maximum_fusion.1.refs_4_), channel_id=1, source_target_pairs={{0,64},{64,0},{128,192},{192,128},{1,65},{65,1},{129,193},{193,129... | collective-permute-start | bytes 589832 | tf_op jit(solution)/shard_map/ppermute | solution.py:19
  115.5 25.7 %all-to-all-start.3 = ((bf16[16,32,256]{2,1,0:T(8,128)(2,1)}), bf16[16,32,256]{2,1,0:T(8,128)(2,1)S(1)}, u32[]{:S(2)}, u32[]{:S(2)}) async-start(bf16[16,32,256]{2,1,0:T(8,128)(2,1)} %get-tuple-element.25.refs_0_), calls=%async_computation.3 | async-start | bytes 524288 | tf_op jit(solution)/shard_map/all_to_all | solution.py:331
  122.0 6.2 %collective-permute-start.19 = (f32[2,2,16,896]{3,2,1,0:T(8,128)}, f32[2,2,16,896]{3,2,1,0:T(8,128)S(1)}, u32[]{:S(2)}, u32[]{:S(2)}) collective-permute-start(f32[2,2,16,896]{3,2,1,0:T(8,128)} %get-tuple-element.21.refs_2_), channel_id=1, source_target_pairs={{0,1},{1,0},{2,3},{3,2},{4,5},{5,4},{6,7},{7,6},{8,9},{9,8},{10,11... | collective-permute-start | bytes 688136 | tf_op jit(solution)/shard_map/ppermute | solution.py:19
  122.6 9.3 %collective-permute-start.20 = (f32[2,2,16,896]{3,2,1,0:T(8,128)}, f32[2,2,16,896]{3,2,1,0:T(8,128)S(1)}, u32[]{:S(2)}, u32[]{:S(2)}) collective-permute-start(f32[2,2,16,896]{3,2,1,0:T(8,128)} %get-tuple-element.22.refs_3_), channel_id=1, source_target_pairs={{0,2},{1,3},{2,0},{3,1},{4,6},{5,7},{6,4},{7,5},{8,10},{9,11},{10,... | collective-permute-start | bytes 688136 | tf_op jit(solution)/shard_map/ppermute | solution.py:19
  125.2 9.1 %collective-permute-start.21 = (f32[2,2,16,896]{3,2,1,0:T(8,128)}, f32[2,2,16,896]{3,2,1,0:T(8,128)S(1)}, u32[]{:S(2)}, u32[]{:S(2)}) collective-permute-start(f32[2,2,16,896]{3,2,1,0:T(8,128)} %get-tuple-element.23.refs_4_), channel_id=1, source_target_pairs={{0,3},{1,2},{2,1},{3,0},{4,7},{5,6},{6,5},{7,4},{8,11},{9,10},{10,... | collective-permute-start | bytes 688136 | tf_op jit(solution)/shard_map/ppermute | solution.py:19
  137.0 14.6 %collective-permute-start.22 = (f32[4,16,896]{2,1,0:T(8,128)}, f32[4,16,896]{2,1,0:T(8,128)S(1)}, u32[]{:S(2)}, u32[]{:S(2)}) collective-permute-start(f32[4,16,896]{2,1,0:T(8,128)} %pick.1), channel_id=1, source_target_pairs={{0,4},{4,0},{1,5},{5,1},{2,6},{6,2},{3,7},{7,3},{8,12},{12,8},{9,1... | collective-permute-start | bytes 688136 | tf_op jit(solution)/shard_map/ppermute | solution.py:19
  141.2 26.1 %copy-start.1 = (bf16[16,32,256]{2,1,0:T(8,128)(2,1)}, bf16[16,32,256]{2,1,0:T(8,128)(2,1)S(1)}, u32[]{:S(2)}) copy-start(bf16[16,32,256]{2,1,0:T(8,128)(2,1)S(1)} %all-to-all-done.3.refs_6_) | copy-start | bytes 786436
  146.8 9.5 %collective-permute-start.31 = (f32[2,16,896]{2,1,0:T(8,128)}, f32[2,16,896]{2,1,0:T(8,128)S(1)}, u32[]{:S(2)}, u32[]{:S(2)}) collective-permute-start(f32[2,16,896]{2,1,0:T(8,128)} %get-tuple-element.27), channel_id=1, source_target_pairs={{0,1},{1,0},{2,3},{3,2},{4,5},{5,4},{6,7},{7,6},{8,9},{9,8},{10,11... | collective-permute-start | bytes 344072 | tf_op jit(solution)/shard_map/ppermute | solution.py:19
  146.8 11.1 %collective-permute-start.32 = (f32[2,16,896]{2,1,0:T(8,128)}, f32[2,16,896]{2,1,0:T(8,128)S(1)}, u32[]{:S(2)}, u32[]{:S(2)}) collective-permute-start(f32[2,16,896]{2,1,0:T(8,128)} %get-tuple-element.28), channel_id=1, source_target_pairs={{0,2},{1,3},{2,0},{3,1},{4,6},{5,7},{6,4},{7,5},{8,10},{9,11},{10,... | collective-permute-start | bytes 344072 | tf_op jit(solution)/shard_map/ppermute | solution.py:19
  149.9 8.1 %collective-permute-start.33 = (f32[2,16,896]{2,1,0:T(8,128)}, f32[2,16,896]{2,1,0:T(8,128)S(1)}, u32[]{:S(2)}, u32[]{:S(2)}) collective-permute-start(f32[2,16,896]{2,1,0:T(8,128)} %get-tuple-element.29), channel_id=1, source_target_pairs={{0,3},{1,2},{2,1},{3,0},{4,7},{5,6},{6,5},{7,4},{8,11},{9,10},{10,... | collective-permute-start | bytes 344072 | tf_op jit(solution)/shard_map/ppermute | solution.py:19
  151.5 39.1 %copy-start.17 = (f32[4,16,896]{2,1,0:T(8,128)}, f32[4,16,896]{2,1,0:T(8,128)S(1)}, u32[]{:S(2)}) copy-start(f32[4,16,896]{2,1,0:T(8,128)S(1)} %collective-permute-done.22.refs_4_) | copy-start | bytes 688132
  151.5 17.5 %collective-permute-start.23 = (f32[4,16,896]{2,1,0:T(8,128)S(1)}, f32[4,16,896]{2,1,0:T(8,128)S(1)}, u32[]{:S(2)}, u32[]{:S(2)}) collective-permute-start(f32[4,16,896]{2,1,0:T(8,128)S(1)} %collective-permute-done.22.refs_4_), channel_id=1, source_target_pairs={{0,8},{8,0},{1,9},{9,1},{2,10},{10,2},{3,11},{11,3},{4,12},{12,4},... | collective-permute-start | bytes 688136 | tf_op jit(solution)/shard_map/ppermute | solution.py:19
  151.5 15.8 %collective-permute-start.27 = (bf16[16,32,256]{2,1,0:T(8,128)(2,1)S(1)}, bf16[16,32,256]{2,1,0:T(8,128)(2,1)S(1)}, u32[]{:S(2)}, u32[]{:S(2)}) collective-permute-start(bf16[16,32,256]{2,1,0:T(8,128)(2,1)S(1)} %all-to-all-done.3.refs_6_), channel_id=1, source_target_pairs={{0,4},{4,0},{1,5},{5,1},{2,6},{6,2},{3,7},{7,3},{8,12},{12,8},{9,1... | collective-permute-start | bytes 786440 | tf_op jit(solution)/shard_map/ppermute | solution.py:19
  156.4 16.0 %collective-permute-start.26 = (bf16[16,32,256]{2,1,0:T(8,128)(2,1)S(1)}, bf16[16,32,256]{2,1,0:T(8,128)(2,1)S(1)}, u32[]{:S(2)}, u32[]{:S(2)}) collective-permute-start(bf16[16,32,256]{2,1,0:T(8,128)(2,1)S(1)} %all-to-all-done.3.refs_6_), channel_id=1, source_target_pairs={{0,3},{1,2},{2,1},{3,0},{4,7},{5,6},{6,5},{7,4},{8,11},{9,10},{10,... | collective-permute-start | bytes 786440 | tf_op jit(solution)/shard_map/ppermute | solution.py:19
  158.9 8.4 %collective-permute-start.34 = (f32[16,896]{1,0:T(8,128)S(1)}, f32[16,896]{1,0:T(8,128)S(1)}, u32[]{:S(2)}, u32[]{:S(2)}) collective-permute-start(f32[16,896]{1,0:T(8,128)S(1)} %slice_bitcast_fusion), channel_id=1, source_target_pairs={{0,4},{4,0},{1,5},{5,1},{2,6},{6,2},{3,7},{7,3},{8,12},{12,8},{9,1... | collective-permute-start | bytes 172040 | tf_op jit(solution)/shard_map/ppermute | solution.py:19
  160.4 30.2 %collective-permute-start.25 = (bf16[16,32,256]{2,1,0:T(8,128)(2,1)S(1)}, bf16[16,32,256]{2,1,0:T(8,128)(2,1)S(1)}, u32[]{:S(2)}, u32[]{:S(2)}) collective-permute-start(bf16[16,32,256]{2,1,0:T(8,128)(2,1)S(1)} %all-to-all-done.3.refs_6_), channel_id=1, source_target_pairs={{0,2},{1,3},{2,0},{3,1},{4,6},{5,7},{6,4},{7,5},{8,10},{9,11},{10,... | collective-permute-start | bytes 786440 | tf_op jit(solution)/shard_map/ppermute | solution.py:19
  167.3 23.3 %collective-permute-start.24 = (bf16[16,32,256]{2,1,0:T(8,128)(2,1)S(1)}, bf16[16,32,256]{2,1,0:T(8,128)(2,1)S(1)}, u32[]{:S(2)}, u32[]{:S(2)}) collective-permute-start(bf16[16,32,256]{2,1,0:T(8,128)(2,1)S(1)} %all-to-all-done.3.refs_6_), channel_id=1, source_target_pairs={{0,1},{1,0},{2,3},{3,2},{4,5},{5,4},{6,7},{7,6},{8,9},{9,8},{10,11... | collective-permute-start | bytes 786440 | tf_op jit(solution)/shard_map/ppermute | solution.py:19
  167.3 23.3 %copy-start.7 = (bf16[16,32,256]{2,1,0:T(8,128)(2,1)}, bf16[16,32,256]{2,1,0:T(8,128)(2,1)S(1)}, u32[]{:S(2)}) copy-start(bf16[16,32,256]{2,1,0:T(8,128)(2,1)S(1)} %collective-permute-done.27.refs_10_) | copy-start | bytes 786436
  167.3 23.3 %collective-permute-start.30 = (bf16[16,32,256]{2,1,0:T(8,128)(2,1)S(1)}, bf16[16,32,256]{2,1,0:T(8,128)(2,1)S(1)}, u32[]{:S(2)}, u32[]{:S(2)}) collective-permute-start(bf16[16,32,256]{2,1,0:T(8,128)(2,1)S(1)} %collective-permute-done.27.refs_10_), channel_id=1, source_target_pairs={{0,3},{1,2},{2,1},{3,0},{4,7},{5,6},{6,5},{7,4},{8,11},{9,10},{10,... | collective-permute-start | bytes 786440 | tf_op jit(solution)/shard_map/ppermute | solution.py:19
  169.1 21.5 %collective-permute-start.29 = (bf16[16,32,256]{2,1,0:T(8,128)(2,1)S(1)}, bf16[16,32,256]{2,1,0:T(8,128)(2,1)S(1)}, u32[]{:S(2)}, u32[]{:S(2)}) collective-permute-start(bf16[16,32,256]{2,1,0:T(8,128)(2,1)S(1)} %collective-permute-done.27.refs_10_), channel_id=1, source_target_pairs={{0,2},{1,3},{2,0},{3,1},{4,6},{5,7},{6,4},{7,5},{8,10},{9,11},{10,... | collective-permute-start | bytes 786440 | tf_op jit(solution)/shard_map/ppermute | solution.py:19
  172.3 18.3 %collective-permute-start.28 = (bf16[16,32,256]{2,1,0:T(8,128)(2,1)S(1)}, bf16[16,32,256]{2,1,0:T(8,128)(2,1)S(1)}, u32[]{:S(2)}, u32[]{:S(2)}) collective-permute-start(bf16[16,32,256]{2,1,0:T(8,128)(2,1)S(1)} %collective-permute-done.27.refs_10_), channel_id=1, source_target_pairs={{0,1},{1,0},{2,3},{3,2},{4,5},{5,4},{6,7},{7,6},{8,9},{9,8},{10,11... | collective-permute-start | bytes 786440 | tf_op jit(solution)/shard_map/ppermute | solution.py:19
  (25 other events, 144.6 us)

commit v3 on v0

v3 whole, which is shorter than its diff:
```python
import functools

import jax
import jax.numpy as jnp
from jax import lax
from jax.experimental import pallas as pl
from jax.experimental.pallas import tpu as pltpu
from jax.sharding import Mesh, PartitionSpec as P

SHAPE = (4, 4, 2, 2, 4)
AXES = ("zl", "x", "core", "zh", "y")
VAR = ("zl", "x", "core")
SIZE = dict(zip(AXES, SHAPE))
MIB = 1024 * 1024
F32, BF16 = jnp.float32, jnp.bfloat16


def swap(value, axis, mask=1):
    if mask == 0:
        return value
    return lax.ppermute(value, axis, [(i, i ^ mask) for i in range(SIZE[axis])])


def near4(value, axis):
    return [value] + [swap(value, axis, k) for k in (1, 2, 3)]


def after(value, other):
    return lax.optimization_barrier((value, other))[0]


def params(mib=56):
    return pltpu.CompilerParams(vmem_limit_bytes=mib * MIB)


SMEM = pl.BlockSpec(memory_space=pltpu.SMEM)
VMEM = pl.BlockSpec(memory_space=pltpu.VMEM)
HBM = pl.BlockSpec(memory_space=pl.ANY)


def part_kernel(x_ref, x_other_ref, gate_ref, up_ref, theirs_ref, width_ref, gains_ref, target_ref, out_ref, gain_ref):
    core = lax.axis_index("core")
    lanes = gate_ref.shape[1] // 128
    mine = jnp.where(core == 0, gate_ref[...], up_ref[...])
    x = jnp.concatenate([x_ref[...], x_other_ref[...]]).T
    part = jnp.dot(x, jnp.concatenate([mine, theirs_ref[...]]), preferred_element_type=F32)
    target = target_ref[...].astype(F32)
    width = gate_ref.shape[1]
    column = (lax.axis_index("zh") * 4 + lax.axis_index("y")) * width + lax.broadcasted_iota(jnp.int32, (1, width), 1)
    gain = jnp.where(column < width_ref[0], gains_ref[...], 0.0)
    gain_ref[...] = gain
    for slot in range(16):
        for e in range(2):
            for lane in range(lanes):
                at = slot * 16 + e * 8
                out_ref[slot, e * lanes + lane] = part[at : at + 8, lane * 128 : lane * 128 + 128]
        for half in range(2):
            at = ((slot // 4) % 2) * 256 + half * 128
            out_ref[slot, 2 * lanes + half] = target[:, at : at + 128]
        out_ref[slot, 2 * lanes + 2] = jnp.zeros((8, 128), F32)
        for lane in range(lanes):
            out_ref[slot, 2 * lanes + 2, lane : lane + 1, :] = gain[:, lane * 128 : lane * 128 + 128]


def part_call(x, x_other, gate, up, theirs, widths, gains, targets):
    lanes = gate.shape[1] // 128
    return pl.pallas_call(
        part_kernel,
        in_specs=[VMEM] * 5 + [SMEM] + [VMEM] * 2,
        out_specs=[VMEM] * 2,
        out_shape=[
            jax.ShapeDtypeStruct((16, 2 * lanes + 3, 8, 128), F32),
            jax.ShapeDtypeStruct(gains.shape, F32),
        ],
        compiler_params=params(),
        name="part",
    )(x, x_other, gate, up, theirs, widths, gains, targets)


def sum_kernel(part_ref, out_ref):
    lanes = out_ref.shape[1] - 6
    for y in range(4):
        for e in range(2):
            for lane in range(lanes):
                t = e * lanes + lane
                total = (part_ref[y, t] + part_ref[4 + y, t]) + (part_ref[8 + y, t] + part_ref[12 + y, t])
                out_ref[:, lane, y * 2 + e, :] = total
    x, y = lax.axis_index("x"), lax.axis_index("y")
    for high in range(2):
        for half in range(2):
            target = part_ref[y * 4 + high * 2 + x // 2, 2 * lanes + half]
            for slot in range(high, 8, 2):
                out_ref[slot, lanes + half] = target
    for k in range(4):
        gain = part_ref[x * 4 + k, 2 * lanes + 2]
        for slot in range(8):
            out_ref[slot, lanes + 2 + k] = gain


def sum_call(part):
    lanes = (part.shape[1] - 3) // 2
    return pl.pallas_call(
        sum_kernel,
        in_specs=[VMEM],
        out_specs=VMEM,
        out_shape=jax.ShapeDtypeStruct((8, lanes + 6, 8, 128), F32),
        compiler_params=params(),
        name="sum_x",
    )(part)


def raw_kernel(mine_ref, other_ref, out_ref, target_ref, gain_ref):
    first = lax.axis_index("core") == 0
    lanes = out_ref.shape[1]
    unit = lax.axis_index("core") * 4
    for lane in range(lanes):
        mine, other = (
            (r[unit, lane] + r[unit + 1, lane]) + (r[unit + 2, lane] + r[unit + 3, lane]) for r in (mine_ref, other_ref)
        )
        raw = jax.nn.silu(jnp.where(first, mine, other)) * jnp.where(first, other, mine)
        for copy in range(4):
            out_ref[copy, lane] = raw
    gain_ref[...] = mine_ref[:, lanes + 2 :]
    source, row = (lax.axis_index("zl") // 2) * 4, lax.axis_index("zh")
    for half in range(2):
        cols = slice(half * 128, half * 128 + 128)
        for x in range(4):
            own, far = mine_ref[source + x, lanes + half], other_ref[source + x, lanes + half]
            for e in range(2):
                target = jnp.where(first == (e == 0), own, far)
                target_ref[e, x * 4 : x * 4 + 4, cols] = jnp.where(row == 0, target[:4], target[4:])


def raw_call(mine, other):
    lanes = mine.shape[1] - 6
    return pl.pallas_call(
        raw_kernel,
        in_specs=[VMEM, VMEM],
        out_specs=[VMEM] * 3,
        out_shape=[
            jax.ShapeDtypeStruct((4, lanes, 8, 128), F32),
            jax.ShapeDtypeStruct((2, 16, 256), F32),
            jax.ShapeDtypeStruct((8, 4, 8, 128), F32),
        ],
        compiler_params=params(),
        name="raw",
    )(mine, other)


def extract_kernel(*refs):
    x, core, y, zh = (lax.axis_index(a) for a in ("x", "core", "y", "zh"))
    raw_refs, other_refs, out_refs, both = refs[:4], refs[4:8], refs[8:10], refs[10]
    for k in range(4):
        at = pl.ds((x ^ k) * 4, 4)
        both[core, at] = raw_refs[k][...]
        both[1 - core, at] = other_refs[k][...]
    for a in range(2):
        for k in range(4):
            for lane in range(both.shape[2]):
                out_refs[a][k, :, lane * 128 : lane * 128 + 128] = both[zh ^ a, :, lane, (y ^ k) * 2 + core, :]


def extract_call(raws, others):
    lanes = raws[0].shape[1]
    return pl.pallas_call(
        extract_kernel,
        in_specs=[VMEM] * 8,
        out_specs=[VMEM] * 2,
        out_shape=[jax.ShapeDtypeStruct((4, 16, lanes * 128), F32)] * 2,
        scratch_shapes=[pltpu.VMEM((2, 16, lanes, 8, 128), F32)],
        compiler_params=params(),
        name="extract",
    )(*raws, *others)


def output_kernel(*refs):
    raw_refs, other_refs, gain_refs, mine_refs, theirs_refs = refs[:4], refs[4:8], refs[8:12], refs[12:20], refs[20:28]
    target_ref, res_ref, row_refs = refs[28], refs[29], refs[30:34]
    raw_all, gain_all, down_all, hidden, total, raw_sem, gain_sem, mine_sem, theirs_sem = refs[34:]
    x, core, y, zh = (lax.axis_index(a) for a in ("x", "core", "y", "zh"))
    lanes = raw_all.shape[2]
    first, second = [], []
    for k in range(4):
        at = pl.ds((x ^ k) * 4, 4)
        first.append(pltpu.make_async_copy(raw_refs[k], raw_all.at[core, at], raw_sem.at[k]))
        first.append(pltpu.make_async_copy(other_refs[k], raw_all.at[1 - core, at], raw_sem.at[4 + k]))
        first.append(pltpu.make_async_copy(gain_refs[k], gain_all.at[x ^ k], gain_sem.at[k]))
    for p in range(8):
        second.append(pltpu.make_async_copy(mine_refs[p], down_all.at[core, p], mine_sem.at[p]))
        second.append(pltpu.make_async_copy(theirs_refs[p], down_all.at[1 - core, p], theirs_sem.at[p]))
    for copy in first + second:
        copy.start()
    for copy in first:
        copy.wait()
    for p in range(8):
        second[2 * p].wait()
        second[2 * p + 1].wait()
        a, k = p // 4, p % 4
        unit, other = zh ^ a, y ^ k
        for lane in range(lanes):
            cols = slice(lane * 128, lane * 128 + 128)
            for e in range(2):
                raw = raw_all[unit, :, lane, other * 2 + e, :]
                row_refs[k][a, e, :, cols] = raw
                for v in range(16):
                    gain = gain_all[v % 4, unit * 4 + v // 4, other, lane : lane + 1, :]
                    at = v * 32 + e * 16
                    hidden[at : at + 16, cols] = (raw * gain).astype(BF16)
        down = jnp.concatenate([down_all[0, p], down_all[1, p]], axis=1)
        term = jnp.dot(hidden[...], down, preferred_element_type=F32)
        if p == 0:
            total[...] = term
        else:
            total[...] += term
    for e in range(2):
        target = target_ref[e]
        for v in range(16):
            at = v * 32 + e * 16
            res = (total[at : at + 16, :] - target).astype(BF16)
            for copy in range(2):
                res_ref[copy * 16 + v, e * 16 : e * 16 + 16, :] = res


def output_call(raws, others, gains, mine, theirs, target):
    lanes = raws[0].shape[1]
    width = lanes * 128
    return pl.pallas_call(
        output_kernel,
        in_specs=[HBM] * 28 + [VMEM],
        out_specs=[VMEM] * 5,
        out_shape=[jax.ShapeDtypeStruct((32, 32, 256), BF16)]
        + [jax.ShapeDtypeStruct((2, 2, 16, width), F32)] * 4,
        scratch_shapes=[
            pltpu.VMEM((2, 16, lanes, 8, 128), F32),
            pltpu.VMEM((4,) + gains[0].shape, F32),
            pltpu.VMEM((2, 8) + mine[0].shape, BF16),
            pltpu.VMEM((512, width), BF16),
            pltpu.VMEM((512, 256), F32),
            pltpu.SemaphoreType.DMA((8,)),
            pltpu.SemaphoreType.DMA((4,)),
            pltpu.SemaphoreType.DMA((8,)),
            pltpu.SemaphoreType.DMA((8,)),
        ],
        compiler_params=params(),
        cost_estimate=pl.CostEstimate(flops=2 * 512 * 8 * width * 256, bytes_accessed=6 * MIB, transcendentals=0),
        name="output",
    )(*raws, *others, *gains, *mine, *theirs, target)


def back_kernel(*refs):
    res_ref, own_refs, mine_refs, theirs_refs, out_ref = refs[0], refs[1:5], refs[5:13], refs[13:21], refs[21]
    first = lax.axis_index("core") == 0
    for k in range(4):
        for a in range(2):
            mine, theirs = mine_refs[a * 4 + k][...], theirs_refs[a * 4 + k][...]
            down = jnp.concatenate([jnp.where(first, mine, theirs), jnp.where(first, theirs, mine)], axis=1)
            raw = jnp.concatenate([own_refs[k][a, 0], own_refs[k][a, 1]])
            for at in range(0, 16, 8):
                res = res_ref[at : at + 8].reshape(256, 256)
                back = lax.dot_general(res, down, (((1,), (1,)), ((), ())), preferred_element_type=F32)
                out_ref[at : at + 8, a * 4 + k, :] = jnp.sum(back.reshape(8, 32, -1) * raw[None], axis=1)


def back_call(res, owns, mine, theirs):
    width = owns[0].shape[3]
    return pl.pallas_call(
        back_kernel,
        in_specs=[VMEM] * 21,
        out_specs=VMEM,
        out_shape=jax.ShapeDtypeStruct((16, 8, width), F32),
        compiler_params=params(),
        cost_estimate=pl.CostEstimate(flops=2 * 512 * 8 * width * 256, bytes_accessed=6 * MIB, transcendentals=0),
        name="back",
    )(res, *owns, *mine, *theirs)


def total_kernel(part_ref, out_ref):
    y, zh = lax.axis_index("y"), lax.axis_index("zh")
    total = jnp.sum(part_ref[...], axis=0)
    for a in range(2):
        for k in range(4):
            p = a * 4 + k
            at = (zh ^ a) * 4 + (y ^ k)
            out_ref[at] = jnp.zeros((8, 128), F32)
            for lane in range(total.shape[1] // 128):
                out_ref[at, lane : lane + 1, :] = total[p : p + 1, lane * 128 : lane * 128 + 128]


def total_call(part):
    return pl.pallas_call(
        total_kernel,
        in_specs=[VMEM],
        out_specs=VMEM,
        out_shape=jax.ShapeDtypeStruct((8, 8, 128), F32),
        compiler_params=params(),
        name="total",
    )(part)


def pair_kernel(near_ref, far_ref, *out_refs):
    for k in range(4):
        out_refs[k][0] = near_ref[k]
        out_refs[k][1] = far_ref[k]


def pair_call(near, far):
    return pl.pallas_call(
        pair_kernel,
        in_specs=[VMEM] * 2,
        out_specs=[VMEM] * 4,
        out_shape=[jax.ShapeDtypeStruct((2,) + near.shape[1:], F32)] * 4,
        compiler_params=params(),
        name="pair",
    )(near, far)


def hidden_kernel(gain_ref, *refs):
    mine_refs, other_refs, out_ref, block = refs[:4], refs[4:8], refs[8], refs[9]
    core, zh = lax.axis_index("core"), lax.axis_index("zh")
    gain = gain_ref[...]
    for k in range(4):
        for z in range(2):
            for e in range(2):
                raw = jnp.where(core == e, mine_refs[k][zh ^ z], other_refs[k][zh ^ z])
                at = (k * 2 + z) * 32 + e * 16
                block[at : at + 16, :] = (raw * gain).astype(BF16)
    out_ref[...] = block[...].T


def hidden_call(gain, mine, others):
    width = gain.shape[1]
    return pl.pallas_call(
        hidden_kernel,
        in_specs=[VMEM] * 9,
        out_specs=VMEM,
        out_shape=jax.ShapeDtypeStruct((width, 256), BF16),
        scratch_shapes=[pltpu.VMEM((256, width), BF16)],
        compiler_params=params(),
        name="hidden",
    )(gain, *mine, *others)


def grad_kernel(scale, hidden_ref, *refs):
    res_refs, out_ref, res_all, sem = refs[:4], refs[4], refs[5], refs[6]
    step = pl.program_id(0)

    @pl.when(step == 0)
    def _():
        copies = [pltpu.make_async_copy(res_refs[k], res_all.at[k], sem.at[k]) for k in range(4)]
        for c in copies:
            c.start()
        for c in copies:
            c.wait()

    some = out_ref.shape[2] // 256
    block = jnp.concatenate(
        [
            jnp.concatenate([res_all[k, z * 16 + step * some + q] for k in range(4) for z in range(2)])
            for q in range(some)
        ],
        axis=1,
    )
    grad = jnp.dot(hidden_ref[...], block, preferred_element_type=F32)
    out_ref[0] = (grad * scale).astype(BF16)


def grad_call(hidden, res4, scale):
    width = hidden.shape[0]
    pieces, rows, feats = res4[0].shape
    blocks, some = pieces // 2, 2
    return pl.pallas_call(
        functools.partial(grad_kernel, scale),
        grid=(blocks // some,),
        in_specs=[pl.BlockSpec(hidden.shape, lambda s: (0, 0))] + [HBM] * 4,
        out_specs=pl.BlockSpec((1, width, some * feats), lambda s: (0, 0, s)),
        out_shape=jax.ShapeDtypeStruct((1, width, blocks * feats), BF16),
        scratch_shapes=[pltpu.VMEM((4, pieces, rows, feats), BF16), pltpu.SemaphoreType.DMA((4,))],
        compiler_params=params(),
        cost_estimate=pl.CostEstimate(
            flops=40 * 8 * rows * width * blocks * feats, bytes_accessed=10 * MIB, transcendentals=0
        ),
        name="grad",
    )(hidden, *res4)


def local(inputs, gate, up, down, targets, widths, gains):
    me = {a: lax.axis_index(a) for a in AXES}
    first = me["core"] == 0
    rows = inputs.shape[1]
    width = gate.shape[1]
    scale = 1.0 / rows**0.5

    theirs = swap(jnp.where(first, up, gate), "core")
    inputs_other = swap(inputs, "core")
    part, gain = part_call(inputs, inputs_other, gate, up, theirs, widths, gains, targets)
    down = after(down, part)
    part = lax.all_to_all(part, ("x", "y"), 0, 0, tiled=True)
    far = swap(down, "zh")
    part = sum_call(after(part, far))
    down, far = after((down, far), part)
    part = lax.all_to_all(part, ("zh", "zl"), 0, 0, tiled=True)
    mine = near4(down, "y")
    part = after(part, mine)
    raw, target, gain_z = raw_call(part, swap(part, "core"))
    mine = after(mine, raw)
    raw = lax.all_to_all(raw, "zl", 0, 0, tiled=True)
    theirs = [swap(d, "core") for d in mine]
    raw = after(raw, theirs)
    raws = near4(raw, "x")
    others = [swap(r, "core") for r in raws]
    far, gain_z = after((far, gain_z), raw)
    mine_far = near4(far, "y")
    theirs_far = [swap(d, "core") for d in mine_far]
    all_gains = near4(gain_z, "x")
    mine, theirs = mine + mine_far, theirs + theirs_far

    near, far = extract_call(raws, others)
    far = swap(far, "zh")
    raws, others = after((raws, others), near)

    res, *rows8 = output_call(raws, others, all_gains, mine, theirs, target)
    res_own = lax.all_to_all(after(res, far), ("zh", "zl", "x"), 0, 0, tiled=True)
    owns = pair_call(*after((near, far), res))
    got = [owns[0]] + [swap(owns[k], "y", k) for k in (1, 2, 3)]
    sums = back_call(after(res, owns), rows8, mine, theirs)
    res_own = after(res_own, (sums, got))
    res4 = near4(res_own, "y")
    sums, got = after((sums, got), res_own)
    sums = lax.all_to_all(sums, ("zl", "x"), 0, 0, tiled=True)
    hidden = hidden_call(gain, got, [swap(g, "core") for g in got])
    sums = lax.all_to_all(total_call(sums), ("zh", "y"), 0, 0, tiled=True)
    grad_down = grad_call(hidden, res4, scale)
    sums = jnp.sum(after(sums, grad_down), axis=0)[: width // 128].reshape(1, width)
    column = (me["zh"] * 4 + me["y"]) * width + lax.broadcasted_iota(jnp.int32, (1, width), 1)
    kept = (column < widths[0]).astype(F32)
    return grad_down, kept * sums * scale


def solution(mesh):
    fine = Mesh(mesh.devices.reshape(SHAPE), AXES)
    tp = ("zh", "y")
    return jax.shard_map(
        local,
        mesh=fine,
        in_specs=(P(VAR, None), P(VAR, tp), P(VAR, tp), P(tp, VAR), P(VAR, tp), P(VAR), P(VAR, tp)),
        out_specs=(P(VAR, tp, None), P(VAR, tp)),
        check_vma=False,
    )
```

time: 590 us -> 184 us (0.31)
  waiting for transfers between devices: 496 us -> 46.6 us
  starting transfers between devices: 0.23 us -> 78.8 us
  Pallas kernels: 0 us -> 37.8 us
  blocking collectives: 43.6 us -> 9.53 us
  matrix products: 32.8 us -> 0 us
  between operations: 14.8 us -> 1.75 us
  local copies, waits for them, and re-layouts: 0.01 us -> 6.47 us
    all_gather x5 -> x0, waiting for transfers between devices: 297 us -> none  [the longest x1 77.7 us: local(): down_whole = lax.all_gather(down_parent, 'var', axis=1, tiled=True)]
    psum x1 -> x0, waiting for transfers between devices: 197 us -> none  [local(): output = lax.psum(partial_value, 'tp')]
    ppermute x0 -> x39, starting transfers between devices: none -> 43.8 us  [swap(): return lax.ppermute(value, axis, [(i, i ^ mask) for i in range(SIZE[axis])])]
    all_gather x1 -> x0, blocking collectives: 43.6 us -> none  [local(): target_part = lax.all_gather(targets, 'var', axis=0, tiled=True)]
    pallas_call x0 -> x10, Pallas kernels: none -> 37.8 us  [the longest x1 9.02 us: output_call(): pl.pallas_call(output_kernel, in_specs=[HBM] * 28 + [VMEM], out_specs=[VM...]
    ppermute x0 -> x39, waiting for transfers between devices: none -> 35.9 us  [swap(): return lax.ppermute(value, axis, [(i, i ^ mask) for i in range(SIZE[axis])])]
    all_to_all x0 -> x5, starting transfers between devices: none -> 34.9 us  [the longest x1 8.47 us: local(): part = lax.all_to_all(part, ('zh', 'zl'), 0, 0, tiled=True)]
    dot_general x5 -> x0, matrix products: 32.8 us -> none  [the longest x1 7.45 us: local(): lax.dot_general(residual, down_whole, (((1,), (1,)), ((), ())), preferred...]
  transfers between devices with their start and end apart: 6 -> 44, of which waited for: 6 -> 21; matrix products, arithmetic and copies ran while one was open for 4% -> 0% of each run, Pallas kernels for 0% -> 17%
where the time goes in v3:
time: 184 us; the launch traced here: 183 us
  starting transfers between devices  78.8 us (43%)
  waiting for transfers between devices  46.6 us (25%)
  Pallas kernels  37.8 us (21%)
  blocking collectives  9.53 us (5%)
  local copies, waits for them, and re-layouts  6.47 us (4%)
    ppermute x39, starting transfers between devices, swap(): return lax.ppermute(value, axis, [(i, i ^ mask) for i in range(SIZE[axis])])  43.8 us
    ppermute x39, waiting for transfers between devices, swap(): return lax.ppermute(value, axis, [(i, i ^ mask) for i in range(SIZE[axis])])  35.9 us
    all_to_all x1, blocking collectives, local(): raw = lax.all_to_all(raw, 'zl', 0, 0, tiled=True)  9.53 us
    pallas_call x1, Pallas kernels, output_call(): pl.pallas_call(output_kernel, in_specs=[HBM] * 28 + [VMEM], out_specs=[VM...  9.02 us
    all_to_all x1, starting transfers between devices, local(): part = lax.all_to_all(part, ('zh', 'zl'), 0, 0, tiled=True)  8.47 us
    pallas_call x1, Pallas kernels, grad_call(): pl.pallas_call(functools.partial(grad_kernel, scale), grid=(blocks // som...  8.27 us
    all_to_all x1, starting transfers between devices, local(): lax.all_to_all(after(res, far), ('zh', 'zl', 'x'), 0, 0, tiled=True)  7.89 us
    all_to_all x1, starting transfers between devices, local(): part = lax.all_to_all(part, ('x', 'y'), 0, 0, tiled=True)  7.61 us
  transfers between devices with their start and end apart: 44, of which 21 were waited for; matrix products, arithmetic and copies ran while one was open for 0% of the time, Pallas kernels for 17%

profile of v3, /device:TPU:2, one launch (start us, length us, event | category | flops | bytes accessed | tf_op | source)
XLA Modules:
  0.0 182.5 jit_solution(2580614677656721953)
XLA Ops:
  0.6 1.0 broadcast_select_fusion
  4.8 2.6 %part.1 = (f32[16,17,8,128]{3,2,1,0:T(8,128)}, f32[1,896]{1,0:T(1,128)}) custom-call(bf16[128,256]{1,0:T(8,128)(2,1)} %x_ref.1, bf16[128,256]{1,0:T(8,128)(2,1)} %copy-done.23, bf16[128,896]{1,0:T(8,128)(2,1)} %gate_ref.1, bf16[128,896]{1,0:T(8,128)(2,1)} %up_ref.1, bf16[128,896]{1,0:T(8,128)(2,1)} %copy-done.7, s32[1]{0:T(128)} %copy.11.width_ref, ...), custom_call_target="tpu_custom_call" | custom-call | tf_op jit(solution)/shard_map/part/pallas_call | solution.py:67
  7.4 7.6 %all-to-all-start = ((f32[16,17,8,128]{3,2,1,0:T(8,128)}), f32[16,17,8,128]{3,2,1,0:T(8,128)S(1)}, u32[]{:S(2)}, u32[]{:S(2)}) async-start(f32[16,17,8,128]{3,2,1,0:T(8,128)} %get-tuple-element.50), calls=%async_computation | async-start | bytes 2228224 | tf_op jit(solution)/shard_map/all_to_all | solution.py:397
  15.0 7.3 %collective-permute-start.2 = (bf16[896,128]{1,0:T(8,128)(2,1)S(1)}, bf16[896,128]{1,0:T(8,128)(2,1)S(1)}, u32[]{:S(2)}, u32[]{:S(2)}) collective-permute-start(bf16[896,128]{1,0:T(8,128)(2,1)S(1)} %copy-done.27), channel_id=1, source_target_pairs={{0,4},{4,0},{1,5},{5,1},{2,6},{6,2},{3,7},{7,3},{8,12},{12,8},{9,1... | collective-permute-start | bytes 688136 | tf_op jit(solution)/shard_map/ppermute | solution.py:21
  22.3 6.5 %collective-permute-done.2.refs_16_.refs_9_ = bf16[896,128]{1,0:T(8,128)(2,1)S(1)} collective-permute-done((bf16[896,128]{1,0:T(8,128)(2,1)S(1)}, bf16[896,128]{1,0:T(8,128)(2,1)S(1)}, u32[]{:S(2)}, u32[]{:S(2)}) %collective-permute-start.2) | collective-permute-done | bytes 229408 | tf_op jit(solution)/shard_map/ppermute | solution.py:21
  28.8 2.3 %all-to-all-done.part_ref = f32[16,17,8,128]{3,2,1,0:T(8,128)S(1)} async-done(((f32[16,17,8,128]{3,2,1,0:T(8,128)}), f32[16,17,8,128]{3,2,1,0:T(8,128)S(1)}, u32[]{:S(2)}, u32[]{:S(2)}) %all-to-all-start) | async-done | bytes 1114144 | tf_op jit(solution)/shard_map/all_to_all | solution.py:397
  31.1 1.0 copy-done
  32.1 2.2 %sum_x.1 = f32[8,13,8,128]{3,2,1,0:T(8,128)} custom-call(f32[16,17,8,128]{3,2,1,0:T(8,128)} %copy-done), custom_call_target="tpu_custom_call" | custom-call | tf_op jit(solution)/shard_map/sum_x/pallas_call | solution.py:102
  34.3 8.5 %all-to-all-start.1 = ((f32[8,13,8,128]{3,2,1,0:T(8,128)}), f32[8,13,8,128]{3,2,1,0:T(8,128)S(1)}, u32[]{:S(2)}, u32[]{:S(2)}) async-start(f32[8,13,8,128]{3,2,1,0:T(8,128)} %sum_x.1), calls=%async_computation.1 | async-start | bytes 851968 | tf_op jit(solution)/shard_map/all_to_all | solution.py:401
  42.8 2.2 %collective-permute-start.5 = (bf16[896,128]{1,0:T(8,128)(2,1)S(1)}, bf16[896,128]{1,0:T(8,128)(2,1)S(1)}, u32[]{:S(2)}, u32[]{:S(2)}) collective-permute-start(bf16[896,128]{1,0:T(8,128)(2,1)S(1)} %copy-done.27), channel_id=1, source_target_pairs={{0,3},{1,2},{2,1},{3,0},{4,7},{5,6},{6,5},{7,4},{8,11},{9,10},{10,... | collective-permute-start | bytes 688136 | tf_op jit(solution)/shard_map/ppermute | solution.py:21
  44.9 0.9 collective-permute-start.4
  45.8 1.1 collective-permute-start.3
  46.9 7.7 %collective-permute-done.5.refs_15_.refs_8_ = bf16[896,128]{1,0:T(8,128)(2,1)S(1)} collective-permute-done((bf16[896,128]{1,0:T(8,128)(2,1)S(1)}, bf16[896,128]{1,0:T(8,128)(2,1)S(1)}, u32[]{:S(2)}, u32[]{:S(2)}) %collective-permute-start.5) | collective-permute-done | bytes 229408 | tf_op jit(solution)/shard_map/ppermute | solution.py:21
  55.2 1.6 all-to-all-done.1.mine_ref
  56.8 1.8 collective-permute-done.6.other_ref
  59.3 1.9 %raw.1 = (f32[4,7,8,128]{3,2,1,0:T(8,128)}, f32[2,16,256]{2,1,0:T(8,128)}, f32[8,4,8,128]{3,2,1,0:T(8,128)}) custom-call(f32[8,13,8,128]{3,2,1,0:T(8,128)} %copy-done.2, f32[8,13,8,128]{3,2,1,0:T(8,128)} %copy-done.5), custom_call_target="tpu_custom_call" | custom-call | tf_op jit(solution)/shard_map/raw/pallas_call | solution.py:136
  62.2 9.5 %all_to_all.30.refs_0_ = f32[4,7,8,128]{3,2,1,0:T(8,128)S(1)} all-to-all(f32[4,7,8,128]{3,2,1,0:T(8,128)} %get-tuple-element.55), channel_id=1, replica_groups=mesh['zl'=4,'x'=4,'core'=2,'zh'=2,'y'=4] {'zl'}, dimensions={0} | all-to-all | bytes 229376 | tf_op jit(solution)/shard_map/all_to_all | solution.py:406
  71.9 1.4 collective-permute-start.13
  73.3 2.6 %collective-permute-start.12 = (f32[4,7,8,128]{3,2,1,0:T(8,128)S(1)}, f32[4,7,8,128]{3,2,1,0:T(8,128)S(1)}, u32[]{:S(2)}, u32[]{:S(2)}) collective-permute-start(f32[4,7,8,128]{3,2,1,0:T(8,128)S(1)} %all_to_all.30.refs_0_), channel_id=1, source_target_pairs={{0,32},{16,48},{32,0},{48,16},{1,33},{17,49},{33,1},{49,17},{2,34}... | collective-permute-start | bytes 344072 | tf_op jit(solution)/shard_map/ppermute | solution.py:21
  76.1 1.3 collective-permute-start.20
  77.4 2.6 %collective-permute-start.19 = (f32[8,4,8,128]{3,2,1,0:T(8,128)}, f32[8,4,8,128]{3,2,1,0:T(8,128)S(1)}, u32[]{:S(2)}, u32[]{:S(2)}) collective-permute-start(f32[8,4,8,128]{3,2,1,0:T(8,128)} %get-tuple-element.72.refs_8_), channel_id=1, source_target_pairs={{0,32},{16,48},{32,0},{48,16},{1,33},{17,49},{33,1},{49,17},{2,34}... | collective-permute-start | bytes 393224 | tf_op jit(solution)/shard_map/ppermute | solution.py:21
  80.0 1.4 collective-permute-start.23
  81.4 2.1 %collective-permute-start.22 = (bf16[896,128]{1,0:T(8,128)(2,1)S(1)}, bf16[896,128]{1,0:T(8,128)(2,1)S(1)}, u32[]{:S(2)}, u32[]{:S(2)}) collective-permute-start(bf16[896,128]{1,0:T(8,128)(2,1)S(1)} %collective-permute-done.2.refs_16_.refs_9_), channel_id=1, source_target_pairs={{0,2},{1,3},{2,0},{3,1},{4,6},{5,7},{6,4},{7,5},{8,10},{9,11},{10,... | collective-permute-start | bytes 688136 | tf_op jit(solution)/shard_map/ppermute | solution.py:21
  84.1 1.5 collective-permute-done.20.refs_11_
  87.4 5.2 %collective-permute-done.23.refs_19_.refs_12_ = bf16[896,128]{1,0:T(8,128)(2,1)S(1)} collective-permute-done((bf16[896,128]{1,0:T(8,128)(2,1)S(1)}, bf16[896,128]{1,0:T(8,128)(2,1)S(1)}, u32[]{:S(2)}, u32[]{:S(2)}) %collective-permute-start.23) | collective-permute-done | bytes 229408 | tf_op jit(solution)/shard_map/ppermute | solution.py:21
  93.3 3.1 %collective-permute-start.18 = (f32[8,4,8,128]{3,2,1,0:T(8,128)}, f32[8,4,8,128]{3,2,1,0:T(8,128)S(1)}, u32[]{:S(2)}, u32[]{:S(2)}) collective-permute-start(f32[8,4,8,128]{3,2,1,0:T(8,128)} %get-tuple-element.72.refs_8_), channel_id=1, source_target_pairs={{0,16},{16,0},{32,48},{48,32},{1,17},{17,1},{33,49},{49,33},{2,18}... | collective-permute-start | bytes 393224 | tf_op jit(solution)/shard_map/ppermute | solution.py:21
  96.5 2.3 %extract.1 = (f32[4,16,896]{2,1,0:T(8,128)}, f32[4,16,896]{2,1,0:T(8,128)}) custom-call(f32[4,7,8,128]{3,2,1,0:T(8,128)} %copy-done.4, f32[4,7,8,128]{3,2,1,0:T(8,128)} %copy-done.19, f32[4,7,8,128]{3,2,1,0:T(8,128)} %copy-done.18, f32[4,7,8,128]{3,2,1,0:T(8,128)} %copy-done.17, f32[4,7,8,128]{3,2,1,0:T(8,128)} %copy-done.16, f32[4,7,8,128]{3,2,1,0:T(8,128)} %copy-done.22, ...), custom_call_target="tpu_custom_call" | custom-call | tf_op jit(solution)/shard_map/extract/pallas_call | solution.py:165
  98.8 1.9 %collective-permute-done.18.refs_9_ = f32[8,4,8,128]{3,2,1,0:T(8,128)S(1)} collective-permute-done((f32[8,4,8,128]{3,2,1,0:T(8,128)}, f32[8,4,8,128]{3,2,1,0:T(8,128)S(1)}, u32[]{:S(2)}, u32[]{:S(2)}) %collective-permute-start.18) | collective-permute-done | bytes 131104 | tf_op jit(solution)/shard_map/ppermute | solution.py:21
  100.7 4.2 %collective-permute-start.28 = (f32[4,16,896]{2,1,0:T(8,128)}, f32[4,16,896]{2,1,0:T(8,128)S(1)}, u32[]{:S(2)}, u32[]{:S(2)}) collective-permute-start(f32[4,16,896]{2,1,0:T(8,128)} %get-tuple-element.76), channel_id=1, source_target_pairs={{0,4},{4,0},{1,5},{5,1},{2,6},{6,2},{3,7},{7,3},{8,12},{12,8},{9,1... | collective-permute-start | bytes 688136 | tf_op jit(solution)/shard_map/ppermute | solution.py:21
  105.8 9.0 %output.1 = (bf16[32,32,256]{2,1,0:T(8,128)(2,1)}, f32[2,2,16,896]{3,2,1,0:T(8,128)}, f32[2,2,16,896]{3,2,1,0:T(8,128)}, f32[2,2,16,896]{3,2,1,0:T(8,128)}, f32[2,2,16,896]{3,2,1,0:T(8,128)}) custom-call(f32[4,7,8,128]{3,2,1,0:T(8,128)} %copy-done.4, f32[4,7,8,128]{3,2,1,0:T(8,128)} %copy-done.19, f32[4,7,8,128]{3,2,1,0:T(8,128)} %copy-done.18, ...), custom_call_target="tpu_custom_call" | custom-call | flops 1879048192 | bytes 6291456 | tf_op jit(solution)/shard_map/output/pallas_call | solution.py:227
  114.8 2.3 %collective-permute-done.28.far_ref = f32[4,16,896]{2,1,0:T(8,128)S(1)} collective-permute-done((f32[4,16,896]{2,1,0:T(8,128)}, f32[4,16,896]{2,1,0:T(8,128)S(1)}, u32[]{:S(2)}, u32[]{:S(2)}) %collective-permute-start.28) | collective-permute-done | bytes 229408 | tf_op jit(solution)/shard_map/ppermute | solution.py:21
  117.1 7.9 %all-to-all-start.3 = ((bf16[32,32,256]{2,1,0:T(8,128)(2,1)}), bf16[32,32,256]{2,1,0:T(8,128)(2,1)S(1)}, u32[]{:S(2)}, u32[]{:S(2)}) async-start(bf16[32,32,256]{2,1,0:T(8,128)(2,1)} %get-tuple-element.88.refs_0_), calls=%async_computation.3 | async-start | bytes 1048576 | tf_op jit(solution)/shard_map/all_to_all | solution.py:422
  125.0 1.9 %pair.1 = (f32[2,16,896]{2,1,0:T(8,128)}, f32[2,16,896]{2,1,0:T(8,128)}, f32[2,16,896]{2,1,0:T(8,128)}, f32[2,16,896]{2,1,0:T(8,128)}) custom-call(f32[4,16,896]{2,1,0:T(8,128)} %get-tuple-element.77.near_ref, f32[4,16,896]{2,1,0:T(8,128)} %copy-done.6), custom_call_target="tpu_custom_call" | custom-call | tf_op jit(solution)/shard_map/pair/pallas_call | solution.py:307
  126.9 1.0 collective-permute-start.29
  127.9 2.8 %collective-permute-start.30 = (f32[2,16,896]{2,1,0:T(8,128)}, f32[2,16,896]{2,1,0:T(8,128)S(1)}, u32[]{:S(2)}, u32[]{:S(2)}) collective-permute-start(f32[2,16,896]{2,1,0:T(8,128)} %get-tuple-element.81), channel_id=1, source_target_pairs={{0,2},{1,3},{2,0},{3,1},{4,6},{5,7},{6,4},{7,5},{8,10},{9,11},{10,... | collective-permute-start | bytes 344072 | tf_op jit(solution)/shard_map/ppermute | solution.py:21
  130.7 0.9 collective-permute-start.31
  131.6 5.9 %back.1 = f32[16,8,896]{2,1,0:T(8,128)} custom-call(bf16[32,32,256]{2,1,0:T(8,128)(2,1)} %get-tuple-element.88.refs_0_, f32[2,2,16,896]{3,2,1,0:T(8,128)} %get-tuple-element.84.refs_1_, f32[2,2,16,896]{3,2,1,0:T(8,128)} %get-tuple-element.85.refs_2_, f32[2,2,16,896]{3,2,1,0:T(8,128)} %get-tuple-element.86.refs_3_, ...), custom_call_target="tpu_custom_call" | custom-call | flops 1879048192 | bytes 6291456 | tf_op jit(solution)/shard_map/back/pallas_call | solution.py:266
  137.6 4.4 %all-to-all-done.3.refs_0_ = bf16[32,32,256]{2,1,0:T(8,128)(2,1)S(1)} async-done(((bf16[32,32,256]{2,1,0:T(8,128)(2,1)}), bf16[32,32,256]{2,1,0:T(8,128)(2,1)S(1)}, u32[]{:S(2)}, u32[]{:S(2)}) %all-to-all-start.3) | async-done | bytes 524320 | tf_op jit(solution)/shard_map/all_to_all | solution.py:422
  142.0 4.8 %all-to-all-start.4 = ((f32[16,8,896]{2,1,0:T(8,128)}), f32[16,8,896]{2,1,0:T(8,128)S(1)}, u32[]{:S(2)}, u32[]{:S(2)}) async-start(f32[16,8,896]{2,1,0:T(8,128)} %back.1), calls=%async_computation.4 | async-start | bytes 917504 | tf_op jit(solution)/shard_map/all_to_all | solution.py:429
  146.9 2.4 %collective-permute-start.38 = (bf16[32,32,256]{2,1,0:T(8,128)(2,1)S(1)}, bf16[32,32,256]{2,1,0:T(8,128)(2,1)S(1)}, u32[]{:S(2)}, u32[]{:S(2)}) collective-permute-start(bf16[32,32,256]{2,1,0:T(8,128)(2,1)S(1)} %all-to-all-done.3.refs_0_), channel_id=1, source_target_pairs={{0,3},{1,2},{2,1},{3,0},{4,7},{5,6},{6,5},{7,4},{8,11},{9,10},{10,... | collective-permute-start | bytes 1572872 | tf_op jit(solution)/shard_map/ppermute | solution.py:21
  149.9 1.0 collective-permute-start.36
  151.5 0.8 collective-permute-done.32.refs_4_
  154.4 2.2 %hidden.1.hidden_ref = bf16[896,256]{1,0:T(8,128)(2,1)} custom-call(f32[1,896]{1,0:T(1,128)} %get-tuple-element.49.gain_ref, f32[2,16,896]{2,1,0:T(8,128)} %get-tuple-element.90.refs_0_, f32[2,16,896]{2,1,0:T(8,128)} %copy-done.9, f32[2,16,896]{2,1,0:T(8,128)} %copy-done.10, f32[2,16,896]{2,1,0:T(8,128)} %copy-done.11, f32[2,16,896]{2,1,0:T(8,128)} %copy-done.12, ...), custom_call_target="tpu_custom_call" | custom-call | tf_op jit(solution)/shard_map/hidden/pallas_call | solution.py:332
  156.6 2.4 %all-to-all-done.4.part_ref = f32[16,8,896]{2,1,0:T(8,128)S(1)} async-done(((f32[16,8,896]{2,1,0:T(8,128)}), f32[16,8,896]{2,1,0:T(8,128)S(1)}, u32[]{:S(2)}, u32[]{:S(2)}) %all-to-all-start.4) | async-done | bytes 458784 | tf_op jit(solution)/shard_map/all_to_all | solution.py:429
  159.8 1.7 total.1
  161.5 6.1 %all-to-all-start.5 = ((f32[8,8,128]{2,1,0:T(8,128)}), f32[8,8,128]{2,1,0:T(8,128)S(1)}, u32[]{:S(2)}, u32[]{:S(2)}) async-start(f32[8,8,128]{2,1,0:T(8,128)} %total.1), calls=%async_computation.5 | async-start | bytes 65536 | tf_op jit(solution)/shard_map/all_to_all | solution.py:431
  167.6 4.2 %collective-permute-done.38.refs_3_ = bf16[32,32,256]{2,1,0:T(8,128)(2,1)S(1)} collective-permute-done((bf16[32,32,256]{2,1,0:T(8,128)(2,1)S(1)}, bf16[32,32,256]{2,1,0:T(8,128)(2,1)S(1)}, u32[]{:S(2)}, u32[]{:S(2)}) %collective-permute-start.38) | collective-permute-done | bytes 524320 | tf_op jit(solution)/shard_map/ppermute | solution.py:21
  173.6 8.3 %grad.1 = bf16[1,896,4096]{2,1,0:T(8,128)(2,1)} custom-call(bf16[896,256]{1,0:T(8,128)(2,1)} %hidden.1.hidden_ref, bf16[32,32,256]{2,1,0:T(8,128)(2,1)} %copy-done.3, bf16[32,32,256]{2,1,0:T(8,128)(2,1)} %copy-done.26, bf16[32,32,256]{2,1,0:T(8,128)(2,1)} %copy-done.25, bf16[32,32,256]{2,1,0:T(8,128)(2,1)} %copy-done.24), custom_call_target="tpu_custom_call" | custom-call | flops 37580963840 | bytes 10485760 | tf_op jit(solution)/shard_map/grad/pallas_call | solution.py:371
  (147 shorter events, 15.7 us)
Async XLA Ops:
  1.6 1.9 %collective-permute-start.1 = (bf16[128,896]{1,0:T(8,128)(2,1)S(1)}, bf16[128,896]{1,0:T(8,128)(2,1)S(1)}, u32[]{:S(2)}, u32[]{:S(2)}) collective-permute-start(bf16[128,896]{1,0:T(8,128)(2,1)S(1)} %broadcast_select_fusion), channel_id=1, source_target_pairs={{0,8},{8,0},{1,9},{9,1},{2,10},{10,2},{3,11},{11,3},{4,12},{12,4},... | collective-permute-start | bytes 688136 | tf_op jit(solution)/shard_map/ppermute | solution.py:21
  1.7 1.8 collective-permute-start
  7.4 23.8 %all-to-all-start = ((f32[16,17,8,128]{3,2,1,0:T(8,128)}), f32[16,17,8,128]{3,2,1,0:T(8,128)S(1)}, u32[]{:S(2)}, u32[]{:S(2)}) async-start(f32[16,17,8,128]{3,2,1,0:T(8,128)} %get-tuple-element.50), calls=%async_computation | async-start | bytes 2228224 | tf_op jit(solution)/shard_map/all_to_all | solution.py:397
  15.0 13.8 %collective-permute-start.2 = (bf16[896,128]{1,0:T(8,128)(2,1)S(1)}, bf16[896,128]{1,0:T(8,128)(2,1)S(1)}, u32[]{:S(2)}, u32[]{:S(2)}) collective-permute-start(bf16[896,128]{1,0:T(8,128)(2,1)S(1)} %copy-done.27), channel_id=1, source_target_pairs={{0,4},{4,0},{1,5},{5,1},{2,6},{6,2},{3,7},{7,3},{8,12},{12,8},{9,1... | collective-permute-start | bytes 688136 | tf_op jit(solution)/shard_map/ppermute | solution.py:21
  28.8 76.1 %copy-start.28 = (bf16[896,128]{1,0:T(8,128)(2,1)}, bf16[896,128]{1,0:T(8,128)(2,1)S(1)}, u32[]{:S(2)}) copy-start(bf16[896,128]{1,0:T(8,128)(2,1)S(1)} %collective-permute-done.2.refs_16_.refs_9_) | copy-start | bytes 688132
  34.3 22.5 %all-to-all-start.1 = ((f32[8,13,8,128]{3,2,1,0:T(8,128)}), f32[8,13,8,128]{3,2,1,0:T(8,128)S(1)}, u32[]{:S(2)}, u32[]{:S(2)}) async-start(f32[8,13,8,128]{3,2,1,0:T(8,128)} %sum_x.1), calls=%async_computation.1 | async-start | bytes 851968 | tf_op jit(solution)/shard_map/all_to_all | solution.py:401
  42.8 11.8 %collective-permute-start.5 = (bf16[896,128]{1,0:T(8,128)(2,1)S(1)}, bf16[896,128]{1,0:T(8,128)(2,1)S(1)}, u32[]{:S(2)}, u32[]{:S(2)}) collective-permute-start(bf16[896,128]{1,0:T(8,128)(2,1)S(1)} %copy-done.27), channel_id=1, source_target_pairs={{0,3},{1,2},{2,1},{3,0},{4,7},{5,6},{6,5},{7,4},{8,11},{9,10},{10,... | collective-permute-start | bytes 688136 | tf_op jit(solution)/shard_map/ppermute | solution.py:21
  44.9 9.7 %collective-permute-start.4 = (bf16[896,128]{1,0:T(8,128)(2,1)S(1)}, bf16[896,128]{1,0:T(8,128)(2,1)S(1)}, u32[]{:S(2)}, u32[]{:S(2)}) collective-permute-start(bf16[896,128]{1,0:T(8,128)(2,1)S(1)} %copy-done.27), channel_id=1, source_target_pairs={{0,2},{1,3},{2,0},{3,1},{4,6},{5,7},{6,4},{7,5},{8,10},{9,11},{10,... | collective-permute-start | bytes 688136 | tf_op jit(solution)/shard_map/ppermute | solution.py:21
  45.8 9.4 %collective-permute-start.3 = (bf16[896,128]{1,0:T(8,128)(2,1)S(1)}, bf16[896,128]{1,0:T(8,128)(2,1)S(1)}, u32[]{:S(2)}, u32[]{:S(2)}) collective-permute-start(bf16[896,128]{1,0:T(8,128)(2,1)S(1)} %copy-done.27), channel_id=1, source_target_pairs={{0,1},{1,0},{2,3},{3,2},{4,5},{5,4},{6,7},{7,6},{8,9},{9,8},{10,11... | collective-permute-start | bytes 688136 | tf_op jit(solution)/shard_map/ppermute | solution.py:21
  54.6 50.4 %copy-start.29 = (bf16[896,128]{1,0:T(8,128)(2,1)}, bf16[896,128]{1,0:T(8,128)(2,1)S(1)}, u32[]{:S(2)}) copy-start(bf16[896,128]{1,0:T(8,128)(2,1)S(1)} %collective-permute-done.5.refs_15_.refs_8_) | copy-start | bytes 688132
  54.6 50.4 %copy-start.30 = (bf16[896,128]{1,0:T(8,128)(2,1)}, bf16[896,128]{1,0:T(8,128)(2,1)S(1)}, u32[]{:S(2)}) copy-start(bf16[896,128]{1,0:T(8,128)(2,1)S(1)} %collective-permute-done.4.refs_14_.refs_7_) | copy-start | bytes 688132
  55.2 49.8 %copy-start.31 = (bf16[896,128]{1,0:T(8,128)(2,1)}, bf16[896,128]{1,0:T(8,128)(2,1)S(1)}, u32[]{:S(2)}) copy-start(bf16[896,128]{1,0:T(8,128)(2,1)S(1)} %collective-permute-done.3.refs_13_.refs_6_) | copy-start | bytes 688132
  56.8 1.8 collective-permute-start.6
  61.2 10.6 %collective-permute-start.7 = (bf16[896,128]{1,0:T(8,128)(2,1)S(1)}, bf16[896,128]{1,0:T(8,128)(2,1)S(1)}, u32[]{:S(2)}, u32[]{:S(2)}) collective-permute-start(bf16[896,128]{1,0:T(8,128)(2,1)S(1)} %copy-done.27), channel_id=1, source_target_pairs={{0,8},{8,0},{1,9},{9,1},{2,10},{10,2},{3,11},{11,3},{4,12},{12,4},... | collective-permute-start | bytes 688136 | tf_op jit(solution)/shard_map/ppermute | solution.py:21
  61.3 10.4 %collective-permute-start.8 = (bf16[896,128]{1,0:T(8,128)(2,1)S(1)}, bf16[896,128]{1,0:T(8,128)(2,1)S(1)}, u32[]{:S(2)}, u32[]{:S(2)}) collective-permute-start(bf16[896,128]{1,0:T(8,128)(2,1)S(1)} %collective-permute-done.3.refs_13_.refs_6_), channel_id=1, source_target_pairs={{0,8},{8,0},{1,9},{9,1},{2,10},{10,2},{3,11},{11,3},{4,12},{12,4},... | collective-permute-start | bytes 688136 | tf_op jit(solution)/shard_map/ppermute | solution.py:21
  61.7 10.1 %collective-permute-start.9 = (bf16[896,128]{1,0:T(8,128)(2,1)S(1)}, bf16[896,128]{1,0:T(8,128)(2,1)S(1)}, u32[]{:S(2)}, u32[]{:S(2)}) collective-permute-start(bf16[896,128]{1,0:T(8,128)(2,1)S(1)} %collective-permute-done.4.refs_14_.refs_7_), channel_id=1, source_target_pairs={{0,8},{8,0},{1,9},{9,1},{2,10},{10,2},{3,11},{11,3},{4,12},{12,4},... | collective-permute-start | bytes 688136 | tf_op jit(solution)/shard_map/ppermute | solution.py:21
  61.8 9.9 %collective-permute-start.10 = (bf16[896,128]{1,0:T(8,128)(2,1)S(1)}, bf16[896,128]{1,0:T(8,128)(2,1)S(1)}, u32[]{:S(2)}, u32[]{:S(2)}) collective-permute-start(bf16[896,128]{1,0:T(8,128)(2,1)S(1)} %collective-permute-done.5.refs_15_.refs_8_), channel_id=1, source_target_pairs={{0,8},{8,0},{1,9},{9,1},{2,10},{10,2},{3,11},{11,3},{4,12},{12,4},... | collective-permute-start | bytes 688136 | tf_op jit(solution)/shard_map/ppermute | solution.py:21
  71.8 5.6 %collective-permute-start.14 = (f32[4,7,8,128]{3,2,1,0:T(8,128)S(1)}, f32[4,7,8,128]{3,2,1,0:T(8,128)S(1)}, u32[]{:S(2)}, u32[]{:S(2)}) collective-permute-start(f32[4,7,8,128]{3,2,1,0:T(8,128)S(1)} %all_to_all.30.refs_0_), channel_id=1, source_target_pairs={{0,8},{8,0},{1,9},{9,1},{2,10},{10,2},{3,11},{11,3},{4,12},{12,4},... | collective-permute-start | bytes 344072 | tf_op jit(solution)/shard_map/ppermute | solution.py:21
  71.9 8.1 %collective-permute-start.13 = (f32[4,7,8,128]{3,2,1,0:T(8,128)S(1)}, f32[4,7,8,128]{3,2,1,0:T(8,128)S(1)}, u32[]{:S(2)}, u32[]{:S(2)}) collective-permute-start(f32[4,7,8,128]{3,2,1,0:T(8,128)S(1)} %all_to_all.30.refs_0_), channel_id=1, source_target_pairs={{0,48},{16,32},{32,16},{48,0},{1,49},{17,33},{33,17},{49,1},{2,50}... | collective-permute-start | bytes 344072 | tf_op jit(solution)/shard_map/ppermute | solution.py:21
  73.3 8.1 %collective-permute-start.12 = (f32[4,7,8,128]{3,2,1,0:T(8,128)S(1)}, f32[4,7,8,128]{3,2,1,0:T(8,128)S(1)}, u32[]{:S(2)}, u32[]{:S(2)}) collective-permute-start(f32[4,7,8,128]{3,2,1,0:T(8,128)S(1)} %all_to_all.30.refs_0_), channel_id=1, source_target_pairs={{0,32},{16,48},{32,0},{48,16},{1,33},{17,49},{33,1},{49,17},{2,34}... | collective-permute-start | bytes 344072 | tf_op jit(solution)/shard_map/ppermute | solution.py:21
  75.9 7.6 %collective-permute-start.11 = (f32[4,7,8,128]{3,2,1,0:T(8,128)S(1)}, f32[4,7,8,128]{3,2,1,0:T(8,128)S(1)}, u32[]{:S(2)}, u32[]{:S(2)}) collective-permute-start(f32[4,7,8,128]{3,2,1,0:T(8,128)S(1)} %all_to_all.30.refs_0_), channel_id=1, source_target_pairs={{0,16},{16,0},{32,48},{48,32},{1,17},{17,1},{33,49},{49,33},{2,18}... | collective-permute-start | bytes 344072 | tf_op jit(solution)/shard_map/ppermute | solution.py:21
  76.1 9.5 %collective-permute-start.20 = (f32[8,4,8,128]{3,2,1,0:T(8,128)}, f32[8,4,8,128]{3,2,1,0:T(8,128)S(1)}, u32[]{:S(2)}, u32[]{:S(2)}) collective-permute-start(f32[8,4,8,128]{3,2,1,0:T(8,128)} %get-tuple-element.72.refs_8_), channel_id=1, source_target_pairs={{0,48},{16,32},{32,16},{48,0},{1,49},{17,33},{33,17},{49,1},{2,50}... | collective-permute-start | bytes 393224 | tf_op jit(solution)/shard_map/ppermute | solution.py:21
  77.4 8.2 %collective-permute-start.19 = (f32[8,4,8,128]{3,2,1,0:T(8,128)}, f32[8,4,8,128]{3,2,1,0:T(8,128)S(1)}, u32[]{:S(2)}, u32[]{:S(2)}) collective-permute-start(f32[8,4,8,128]{3,2,1,0:T(8,128)} %get-tuple-element.72.refs_8_), channel_id=1, source_target_pairs={{0,32},{16,48},{32,0},{48,16},{1,33},{17,49},{33,1},{49,17},{2,34}... | collective-permute-start | bytes 393224 | tf_op jit(solution)/shard_map/ppermute | solution.py:21
  80.0 12.7 %collective-permute-start.23 = (bf16[896,128]{1,0:T(8,128)(2,1)S(1)}, bf16[896,128]{1,0:T(8,128)(2,1)S(1)}, u32[]{:S(2)}, u32[]{:S(2)}) collective-permute-start(bf16[896,128]{1,0:T(8,128)(2,1)S(1)} %collective-permute-done.2.refs_16_.refs_9_), channel_id=1, source_target_pairs={{0,3},{1,2},{2,1},{3,0},{4,7},{5,6},{6,5},{7,4},{8,11},{9,10},{10,... | collective-permute-start | bytes 688136 | tf_op jit(solution)/shard_map/ppermute | solution.py:21
  81.4 11.3 %collective-permute-start.22 = (bf16[896,128]{1,0:T(8,128)(2,1)S(1)}, bf16[896,128]{1,0:T(8,128)(2,1)S(1)}, u32[]{:S(2)}, u32[]{:S(2)}) collective-permute-start(bf16[896,128]{1,0:T(8,128)(2,1)S(1)} %collective-permute-done.2.refs_16_.refs_9_), channel_id=1, source_target_pairs={{0,2},{1,3},{2,0},{3,1},{4,6},{5,7},{6,4},{7,5},{8,10},{9,11},{10,... | collective-permute-start | bytes 688136 | tf_op jit(solution)/shard_map/ppermute | solution.py:21
  83.5 9.8 %collective-permute-start.21 = (bf16[896,128]{1,0:T(8,128)(2,1)S(1)}, bf16[896,128]{1,0:T(8,128)(2,1)S(1)}, u32[]{:S(2)}, u32[]{:S(2)}) collective-permute-start(bf16[896,128]{1,0:T(8,128)(2,1)S(1)} %collective-permute-done.2.refs_16_.refs_9_), channel_id=1, source_target_pairs={{0,1},{1,0},{2,3},{3,2},{4,5},{5,4},{6,7},{7,6},{8,9},{9,8},{10,11... | collective-permute-start | bytes 688136 | tf_op jit(solution)/shard_map/ppermute | solution.py:21
  85.6 1.3 collective-permute-start.17
  85.6 1.5 collective-permute-start.16
  86.9 6.4 %collective-permute-start.15 = (f32[4,7,8,128]{3,2,1,0:T(8,128)S(1)}, f32[4,7,8,128]{3,2,1,0:T(8,128)S(1)}, u32[]{:S(2)}, u32[]{:S(2)}) collective-permute-start(f32[4,7,8,128]{3,2,1,0:T(8,128)S(1)} %collective-permute-done.11.refs_1_), channel_id=1, source_target_pairs={{0,8},{8,0},{1,9},{9,1},{2,10},{10,2},{3,11},{11,3},{4,12},{12,4},... | collective-permute-start | bytes 344072 | tf_op jit(solution)/shard_map/ppermute | solution.py:21
  87.1 17.8 %collective-permute-start.24 = (bf16[896,128]{1,0:T(8,128)(2,1)S(1)}, bf16[896,128]{1,0:T(8,128)(2,1)S(1)}, u32[]{:S(2)}, u32[]{:S(2)}) collective-permute-start(bf16[896,128]{1,0:T(8,128)(2,1)S(1)} %collective-permute-done.2.refs_16_.refs_9_), channel_id=1, source_target_pairs={{0,8},{8,0},{1,9},{9,1},{2,10},{10,2},{3,11},{11,3},{4,12},{12,4},... | collective-permute-start | bytes 688136 | tf_op jit(solution)/shard_map/ppermute | solution.py:21
  92.7 12.2 %collective-permute-start.27 = (bf16[896,128]{1,0:T(8,128)(2,1)S(1)}, bf16[896,128]{1,0:T(8,128)(2,1)S(1)}, u32[]{:S(2)}, u32[]{:S(2)}) collective-permute-start(bf16[896,128]{1,0:T(8,128)(2,1)S(1)} %collective-permute-done.23.refs_19_.refs_12_), channel_id=1, source_target_pairs={{0,8},{8,0},{1,9},{9,1},{2,10},{10,2},{3,11},{11,3},{4,12},{12,4},... | collective-permute-start | bytes 688136 | tf_op jit(solution)/shard_map/ppermute | solution.py:21
  92.7 12.2 %collective-permute-start.26 = (bf16[896,128]{1,0:T(8,128)(2,1)S(1)}, bf16[896,128]{1,0:T(8,128)(2,1)S(1)}, u32[]{:S(2)}, u32[]{:S(2)}) collective-permute-start(bf16[896,128]{1,0:T(8,128)(2,1)S(1)} %collective-permute-done.22.refs_18_.refs_11_), channel_id=1, source_target_pairs={{0,8},{8,0},{1,9},{9,1},{2,10},{10,2},{3,11},{11,3},{4,12},{12,4},... | collective-permute-start | bytes 688136 | tf_op jit(solution)/shard_map/ppermute | solution.py:21
  93.3 11.6 %collective-permute-start.25 = (bf16[896,128]{1,0:T(8,128)(2,1)S(1)}, bf16[896,128]{1,0:T(8,128)(2,1)S(1)}, u32[]{:S(2)}, u32[]{:S(2)}) collective-permute-start(bf16[896,128]{1,0:T(8,128)(2,1)S(1)} %collective-permute-done.21.refs_17_.refs_10_), channel_id=1, source_target_pairs={{0,8},{8,0},{1,9},{9,1},{2,10},{10,2},{3,11},{11,3},{4,12},{12,4},... | collective-permute-start | bytes 688136 | tf_op jit(solution)/shard_map/ppermute | solution.py:21
  93.3 7.4 %collective-permute-start.18 = (f32[8,4,8,128]{3,2,1,0:T(8,128)}, f32[8,4,8,128]{3,2,1,0:T(8,128)S(1)}, u32[]{:S(2)}, u32[]{:S(2)}) collective-permute-start(f32[8,4,8,128]{3,2,1,0:T(8,128)} %get-tuple-element.72.refs_8_), channel_id=1, source_target_pairs={{0,16},{16,0},{32,48},{48,32},{1,17},{17,1},{33,49},{49,33},{2,18}... | collective-permute-start | bytes 393224 | tf_op jit(solution)/shard_map/ppermute | solution.py:21
  100.7 16.4 %collective-permute-start.28 = (f32[4,16,896]{2,1,0:T(8,128)}, f32[4,16,896]{2,1,0:T(8,128)S(1)}, u32[]{:S(2)}, u32[]{:S(2)}) collective-permute-start(f32[4,16,896]{2,1,0:T(8,128)} %get-tuple-element.76), channel_id=1, source_target_pairs={{0,4},{4,0},{1,5},{5,1},{2,6},{6,2},{3,7},{7,3},{8,12},{12,8},{9,1... | collective-permute-start | bytes 688136 | tf_op jit(solution)/shard_map/ppermute | solution.py:21
  117.1 24.9 %all-to-all-start.3 = ((bf16[32,32,256]{2,1,0:T(8,128)(2,1)}), bf16[32,32,256]{2,1,0:T(8,128)(2,1)S(1)}, u32[]{:S(2)}, u32[]{:S(2)}) async-start(bf16[32,32,256]{2,1,0:T(8,128)(2,1)} %get-tuple-element.88.refs_0_), calls=%async_computation.3 | async-start | bytes 1048576 | tf_op jit(solution)/shard_map/all_to_all | solution.py:422
  126.9 10.6 %collective-permute-start.29 = (f32[2,16,896]{2,1,0:T(8,128)}, f32[2,16,896]{2,1,0:T(8,128)S(1)}, u32[]{:S(2)}, u32[]{:S(2)}) collective-permute-start(f32[2,16,896]{2,1,0:T(8,128)} %get-tuple-element.80), channel_id=1, source_target_pairs={{0,1},{1,0},{2,3},{3,2},{4,5},{5,4},{6,7},{7,6},{8,9},{9,8},{10,11... | collective-permute-start | bytes 344072 | tf_op jit(solution)/shard_map/ppermute | solution.py:21
  127.9 9.6 %collective-permute-start.30 = (f32[2,16,896]{2,1,0:T(8,128)}, f32[2,16,896]{2,1,0:T(8,128)S(1)}, u32[]{:S(2)}, u32[]{:S(2)}) collective-permute-start(f32[2,16,896]{2,1,0:T(8,128)} %get-tuple-element.81), channel_id=1, source_target_pairs={{0,2},{1,3},{2,0},{3,1},{4,6},{5,7},{6,4},{7,5},{8,10},{9,11},{10,... | collective-permute-start | bytes 344072 | tf_op jit(solution)/shard_map/ppermute | solution.py:21
  130.7 6.9 %collective-permute-start.31 = (f32[2,16,896]{2,1,0:T(8,128)}, f32[2,16,896]{2,1,0:T(8,128)S(1)}, u32[]{:S(2)}, u32[]{:S(2)}) collective-permute-start(f32[2,16,896]{2,1,0:T(8,128)} %get-tuple-element.82), channel_id=1, source_target_pairs={{0,3},{1,2},{2,1},{3,0},{4,7},{5,6},{6,5},{7,4},{8,11},{9,10},{10,... | collective-permute-start | bytes 344072 | tf_op jit(solution)/shard_map/ppermute | solution.py:21
  142.0 17.0 %all-to-all-start.4 = ((f32[16,8,896]{2,1,0:T(8,128)}), f32[16,8,896]{2,1,0:T(8,128)S(1)}, u32[]{:S(2)}, u32[]{:S(2)}) async-start(f32[16,8,896]{2,1,0:T(8,128)} %back.1), calls=%async_computation.4 | async-start | bytes 917504 | tf_op jit(solution)/shard_map/all_to_all | solution.py:429
  146.9 25.0 %collective-permute-start.38 = (bf16[32,32,256]{2,1,0:T(8,128)(2,1)S(1)}, bf16[32,32,256]{2,1,0:T(8,128)(2,1)S(1)}, u32[]{:S(2)}, u32[]{:S(2)}) collective-permute-start(bf16[32,32,256]{2,1,0:T(8,128)(2,1)S(1)} %all-to-all-done.3.refs_0_), channel_id=1, source_target_pairs={{0,3},{1,2},{2,1},{3,0},{4,7},{5,6},{6,5},{7,4},{8,11},{9,10},{10,... | collective-permute-start | bytes 1572872 | tf_op jit(solution)/shard_map/ppermute | solution.py:21
  149.2 22.6 %collective-permute-start.37 = (bf16[32,32,256]{2,1,0:T(8,128)(2,1)S(1)}, bf16[32,32,256]{2,1,0:T(8,128)(2,1)S(1)}, u32[]{:S(2)}, u32[]{:S(2)}) collective-permute-start(bf16[32,32,256]{2,1,0:T(8,128)(2,1)S(1)} %all-to-all-done.3.refs_0_), channel_id=1, source_target_pairs={{0,2},{1,3},{2,0},{3,1},{4,6},{5,7},{6,4},{7,5},{8,10},{9,11},{10,... | collective-permute-start | bytes 1572872 | tf_op jit(solution)/shard_map/ppermute | solution.py:21
  149.9 22.5 %collective-permute-start.36 = (bf16[32,32,256]{2,1,0:T(8,128)(2,1)S(1)}, bf16[32,32,256]{2,1,0:T(8,128)(2,1)S(1)}, u32[]{:S(2)}, u32[]{:S(2)}) collective-permute-start(bf16[32,32,256]{2,1,0:T(8,128)(2,1)S(1)} %all-to-all-done.3.refs_0_), channel_id=1, source_target_pairs={{0,1},{1,0},{2,3},{3,2},{4,5},{5,4},{6,7},{7,6},{8,9},{9,8},{10,11... | collective-permute-start | bytes 1572872 | tf_op jit(solution)/shard_map/ppermute | solution.py:21
  150.9 1.3 collective-permute-start.32
  151.0 1.5 collective-permute-start.33
  152.3 1.3 collective-permute-start.34
  152.4 1.3 collective-permute-start.35
  161.5 20.4 %all-to-all-start.5 = ((f32[8,8,128]{2,1,0:T(8,128)}), f32[8,8,128]{2,1,0:T(8,128)S(1)}, u32[]{:S(2)}, u32[]{:S(2)}) async-start(f32[8,8,128]{2,1,0:T(8,128)} %total.1), calls=%async_computation.5 | async-start | bytes 65536 | tf_op jit(solution)/shard_map/all_to_all | solution.py:431
  (42 other events, 436.8 us)

commit v4 on v3

--- a/solution.py
+++ b/solution.py
@@ -35,7 +35,7 @@
 
 SMEM = pl.BlockSpec(memory_space=pltpu.SMEM)
 VMEM = pl.BlockSpec(memory_space=pltpu.VMEM)
-HBM = pl.BlockSpec(memory_space=pl.ANY)
+HBM = pl.BlockSpec(memory_space=pltpu.HBM)
 
 
 def part_kernel(x_ref, x_other_ref, gate_ref, up_ref, theirs_ref, width_ref, gains_ref, target_ref, out_ref, gain_ref):
@@ -77,22 +77,31 @@
     )(x, x_other, gate, up, theirs, widths, gains, targets)
 
 
-def sum_kernel(part_ref, out_ref):
+def sum_kernel(part_ref, out_ref, held, sem):
     lanes = out_ref.shape[1] - 6
+    copies = [
+        pltpu.make_async_copy(part_ref.at[i * 4 + y], held.at[i * 4 + y], sem.at[i * 4 + y])
+        for y in range(4)
+        for i in range(4)
+    ]
+    for copy in copies:
+        copy.start()
     for y in range(4):
+        for copy in copies[y * 4 : y * 4 + 4]:
+            copy.wait()
         for e in range(2):
             for lane in range(lanes):
                 t = e * lanes + lane
-                total = (part_ref[y, t] + part_ref[4 + y, t]) + (part_ref[8 + y, t] + part_ref[12 + y, t])
+                total = (held[y, t] + held[4 + y, t]) + (held[8 + y, t] + held[12 + y, t])
                 out_ref[:, lane, y * 2 + e, :] = total
     x, y = lax.axis_index("x"), lax.axis_index("y")
     for high in range(2):
         for half in range(2):
-            target = part_ref[y * 4 + high * 2 + x // 2, 2 * lanes + half]
+            target = held[y * 4 + high * 2 + x // 2, 2 * lanes + half]
             for slot in range(high, 8, 2):
                 out_ref[slot, lanes + half] = target
     for k in range(4):
-        gain = part_ref[x * 4 + k, 2 * lanes + 2]
+        gain = held[k * 4 + y, 2 * lanes + 2]
         for slot in range(8):
             out_ref[slot, lanes + 2 + k] = gain
 
@@ -101,9 +110,10 @@
     lanes = (part.shape[1] - 3) // 2
     return pl.pallas_call(
         sum_kernel,
-        in_specs=[VMEM],
+        in_specs=[HBM],
         out_specs=VMEM,
         out_shape=jax.ShapeDtypeStruct((8, lanes + 6, 8, 128), F32),
+        scratch_shapes=[pltpu.VMEM(part.shape, F32), pltpu.SemaphoreType.DMA((16,))],
         compiler_params=params(),
         name="sum_x",
     )(part)
@@ -184,7 +194,7 @@
         at = pl.ds((x ^ k) * 4, 4)
         first.append(pltpu.make_async_copy(raw_refs[k], raw_all.at[core, at], raw_sem.at[k]))
         first.append(pltpu.make_async_copy(other_refs[k], raw_all.at[1 - core, at], raw_sem.at[4 + k]))
-        first.append(pltpu.make_async_copy(gain_refs[k], gain_all.at[x ^ k], gain_sem.at[k]))
+        first.append(pltpu.make_async_copy(gain_refs[k], gain_all.at[y ^ k], gain_sem.at[k]))
     for p in range(8):
         second.append(pltpu.make_async_copy(mine_refs[p], down_all.at[core, p], mine_sem.at[p]))
         second.append(pltpu.make_async_copy(theirs_refs[p], down_all.at[1 - core, p], theirs_sem.at[p]))
@@ -203,7 +213,7 @@
                 raw = raw_all[unit, :, lane, other * 2 + e, :]
                 row_refs[k][a, e, :, cols] = raw
                 for v in range(16):
-                    gain = gain_all[v % 4, unit * 4 + v // 4, other, lane : lane + 1, :]
+                    gain = gain_all[other, unit * 4 + v // 4, v % 4, lane : lane + 1, :]
                     at = v * 32 + e * 16
                     hidden[at : at + 16, cols] = (raw * gain).astype(BF16)
         down = jnp.concatenate([down_all[0, p], down_all[1, p]], axis=1)
@@ -343,16 +353,23 @@
 def grad_kernel(scale, hidden_ref, *refs):
     res_refs, out_ref, res_all, sem = refs[:4], refs[4], refs[5], refs[6]
     step = pl.program_id(0)
+    some = out_ref.shape[2] // 256
+
+    def copies(at):
+        for k in range(4):
+            for z in range(2):
+                part = pl.ds(z * 16 + at * some, some)
+                yield pltpu.make_async_copy(res_refs[k].at[part], res_all.at[k, part], sem.at[at, k * 2 + z])
 
     @pl.when(step == 0)
     def _():
-        copies = [pltpu.make_async_copy(res_refs[k], res_all.at[k], sem.at[k]) for k in range(4)]
-        for c in copies:
-            c.start()
-        for c in copies:
-            c.wait()
-
-    some = out_ref.shape[2] // 256
+        for at in range(16 // some):
+            for copy in copies(at):
+                copy.start()
+
+    for copy in copies(step):
+        copy.wait()
+
     block = jnp.concatenate(
         [
             jnp.concatenate([res_all[k, z * 16 + step * some + q] for k in range(4) for z in range(2)])
@@ -367,14 +384,14 @@
 def grad_call(hidden, res4, scale):
     width = hidden.shape[0]
     pieces, rows, feats = res4[0].shape
-    blocks, some = pieces // 2, 2
+    blocks, some = pieces // 2, 4
     return pl.pallas_call(
         functools.partial(grad_kernel, scale),
         grid=(blocks // some,),
         in_specs=[pl.BlockSpec(hidden.shape, lambda s: (0, 0))] + [HBM] * 4,
         out_specs=pl.BlockSpec((1, width, some * feats), lambda s: (0, 0, s)),
         out_shape=jax.ShapeDtypeStruct((1, width, blocks * feats), BF16),
-        scratch_shapes=[pltpu.VMEM((4, pieces, rows, feats), BF16), pltpu.SemaphoreType.DMA((4,))],
+        scratch_shapes=[pltpu.VMEM((4, pieces, rows, feats), BF16), pltpu.SemaphoreType.DMA((blocks // some, 8))],
         compiler_params=params(),
         cost_estimate=pl.CostEstimate(
             flops=40 * 8 * rows * width * blocks * feats, bytes_accessed=10 * MIB, transcendentals=0
@@ -402,16 +419,16 @@
     mine = near4(down, "y")
     part = after(part, mine)
     raw, target, gain_z = raw_call(part, swap(part, "core"))
-    mine = after(mine, raw)
+    mine, far = after((mine, far), raw)
     raw = lax.all_to_all(raw, "zl", 0, 0, tiled=True)
     theirs = [swap(d, "core") for d in mine]
-    raw = after(raw, theirs)
+    mine_far = near4(far, "y")
+    raw = after(raw, (theirs, mine_far))
     raws = near4(raw, "x")
     others = [swap(r, "core") for r in raws]
-    far, gain_z = after((far, gain_z), raw)
-    mine_far = near4(far, "y")
+    mine_far, gain_z = after((mine_far, gain_z), raw)
     theirs_far = [swap(d, "core") for d in mine_far]
-    all_gains = near4(gain_z, "x")
+    all_gains = near4(gain_z, "y")
     mine, theirs = mine + mine_far, theirs + theirs_far
 
     near, far = extract_call(raws, others)

time: 184 us -> 178 us (0.967)
  starting transfers between devices: 78.8 us -> 75.2 us
    ppermute x39, starting transfers between devices: 43.8 us -> 39.7 us  [swap(): return lax.ppermute(value, axis, [(i, i ^ mask) for i in range(SIZE[axis])])]
where the time goes in v4:
time: 178 us; the launch traced here: 177 us
  starting transfers between devices  75.2 us (42%)
  waiting for transfers between devices  45.8 us (26%)
  Pallas kernels  36.4 us (20%)
  blocking collectives  9.2 us (5%)
  local copies, waits for them, and re-layouts  7.02 us (4%)
    ppermute x39, starting transfers between devices, swap(): return lax.ppermute(value, axis, [(i, i ^ mask) for i in range(SIZE[axis])])  39.7 us
    ppermute x39, waiting for transfers between devices, swap(): return lax.ppermute(value, axis, [(i, i ^ mask) for i in range(SIZE[axis])])  35.4 us
    all_to_all x1, blocking collectives, local(): raw = lax.all_to_all(raw, 'zl', 0, 0, tiled=True)  9.2 us
    pallas_call x1, Pallas kernels, output_call(): pl.pallas_call(output_kernel, in_specs=[HBM] * 28 + [VMEM], out_specs=[VM...  9 us
    all_to_all x1, starting transfers between devices, local(): lax.all_to_all(after(res, far), ('zh', 'zl', 'x'), 0, 0, tiled=True)  8.49 us
    all_to_all x1, starting transfers between devices, local(): part = lax.all_to_all(part, ('zh', 'zl'), 0, 0, tiled=True)  8.48 us
    all_to_all x1, starting transfers between devices, local(): part = lax.all_to_all(part, ('x', 'y'), 0, 0, tiled=True)  7.61 us
    unnamed x93, local copies, waits for them, and re-layouts  7.02 us
  transfers between devices with their start and end apart: 44, of which 21 were waited for; matrix products, arithmetic and copies ran while one was open for 0% of the time, Pallas kernels for 17%

profile of v4, /device:TPU:2, one launch (start us, length us, event | category | flops | bytes accessed | tf_op | source)
XLA Modules:
  0.0 177.0 jit_solution(14111628380582040989)
XLA Ops:
  0.6 1.0 broadcast_select_fusion
  4.8 2.6 %part.1 = (f32[16,17,8,128]{3,2,1,0:T(8,128)}, f32[1,896]{1,0:T(1,128)}) custom-call(bf16[128,256]{1,0:T(8,128)(2,1)} %x_ref.1, bf16[128,256]{1,0:T(8,128)(2,1)} %copy-done.23, bf16[128,896]{1,0:T(8,128)(2,1)} %gate_ref.1, bf16[128,896]{1,0:T(8,128)(2,1)} %up_ref.1, bf16[128,896]{1,0:T(8,128)(2,1)} %copy-done.7, s32[1]{0:T(128)} %copy.11.width_ref, ...), custom_call_target="tpu_custom_call" | custom-call | tf_op jit(solution)/shard_map/part/pallas_call | solution.py:67
  7.4 7.6 %all-to-all-start = ((f32[16,17,8,128]{3,2,1,0:T(8,128)}), f32[16,17,8,128]{3,2,1,0:T(8,128)S(1)}, u32[]{:S(2)}, u32[]{:S(2)}) async-start(f32[16,17,8,128]{3,2,1,0:T(8,128)} %get-tuple-element.54), calls=%async_computation | async-start | bytes 2228224 | tf_op jit(solution)/shard_map/all_to_all | solution.py:414
  15.0 7.3 %collective-permute-start.2 = (bf16[896,128]{1,0:T(8,128)(2,1)S(1)}, bf16[896,128]{1,0:T(8,128)(2,1)S(1)}, u32[]{:S(2)}, u32[]{:S(2)}) collective-permute-start(bf16[896,128]{1,0:T(8,128)(2,1)S(1)} %copy-done.27), channel_id=1, source_target_pairs={{0,4},{4,0},{1,5},{5,1},{2,6},{6,2},{3,7},{7,3},{8,12},{12,8},{9,1... | collective-permute-start | bytes 688136 | tf_op jit(solution)/shard_map/ppermute | solution.py:21
  22.3 6.5 %collective-permute-done.2.refs_16_.refs_9_ = bf16[896,128]{1,0:T(8,128)(2,1)S(1)} collective-permute-done((bf16[896,128]{1,0:T(8,128)(2,1)S(1)}, bf16[896,128]{1,0:T(8,128)(2,1)S(1)}, u32[]{:S(2)}, u32[]{:S(2)}) %collective-permute-start.2) | collective-permute-done | bytes 229408 | tf_op jit(solution)/shard_map/ppermute | solution.py:21
  28.8 2.3 %all-to-all-done.part_ref = f32[16,17,8,128]{3,2,1,0:T(8,128)S(1)} async-done(((f32[16,17,8,128]{3,2,1,0:T(8,128)}), f32[16,17,8,128]{3,2,1,0:T(8,128)S(1)}, u32[]{:S(2)}, u32[]{:S(2)}) %all-to-all-start) | async-done | bytes 1114144 | tf_op jit(solution)/shard_map/all_to_all | solution.py:414
  31.2 1.0 copy-done
  32.1 2.2 %sum_x.1 = f32[8,13,8,128]{3,2,1,0:T(8,128)} custom-call(f32[16,17,8,128]{3,2,1,0:T(8,128)} %copy-done), custom_call_target="tpu_custom_call" | custom-call | tf_op jit(solution)/shard_map/sum_x/pallas_call | solution.py:111
  34.4 8.5 %all-to-all-start.1 = ((f32[8,13,8,128]{3,2,1,0:T(8,128)}), f32[8,13,8,128]{3,2,1,0:T(8,128)S(1)}, u32[]{:S(2)}, u32[]{:S(2)}) async-start(f32[8,13,8,128]{3,2,1,0:T(8,128)} %sum_x.1), calls=%async_computation.1 | async-start | bytes 851968 | tf_op jit(solution)/shard_map/all_to_all | solution.py:418
  42.9 2.2 %collective-permute-start.5 = (bf16[896,128]{1,0:T(8,128)(2,1)S(1)}, bf16[896,128]{1,0:T(8,128)(2,1)S(1)}, u32[]{:S(2)}, u32[]{:S(2)}) collective-permute-start(bf16[896,128]{1,0:T(8,128)(2,1)S(1)} %copy-done.27), channel_id=1, source_target_pairs={{0,3},{1,2},{2,1},{3,0},{4,7},{5,6},{6,5},{7,4},{8,11},{9,10},{10,... | collective-permute-start | bytes 688136 | tf_op jit(solution)/shard_map/ppermute | solution.py:21
  45.0 0.9 collective-permute-start.4
  45.9 1.1 collective-permute-start.3
  47.0 7.7 %collective-permute-done.5.refs_15_.refs_8_ = bf16[896,128]{1,0:T(8,128)(2,1)S(1)} collective-permute-done((bf16[896,128]{1,0:T(8,128)(2,1)S(1)}, bf16[896,128]{1,0:T(8,128)(2,1)S(1)}, u32[]{:S(2)}, u32[]{:S(2)}) %collective-permute-start.5) | collective-permute-done | bytes 229408 | tf_op jit(solution)/shard_map/ppermute | solution.py:21
  55.3 1.6 all-to-all-done.1.mine_ref
  56.9 1.8 collective-permute-done.6.other_ref
  59.4 1.9 %raw.1 = (f32[4,7,8,128]{3,2,1,0:T(8,128)}, f32[2,16,256]{2,1,0:T(8,128)}, f32[8,4,8,128]{3,2,1,0:T(8,128)}) custom-call(f32[8,13,8,128]{3,2,1,0:T(8,128)} %copy-done.2, f32[8,13,8,128]{3,2,1,0:T(8,128)} %copy-done.5), custom_call_target="tpu_custom_call" | custom-call | tf_op jit(solution)/shard_map/raw/pallas_call | solution.py:146
  62.3 2.3 %collective-permute-start.13 = (bf16[896,128]{1,0:T(8,128)(2,1)S(1)}, bf16[896,128]{1,0:T(8,128)(2,1)S(1)}, u32[]{:S(2)}, u32[]{:S(2)}) collective-permute-start(bf16[896,128]{1,0:T(8,128)(2,1)S(1)} %collective-permute-done.2.refs_16_.refs_9_), channel_id=1, source_target_pairs={{0,3},{1,2},{2,1},{3,0},{4,7},{5,6},{6,5},{7,4},{8,11},{9,10},{10,... | collective-permute-start | bytes 688136 | tf_op jit(solution)/shard_map/ppermute | solution.py:21
  64.6 0.9 collective-permute-start.12
  65.5 1.0 collective-permute-start.11
  66.4 9.2 %all_to_all.30.refs_0_ = f32[4,7,8,128]{3,2,1,0:T(8,128)S(1)} all-to-all(f32[4,7,8,128]{3,2,1,0:T(8,128)} %get-tuple-element.59), channel_id=1, replica_groups=mesh['zl'=4,'x'=4,'core'=2,'zh'=2,'y'=4] {'zl'}, dimensions={0} | all-to-all | bytes 229376 | tf_op jit(solution)/shard_map/all_to_all | solution.py:423
  76.7 1.3 collective-permute-start.16
  78.0 2.6 %collective-permute-start.15 = (f32[4,7,8,128]{3,2,1,0:T(8,128)S(1)}, f32[4,7,8,128]{3,2,1,0:T(8,128)S(1)}, u32[]{:S(2)}, u32[]{:S(2)}) collective-permute-start(f32[4,7,8,128]{3,2,1,0:T(8,128)S(1)} %all_to_all.30.refs_0_), channel_id=1, source_target_pairs={{0,32},{16,48},{32,0},{48,16},{1,33},{17,49},{33,1},{49,17},{2,34}... | collective-permute-start | bytes 344072 | tf_op jit(solution)/shard_map/ppermute | solution.py:21
  80.8 2.3 %collective-permute-start.23 = (f32[8,4,8,128]{3,2,1,0:T(8,128)}, f32[8,4,8,128]{3,2,1,0:T(8,128)S(1)}, u32[]{:S(2)}, u32[]{:S(2)}) collective-permute-start(f32[8,4,8,128]{3,2,1,0:T(8,128)} %get-tuple-element.77.refs_8_), channel_id=1, source_target_pairs={{0,3},{1,2},{2,1},{3,0},{4,7},{5,6},{6,5},{7,4},{8,11},{9,10},{10,... | collective-permute-start | bytes 393224 | tf_op jit(solution)/shard_map/ppermute | solution.py:21
  83.1 1.1 collective-permute-start.22
  84.3 1.2 collective-permute-done.15.refs_2_
  85.5 1.1 collective-permute-done.14.refs_1_
  86.6 3.6 %collective-permute-done.23.refs_11_ = f32[8,4,8,128]{3,2,1,0:T(8,128)S(1)} collective-permute-done((f32[8,4,8,128]{3,2,1,0:T(8,128)}, f32[8,4,8,128]{3,2,1,0:T(8,128)S(1)}, u32[]{:S(2)}, u32[]{:S(2)}) %collective-permute-start.23) | collective-permute-done | bytes 131104 | tf_op jit(solution)/shard_map/ppermute | solution.py:21
  91.9 2.3 %extract.1 = (f32[4,16,896]{2,1,0:T(8,128)}, f32[4,16,896]{2,1,0:T(8,128)}) custom-call(f32[4,7,8,128]{3,2,1,0:T(8,128)} %copy-done.4, f32[4,7,8,128]{3,2,1,0:T(8,128)} %copy-done.19, f32[4,7,8,128]{3,2,1,0:T(8,128)} %copy-done.18, f32[4,7,8,128]{3,2,1,0:T(8,128)} %copy-done.17, f32[4,7,8,128]{3,2,1,0:T(8,128)} %copy-done.16, f32[4,7,8,128]{3,2,1,0:T(8,128)} %copy-done.22, ...), custom_call_target="tpu_custom_call" | custom-call | tf_op jit(solution)/shard_map/extract/pallas_call | solution.py:175
  94.2 2.8 %collective-permute-done.21.refs_9_ = f32[8,4,8,128]{3,2,1,0:T(8,128)S(1)} collective-permute-done((f32[8,4,8,128]{3,2,1,0:T(8,128)}, f32[8,4,8,128]{3,2,1,0:T(8,128)S(1)}, u32[]{:S(2)}, u32[]{:S(2)}) %collective-permute-start.21) | collective-permute-done | bytes 131104 | tf_op jit(solution)/shard_map/ppermute | solution.py:21
  97.0 4.2 %collective-permute-start.28 = (f32[4,16,896]{2,1,0:T(8,128)}, f32[4,16,896]{2,1,0:T(8,128)S(1)}, u32[]{:S(2)}, u32[]{:S(2)}) collective-permute-start(f32[4,16,896]{2,1,0:T(8,128)} %get-tuple-element.84), channel_id=1, source_target_pairs={{0,4},{4,0},{1,5},{5,1},{2,6},{6,2},{3,7},{7,3},{8,12},{12,8},{9,1... | collective-permute-start | bytes 688136 | tf_op jit(solution)/shard_map/ppermute | solution.py:21
  102.1 9.0 %output.1 = (bf16[32,32,256]{2,1,0:T(8,128)(2,1)}, f32[2,2,16,896]{3,2,1,0:T(8,128)}, f32[2,2,16,896]{3,2,1,0:T(8,128)}, f32[2,2,16,896]{3,2,1,0:T(8,128)}, f32[2,2,16,896]{3,2,1,0:T(8,128)}) custom-call(f32[4,7,8,128]{3,2,1,0:T(8,128)} %copy-done.4, f32[4,7,8,128]{3,2,1,0:T(8,128)} %copy-done.19, f32[4,7,8,128]{3,2,1,0:T(8,128)} %copy-done.18, ...), custom_call_target="tpu_custom_call" | custom-call | flops 1879048192 | bytes 6291456 | tf_op jit(solution)/shard_map/output/pallas_call | solution.py:237
  111.1 1.7 collective-permute-done.28.far_ref
  112.8 8.5 %all-to-all-start.3 = ((bf16[32,32,256]{2,1,0:T(8,128)(2,1)}), bf16[32,32,256]{2,1,0:T(8,128)(2,1)S(1)}, u32[]{:S(2)}, u32[]{:S(2)}) async-start(bf16[32,32,256]{2,1,0:T(8,128)(2,1)} %get-tuple-element.96.refs_0_), calls=%async_computation.3 | async-start | bytes 1048576 | tf_op jit(solution)/shard_map/all_to_all | solution.py:439
  121.3 1.8 %pair.1 = (f32[2,16,896]{2,1,0:T(8,128)}, f32[2,16,896]{2,1,0:T(8,128)}, f32[2,16,896]{2,1,0:T(8,128)}, f32[2,16,896]{2,1,0:T(8,128)}) custom-call(f32[4,16,896]{2,1,0:T(8,128)} %get-tuple-element.85.near_ref, f32[4,16,896]{2,1,0:T(8,128)} %copy-done.6), custom_call_target="tpu_custom_call" | custom-call | tf_op jit(solution)/shard_map/pair/pallas_call | solution.py:317
  123.8 3.1 %collective-permute-start.30 = (f32[2,16,896]{2,1,0:T(8,128)}, f32[2,16,896]{2,1,0:T(8,128)S(1)}, u32[]{:S(2)}, u32[]{:S(2)}) collective-permute-start(f32[2,16,896]{2,1,0:T(8,128)} %get-tuple-element.89), channel_id=1, source_target_pairs={{0,2},{1,3},{2,0},{3,1},{4,6},{5,7},{6,4},{7,5},{8,10},{9,11},{10,... | collective-permute-start | bytes 344072 | tf_op jit(solution)/shard_map/ppermute | solution.py:21
  126.9 1.0 collective-permute-start.31
  127.9 5.8 %back.1 = f32[16,8,896]{2,1,0:T(8,128)} custom-call(bf16[32,32,256]{2,1,0:T(8,128)(2,1)} %get-tuple-element.96.refs_0_, f32[2,2,16,896]{3,2,1,0:T(8,128)} %get-tuple-element.92.refs_1_, f32[2,2,16,896]{3,2,1,0:T(8,128)} %get-tuple-element.93.refs_2_, f32[2,2,16,896]{3,2,1,0:T(8,128)} %get-tuple-element.94.refs_3_, ...), custom_call_target="tpu_custom_call" | custom-call | flops 1879048192 | bytes 6291456 | tf_op jit(solution)/shard_map/back/pallas_call | solution.py:276
  133.8 4.1 %all-to-all-done.3.refs_0_ = bf16[32,32,256]{2,1,0:T(8,128)(2,1)S(1)} async-done(((bf16[32,32,256]{2,1,0:T(8,128)(2,1)}), bf16[32,32,256]{2,1,0:T(8,128)(2,1)S(1)}, u32[]{:S(2)}, u32[]{:S(2)}) %all-to-all-start.3) | async-done | bytes 524320 | tf_op jit(solution)/shard_map/all_to_all | solution.py:439
  137.9 4.8 %all-to-all-start.4 = ((f32[16,8,896]{2,1,0:T(8,128)}), f32[16,8,896]{2,1,0:T(8,128)S(1)}, u32[]{:S(2)}, u32[]{:S(2)}) async-start(f32[16,8,896]{2,1,0:T(8,128)} %back.1), calls=%async_computation.4 | async-start | bytes 917504 | tf_op jit(solution)/shard_map/all_to_all | solution.py:446
  142.8 2.3 %collective-permute-start.38 = (bf16[32,32,256]{2,1,0:T(8,128)(2,1)S(1)}, bf16[32,32,256]{2,1,0:T(8,128)(2,1)S(1)}, u32[]{:S(2)}, u32[]{:S(2)}) collective-permute-start(bf16[32,32,256]{2,1,0:T(8,128)(2,1)S(1)} %all-to-all-done.3.refs_0_), channel_id=1, source_target_pairs={{0,3},{1,2},{2,1},{3,0},{4,7},{5,6},{6,5},{7,4},{8,11},{9,10},{10,... | collective-permute-start | bytes 1572872 | tf_op jit(solution)/shard_map/ppermute | solution.py:21
  145.8 1.1 collective-permute-start.36
  147.4 0.8 collective-permute-done.32.refs_4_
  150.3 2.2 %hidden.1.hidden_ref = bf16[896,256]{1,0:T(8,128)(2,1)} custom-call(f32[1,896]{1,0:T(1,128)} %get-tuple-element.53.gain_ref, f32[2,16,896]{2,1,0:T(8,128)} %get-tuple-element.98.refs_0_, f32[2,16,896]{2,1,0:T(8,128)} %copy-done.9, f32[2,16,896]{2,1,0:T(8,128)} %copy-done.10, f32[2,16,896]{2,1,0:T(8,128)} %copy-done.11, f32[2,16,896]{2,1,0:T(8,128)} %copy-done.12, ...), custom_call_target="tpu_custom_call" | custom-call | tf_op jit(solution)/shard_map/hidden/pallas_call | solution.py:342
  152.6 2.4 %all-to-all-done.4.part_ref = f32[16,8,896]{2,1,0:T(8,128)S(1)} async-done(((f32[16,8,896]{2,1,0:T(8,128)}), f32[16,8,896]{2,1,0:T(8,128)S(1)}, u32[]{:S(2)}, u32[]{:S(2)}) %all-to-all-start.4) | async-done | bytes 458784 | tf_op jit(solution)/shard_map/all_to_all | solution.py:446
  155.7 1.7 total.1
  157.4 6.1 %all-to-all-start.5 = ((f32[8,8,128]{2,1,0:T(8,128)}), f32[8,8,128]{2,1,0:T(8,128)S(1)}, u32[]{:S(2)}, u32[]{:S(2)}) async-start(f32[8,8,128]{2,1,0:T(8,128)} %total.1), calls=%async_computation.5 | async-start | bytes 65536 | tf_op jit(solution)/shard_map/all_to_all | solution.py:448
  163.5 4.2 %collective-permute-done.38.refs_3_ = bf16[32,32,256]{2,1,0:T(8,128)(2,1)S(1)} collective-permute-done((bf16[32,32,256]{2,1,0:T(8,128)(2,1)S(1)}, bf16[32,32,256]{2,1,0:T(8,128)(2,1)S(1)}, u32[]{:S(2)}, u32[]{:S(2)}) %collective-permute-start.38) | collective-permute-done | bytes 524320 | tf_op jit(solution)/shard_map/ppermute | solution.py:21
  169.5 6.8 %grad.1 = bf16[1,896,4096]{2,1,0:T(8,128)(2,1)} custom-call(bf16[896,256]{1,0:T(8,128)(2,1)} %hidden.1.hidden_ref, bf16[32,32,256]{2,1,0:T(8,128)(2,1)} %copy-done.3, bf16[32,32,256]{2,1,0:T(8,128)(2,1)} %copy-done.26, bf16[32,32,256]{2,1,0:T(8,128)(2,1)} %copy-done.25, bf16[32,32,256]{2,1,0:T(8,128)(2,1)} %copy-done.24), custom_call_target="tpu_custom_call" | custom-call | flops 37580963840 | bytes 10485760 | tf_op jit(solution)/shard_map/grad/pallas_call | solution.py:388
  (147 shorter events, 15.9 us)
Async XLA Ops:
  1.6 1.9 %collective-permute-start.1 = (bf16[128,896]{1,0:T(8,128)(2,1)S(1)}, bf16[128,896]{1,0:T(8,128)(2,1)S(1)}, u32[]{:S(2)}, u32[]{:S(2)}) collective-permute-start(bf16[128,896]{1,0:T(8,128)(2,1)S(1)} %broadcast_select_fusion), channel_id=1, source_target_pairs={{0,8},{8,0},{1,9},{9,1},{2,10},{10,2},{3,11},{11,3},{4,12},{12,4},... | collective-permute-start | bytes 688136 | tf_op jit(solution)/shard_map/ppermute | solution.py:21
  1.7 1.8 %collective-permute-start = (bf16[128,256]{1,0:T(8,128)(2,1)}, bf16[128,256]{1,0:T(8,128)(2,1)S(1)}, u32[]{:S(2)}, u32[]{:S(2)}) collective-permute-start(bf16[128,256]{1,0:T(8,128)(2,1)} %x_ref.1), channel_id=1, source_target_pairs={{0,8},{8,0},{1,9},{9,1},{2,10},{10,2},{3,11},{11,3},{4,12},{12,4},... | collective-permute-start | bytes 196616 | tf_op jit(solution)/shard_map/ppermute | solution.py:21
  7.4 23.8 %all-to-all-start = ((f32[16,17,8,128]{3,2,1,0:T(8,128)}), f32[16,17,8,128]{3,2,1,0:T(8,128)S(1)}, u32[]{:S(2)}, u32[]{:S(2)}) async-start(f32[16,17,8,128]{3,2,1,0:T(8,128)} %get-tuple-element.54), calls=%async_computation | async-start | bytes 2228224 | tf_op jit(solution)/shard_map/all_to_all | solution.py:414
  15.0 13.8 %collective-permute-start.2 = (bf16[896,128]{1,0:T(8,128)(2,1)S(1)}, bf16[896,128]{1,0:T(8,128)(2,1)S(1)}, u32[]{:S(2)}, u32[]{:S(2)}) collective-permute-start(bf16[896,128]{1,0:T(8,128)(2,1)S(1)} %copy-done.27), channel_id=1, source_target_pairs={{0,4},{4,0},{1,5},{5,1},{2,6},{6,2},{3,7},{7,3},{8,12},{12,8},{9,1... | collective-permute-start | bytes 688136 | tf_op jit(solution)/shard_map/ppermute | solution.py:21
  28.8 72.4 %copy-start.28 = (bf16[896,128]{1,0:T(8,128)(2,1)}, bf16[896,128]{1,0:T(8,128)(2,1)S(1)}, u32[]{:S(2)}) copy-start(bf16[896,128]{1,0:T(8,128)(2,1)S(1)} %collective-permute-done.2.refs_16_.refs_9_) | copy-start | bytes 688132
  34.4 22.5 %all-to-all-start.1 = ((f32[8,13,8,128]{3,2,1,0:T(8,128)}), f32[8,13,8,128]{3,2,1,0:T(8,128)S(1)}, u32[]{:S(2)}, u32[]{:S(2)}) async-start(f32[8,13,8,128]{3,2,1,0:T(8,128)} %sum_x.1), calls=%async_computation.1 | async-start | bytes 851968 | tf_op jit(solution)/shard_map/all_to_all | solution.py:418
  42.9 11.8 %collective-permute-start.5 = (bf16[896,128]{1,0:T(8,128)(2,1)S(1)}, bf16[896,128]{1,0:T(8,128)(2,1)S(1)}, u32[]{:S(2)}, u32[]{:S(2)}) collective-permute-start(bf16[896,128]{1,0:T(8,128)(2,1)S(1)} %copy-done.27), channel_id=1, source_target_pairs={{0,3},{1,2},{2,1},{3,0},{4,7},{5,6},{6,5},{7,4},{8,11},{9,10},{10,... | collective-permute-start | bytes 688136 | tf_op jit(solution)/shard_map/ppermute | solution.py:21
  45.0 9.6 %collective-permute-start.4 = (bf16[896,128]{1,0:T(8,128)(2,1)S(1)}, bf16[896,128]{1,0:T(8,128)(2,1)S(1)}, u32[]{:S(2)}, u32[]{:S(2)}) collective-permute-start(bf16[896,128]{1,0:T(8,128)(2,1)S(1)} %copy-done.27), channel_id=1, source_target_pairs={{0,2},{1,3},{2,0},{3,1},{4,6},{5,7},{6,4},{7,5},{8,10},{9,11},{10,... | collective-permute-start | bytes 688136 | tf_op jit(solution)/shard_map/ppermute | solution.py:21
  45.9 9.4 %collective-permute-start.3 = (bf16[896,128]{1,0:T(8,128)(2,1)S(1)}, bf16[896,128]{1,0:T(8,128)(2,1)S(1)}, u32[]{:S(2)}, u32[]{:S(2)}) collective-permute-start(bf16[896,128]{1,0:T(8,128)(2,1)S(1)} %copy-done.27), channel_id=1, source_target_pairs={{0,1},{1,0},{2,3},{3,2},{4,5},{5,4},{6,7},{7,6},{8,9},{9,8},{10,11... | collective-permute-start | bytes 688136 | tf_op jit(solution)/shard_map/ppermute | solution.py:21
  54.7 46.6 %copy-start.29 = (bf16[896,128]{1,0:T(8,128)(2,1)}, bf16[896,128]{1,0:T(8,128)(2,1)S(1)}, u32[]{:S(2)}) copy-start(bf16[896,128]{1,0:T(8,128)(2,1)S(1)} %collective-permute-done.5.refs_15_.refs_8_) | copy-start | bytes 688132
  54.7 46.6 %copy-start.30 = (bf16[896,128]{1,0:T(8,128)(2,1)}, bf16[896,128]{1,0:T(8,128)(2,1)S(1)}, u32[]{:S(2)}) copy-start(bf16[896,128]{1,0:T(8,128)(2,1)S(1)} %collective-permute-done.4.refs_14_.refs_7_) | copy-start | bytes 688132
  55.3 46.0 %copy-start.31 = (bf16[896,128]{1,0:T(8,128)(2,1)}, bf16[896,128]{1,0:T(8,128)(2,1)S(1)}, u32[]{:S(2)}) copy-start(bf16[896,128]{1,0:T(8,128)(2,1)S(1)} %collective-permute-done.3.refs_13_.refs_6_) | copy-start | bytes 688132
  56.9 1.8 %collective-permute-start.6 = (f32[8,13,8,128]{3,2,1,0:T(8,128)S(1)}, f32[8,13,8,128]{3,2,1,0:T(8,128)S(1)}, u32[]{:S(2)}, u32[]{:S(2)}) collective-permute-start(f32[8,13,8,128]{3,2,1,0:T(8,128)S(1)} %all-to-all-done.1.mine_ref), channel_id=1, source_target_pairs={{0,8},{8,0},{1,9},{9,1},{2,10},{10,2},{3,11},{11,3},{4,12},{12,4},... | collective-permute-start | bytes 1277960 | tf_op jit(solution)/shard_map/ppermute | solution.py:21
  61.3 3.3 %collective-permute-start.7 = (bf16[896,128]{1,0:T(8,128)(2,1)S(1)}, bf16[896,128]{1,0:T(8,128)(2,1)S(1)}, u32[]{:S(2)}, u32[]{:S(2)}) collective-permute-start(bf16[896,128]{1,0:T(8,128)(2,1)S(1)} %copy-done.27), channel_id=1, source_target_pairs={{0,8},{8,0},{1,9},{9,1},{2,10},{10,2},{3,11},{11,3},{4,12},{12,4},... | collective-permute-start | bytes 688136 | tf_op jit(solution)/shard_map/ppermute | solution.py:21
  61.4 4.0 %collective-permute-start.8 = (bf16[896,128]{1,0:T(8,128)(2,1)S(1)}, bf16[896,128]{1,0:T(8,128)(2,1)S(1)}, u32[]{:S(2)}, u32[]{:S(2)}) collective-permute-start(bf16[896,128]{1,0:T(8,128)(2,1)S(1)} %collective-permute-done.3.refs_13_.refs_6_), channel_id=1, source_target_pairs={{0,8},{8,0},{1,9},{9,1},{2,10},{10,2},{3,11},{11,3},{4,12},{12,4},... | collective-permute-start | bytes 688136 | tf_op jit(solution)/shard_map/ppermute | solution.py:21
  61.8 13.8 %collective-permute-start.9 = (bf16[896,128]{1,0:T(8,128)(2,1)S(1)}, bf16[896,128]{1,0:T(8,128)(2,1)S(1)}, u32[]{:S(2)}, u32[]{:S(2)}) collective-permute-start(bf16[896,128]{1,0:T(8,128)(2,1)S(1)} %collective-permute-done.4.refs_14_.refs_7_), channel_id=1, source_target_pairs={{0,8},{8,0},{1,9},{9,1},{2,10},{10,2},{3,11},{11,3},{4,12},{12,4},... | collective-permute-start | bytes 688136 | tf_op jit(solution)/shard_map/ppermute | solution.py:21
  62.0 13.7 %collective-permute-start.10 = (bf16[896,128]{1,0:T(8,128)(2,1)S(1)}, bf16[896,128]{1,0:T(8,128)(2,1)S(1)}, u32[]{:S(2)}, u32[]{:S(2)}) collective-permute-start(bf16[896,128]{1,0:T(8,128)(2,1)S(1)} %collective-permute-done.5.refs_15_.refs_8_), channel_id=1, source_target_pairs={{0,8},{8,0},{1,9},{9,1},{2,10},{10,2},{3,11},{11,3},{4,12},{12,4},... | collective-permute-start | bytes 688136 | tf_op jit(solution)/shard_map/ppermute | solution.py:21
  62.3 13.8 %collective-permute-start.13 = (bf16[896,128]{1,0:T(8,128)(2,1)S(1)}, bf16[896,128]{1,0:T(8,128)(2,1)S(1)}, u32[]{:S(2)}, u32[]{:S(2)}) collective-permute-start(bf16[896,128]{1,0:T(8,128)(2,1)S(1)} %collective-permute-done.2.refs_16_.refs_9_), channel_id=1, source_target_pairs={{0,3},{1,2},{2,1},{3,0},{4,7},{5,6},{6,5},{7,4},{8,11},{9,10},{10,... | collective-permute-start | bytes 688136 | tf_op jit(solution)/shard_map/ppermute | solution.py:21
  64.6 11.5 %collective-permute-start.12 = (bf16[896,128]{1,0:T(8,128)(2,1)S(1)}, bf16[896,128]{1,0:T(8,128)(2,1)S(1)}, u32[]{:S(2)}, u32[]{:S(2)}) collective-permute-start(bf16[896,128]{1,0:T(8,128)(2,1)S(1)} %collective-permute-done.2.refs_16_.refs_9_), channel_id=1, source_target_pairs={{0,2},{1,3},{2,0},{3,1},{4,6},{5,7},{6,4},{7,5},{8,10},{9,11},{10,... | collective-permute-start | bytes 688136 | tf_op jit(solution)/shard_map/ppermute | solution.py:21
  65.5 11.3 %collective-permute-start.11 = (bf16[896,128]{1,0:T(8,128)(2,1)S(1)}, bf16[896,128]{1,0:T(8,128)(2,1)S(1)}, u32[]{:S(2)}, u32[]{:S(2)}) collective-permute-start(bf16[896,128]{1,0:T(8,128)(2,1)S(1)} %collective-permute-done.2.refs_16_.refs_9_), channel_id=1, source_target_pairs={{0,1},{1,0},{2,3},{3,2},{4,5},{5,4},{6,7},{7,6},{8,9},{9,8},{10,11... | collective-permute-start | bytes 688136 | tf_op jit(solution)/shard_map/ppermute | solution.py:21
  76.7 6.4 %collective-permute-start.17 = (f32[4,7,8,128]{3,2,1,0:T(8,128)S(1)}, f32[4,7,8,128]{3,2,1,0:T(8,128)S(1)}, u32[]{:S(2)}, u32[]{:S(2)}) collective-permute-start(f32[4,7,8,128]{3,2,1,0:T(8,128)S(1)} %all_to_all.30.refs_0_), channel_id=1, source_target_pairs={{0,8},{8,0},{1,9},{9,1},{2,10},{10,2},{3,11},{11,3},{4,12},{12,4},... | collective-permute-start | bytes 344072 | tf_op jit(solution)/shard_map/ppermute | solution.py:21
  76.7 7.5 %collective-permute-start.16 = (f32[4,7,8,128]{3,2,1,0:T(8,128)S(1)}, f32[4,7,8,128]{3,2,1,0:T(8,128)S(1)}, u32[]{:S(2)}, u32[]{:S(2)}) collective-permute-start(f32[4,7,8,128]{3,2,1,0:T(8,128)S(1)} %all_to_all.30.refs_0_), channel_id=1, source_target_pairs={{0,48},{16,32},{32,16},{48,0},{1,49},{17,33},{33,17},{49,1},{2,50}... | collective-permute-start | bytes 344072 | tf_op jit(solution)/shard_map/ppermute | solution.py:21
  78.0 7.5 %collective-permute-start.15 = (f32[4,7,8,128]{3,2,1,0:T(8,128)S(1)}, f32[4,7,8,128]{3,2,1,0:T(8,128)S(1)}, u32[]{:S(2)}, u32[]{:S(2)}) collective-permute-start(f32[4,7,8,128]{3,2,1,0:T(8,128)S(1)} %all_to_all.30.refs_0_), channel_id=1, source_target_pairs={{0,32},{16,48},{32,0},{48,16},{1,33},{17,49},{33,1},{49,17},{2,34}... | collective-permute-start | bytes 344072 | tf_op jit(solution)/shard_map/ppermute | solution.py:21
  80.6 6.0 %collective-permute-start.14 = (f32[4,7,8,128]{3,2,1,0:T(8,128)S(1)}, f32[4,7,8,128]{3,2,1,0:T(8,128)S(1)}, u32[]{:S(2)}, u32[]{:S(2)}) collective-permute-start(f32[4,7,8,128]{3,2,1,0:T(8,128)S(1)} %all_to_all.30.refs_0_), channel_id=1, source_target_pairs={{0,16},{16,0},{32,48},{48,32},{1,17},{17,1},{33,49},{49,33},{2,18}... | collective-permute-start | bytes 344072 | tf_op jit(solution)/shard_map/ppermute | solution.py:21
  80.8 9.4 %collective-permute-start.23 = (f32[8,4,8,128]{3,2,1,0:T(8,128)}, f32[8,4,8,128]{3,2,1,0:T(8,128)S(1)}, u32[]{:S(2)}, u32[]{:S(2)}) collective-permute-start(f32[8,4,8,128]{3,2,1,0:T(8,128)} %get-tuple-element.77.refs_8_), channel_id=1, source_target_pairs={{0,3},{1,2},{2,1},{3,0},{4,7},{5,6},{6,5},{7,4},{8,11},{9,10},{10,... | collective-permute-start | bytes 393224 | tf_op jit(solution)/shard_map/ppermute | solution.py:21
  83.1 7.1 %collective-permute-start.22 = (f32[8,4,8,128]{3,2,1,0:T(8,128)}, f32[8,4,8,128]{3,2,1,0:T(8,128)S(1)}, u32[]{:S(2)}, u32[]{:S(2)}) collective-permute-start(f32[8,4,8,128]{3,2,1,0:T(8,128)} %get-tuple-element.77.refs_8_), channel_id=1, source_target_pairs={{0,2},{1,3},{2,0},{3,1},{4,6},{5,7},{6,4},{7,5},{8,10},{9,11},{10,... | collective-permute-start | bytes 393224 | tf_op jit(solution)/shard_map/ppermute | solution.py:21
  84.2 6.5 %collective-permute-start.20 = (f32[4,7,8,128]{3,2,1,0:T(8,128)S(1)}, f32[4,7,8,128]{3,2,1,0:T(8,128)S(1)}, u32[]{:S(2)}, u32[]{:S(2)}) collective-permute-start(f32[4,7,8,128]{3,2,1,0:T(8,128)S(1)} %collective-permute-done.16.refs_3_), channel_id=1, source_target_pairs={{0,8},{8,0},{1,9},{9,1},{2,10},{10,2},{3,11},{11,3},{4,12},{12,4},... | collective-permute-start | bytes 344072 | tf_op jit(solution)/shard_map/ppermute | solution.py:21
  85.5 5.4 %collective-permute-start.19 = (f32[4,7,8,128]{3,2,1,0:T(8,128)S(1)}, f32[4,7,8,128]{3,2,1,0:T(8,128)S(1)}, u32[]{:S(2)}, u32[]{:S(2)}) collective-permute-start(f32[4,7,8,128]{3,2,1,0:T(8,128)S(1)} %collective-permute-done.15.refs_2_), channel_id=1, source_target_pairs={{0,8},{8,0},{1,9},{9,1},{2,10},{10,2},{3,11},{11,3},{4,12},{12,4},... | collective-permute-start | bytes 344072 | tf_op jit(solution)/shard_map/ppermute | solution.py:21
  86.6 4.7 %collective-permute-start.18 = (f32[4,7,8,128]{3,2,1,0:T(8,128)S(1)}, f32[4,7,8,128]{3,2,1,0:T(8,128)S(1)}, u32[]{:S(2)}, u32[]{:S(2)}) collective-permute-start(f32[4,7,8,128]{3,2,1,0:T(8,128)S(1)} %collective-permute-done.14.refs_1_), channel_id=1, source_target_pairs={{0,8},{8,0},{1,9},{9,1},{2,10},{10,2},{3,11},{11,3},{4,12},{12,4},... | collective-permute-start | bytes 344072 | tf_op jit(solution)/shard_map/ppermute | solution.py:21
  90.2 11.0 %collective-permute-start.24 = (bf16[896,128]{1,0:T(8,128)(2,1)S(1)}, bf16[896,128]{1,0:T(8,128)(2,1)S(1)}, u32[]{:S(2)}, u32[]{:S(2)}) collective-permute-start(bf16[896,128]{1,0:T(8,128)(2,1)S(1)} %collective-permute-done.2.refs_16_.refs_9_), channel_id=1, source_target_pairs={{0,8},{8,0},{1,9},{9,1},{2,10},{10,2},{3,11},{11,3},{4,12},{12,4},... | collective-permute-start | bytes 688136 | tf_op jit(solution)/shard_map/ppermute | solution.py:21
  90.2 11.0 %collective-permute-start.25 = (bf16[896,128]{1,0:T(8,128)(2,1)S(1)}, bf16[896,128]{1,0:T(8,128)(2,1)S(1)}, u32[]{:S(2)}, u32[]{:S(2)}) collective-permute-start(bf16[896,128]{1,0:T(8,128)(2,1)S(1)} %collective-permute-done.11.refs_17_.refs_10_), channel_id=1, source_target_pairs={{0,8},{8,0},{1,9},{9,1},{2,10},{10,2},{3,11},{11,3},{4,12},{12,4},... | collective-permute-start | bytes 688136 | tf_op jit(solution)/shard_map/ppermute | solution.py:21
  90.7 10.5 %collective-permute-start.26 = (bf16[896,128]{1,0:T(8,128)(2,1)S(1)}, bf16[896,128]{1,0:T(8,128)(2,1)S(1)}, u32[]{:S(2)}, u32[]{:S(2)}) collective-permute-start(bf16[896,128]{1,0:T(8,128)(2,1)S(1)} %collective-permute-done.12.refs_18_.refs_11_), channel_id=1, source_target_pairs={{0,8},{8,0},{1,9},{9,1},{2,10},{10,2},{3,11},{11,3},{4,12},{12,4},... | collective-permute-start | bytes 688136 | tf_op jit(solution)/shard_map/ppermute | solution.py:21
  90.8 10.4 %collective-permute-start.27 = (bf16[896,128]{1,0:T(8,128)(2,1)S(1)}, bf16[896,128]{1,0:T(8,128)(2,1)S(1)}, u32[]{:S(2)}, u32[]{:S(2)}) collective-permute-start(bf16[896,128]{1,0:T(8,128)(2,1)S(1)} %collective-permute-done.13.refs_19_.refs_12_), channel_id=1, source_target_pairs={{0,8},{8,0},{1,9},{9,1},{2,10},{10,2},{3,11},{11,3},{4,12},{12,4},... | collective-permute-start | bytes 688136 | tf_op jit(solution)/shard_map/ppermute | solution.py:21
  91.3 5.7 %collective-permute-start.21 = (f32[8,4,8,128]{3,2,1,0:T(8,128)}, f32[8,4,8,128]{3,2,1,0:T(8,128)S(1)}, u32[]{:S(2)}, u32[]{:S(2)}) collective-permute-start(f32[8,4,8,128]{3,2,1,0:T(8,128)} %get-tuple-element.77.refs_8_), channel_id=1, source_target_pairs={{0,1},{1,0},{2,3},{3,2},{4,5},{5,4},{6,7},{7,6},{8,9},{9,8},{10,11... | collective-permute-start | bytes 393224 | tf_op jit(solution)/shard_map/ppermute | solution.py:21
  97.0 15.9 %collective-permute-start.28 = (f32[4,16,896]{2,1,0:T(8,128)}, f32[4,16,896]{2,1,0:T(8,128)S(1)}, u32[]{:S(2)}, u32[]{:S(2)}) collective-permute-start(f32[4,16,896]{2,1,0:T(8,128)} %get-tuple-element.84), channel_id=1, source_target_pairs={{0,4},{4,0},{1,5},{5,1},{2,6},{6,2},{3,7},{7,3},{8,12},{12,8},{9,1... | collective-permute-start | bytes 688136 | tf_op jit(solution)/shard_map/ppermute | solution.py:21
  112.8 25.1 %all-to-all-start.3 = ((bf16[32,32,256]{2,1,0:T(8,128)(2,1)}), bf16[32,32,256]{2,1,0:T(8,128)(2,1)S(1)}, u32[]{:S(2)}, u32[]{:S(2)}) async-start(bf16[32,32,256]{2,1,0:T(8,128)(2,1)} %get-tuple-element.96.refs_0_), calls=%async_computation.3 | async-start | bytes 1048576 | tf_op jit(solution)/shard_map/all_to_all | solution.py:439
  123.2 10.5 %collective-permute-start.29 = (f32[2,16,896]{2,1,0:T(8,128)}, f32[2,16,896]{2,1,0:T(8,128)S(1)}, u32[]{:S(2)}, u32[]{:S(2)}) collective-permute-start(f32[2,16,896]{2,1,0:T(8,128)} %get-tuple-element.88), channel_id=1, source_target_pairs={{0,1},{1,0},{2,3},{3,2},{4,5},{5,4},{6,7},{7,6},{8,9},{9,8},{10,11... | collective-permute-start | bytes 344072 | tf_op jit(solution)/shard_map/ppermute | solution.py:21
  123.8 10.0 %collective-permute-start.30 = (f32[2,16,896]{2,1,0:T(8,128)}, f32[2,16,896]{2,1,0:T(8,128)S(1)}, u32[]{:S(2)}, u32[]{:S(2)}) collective-permute-start(f32[2,16,896]{2,1,0:T(8,128)} %get-tuple-element.89), channel_id=1, source_target_pairs={{0,2},{1,3},{2,0},{3,1},{4,6},{5,7},{6,4},{7,5},{8,10},{9,11},{10,... | collective-permute-start | bytes 344072 | tf_op jit(solution)/shard_map/ppermute | solution.py:21
  126.9 6.9 %collective-permute-start.31 = (f32[2,16,896]{2,1,0:T(8,128)}, f32[2,16,896]{2,1,0:T(8,128)S(1)}, u32[]{:S(2)}, u32[]{:S(2)}) collective-permute-start(f32[2,16,896]{2,1,0:T(8,128)} %get-tuple-element.90), channel_id=1, source_target_pairs={{0,3},{1,2},{2,1},{3,0},{4,7},{5,6},{6,5},{7,4},{8,11},{9,10},{10,... | collective-permute-start | bytes 344072 | tf_op jit(solution)/shard_map/ppermute | solution.py:21
  137.9 17.0 %all-to-all-start.4 = ((f32[16,8,896]{2,1,0:T(8,128)}), f32[16,8,896]{2,1,0:T(8,128)S(1)}, u32[]{:S(2)}, u32[]{:S(2)}) async-start(f32[16,8,896]{2,1,0:T(8,128)} %back.1), calls=%async_computation.4 | async-start | bytes 917504 | tf_op jit(solution)/shard_map/all_to_all | solution.py:446
  142.8 24.9 %collective-permute-start.38 = (bf16[32,32,256]{2,1,0:T(8,128)(2,1)S(1)}, bf16[32,32,256]{2,1,0:T(8,128)(2,1)S(1)}, u32[]{:S(2)}, u32[]{:S(2)}) collective-permute-start(bf16[32,32,256]{2,1,0:T(8,128)(2,1)S(1)} %all-to-all-done.3.refs_0_), channel_id=1, source_target_pairs={{0,3},{1,2},{2,1},{3,0},{4,7},{5,6},{6,5},{7,4},{8,11},{9,10},{10,... | collective-permute-start | bytes 1572872 | tf_op jit(solution)/shard_map/ppermute | solution.py:21
  145.0 22.7 %collective-permute-start.37 = (bf16[32,32,256]{2,1,0:T(8,128)(2,1)S(1)}, bf16[32,32,256]{2,1,0:T(8,128)(2,1)S(1)}, u32[]{:S(2)}, u32[]{:S(2)}) collective-permute-start(bf16[32,32,256]{2,1,0:T(8,128)(2,1)S(1)} %all-to-all-done.3.refs_0_), channel_id=1, source_target_pairs={{0,2},{1,3},{2,0},{3,1},{4,6},{5,7},{6,4},{7,5},{8,10},{9,11},{10,... | collective-permute-start | bytes 1572872 | tf_op jit(solution)/shard_map/ppermute | solution.py:21
  145.8 22.5 %collective-permute-start.36 = (bf16[32,32,256]{2,1,0:T(8,128)(2,1)S(1)}, bf16[32,32,256]{2,1,0:T(8,128)(2,1)S(1)}, u32[]{:S(2)}, u32[]{:S(2)}) collective-permute-start(bf16[32,32,256]{2,1,0:T(8,128)(2,1)S(1)} %all-to-all-done.3.refs_0_), channel_id=1, source_target_pairs={{0,1},{1,0},{2,3},{3,2},{4,5},{5,4},{6,7},{7,6},{8,9},{9,8},{10,11... | collective-permute-start | bytes 1572872 | tf_op jit(solution)/shard_map/ppermute | solution.py:21
  146.9 1.3 collective-permute-start.32
  146.9 1.5 collective-permute-start.33
  148.2 1.3 collective-permute-start.34
  148.4 1.3 collective-permute-start.35
  157.4 19.0 %all-to-all-start.5 = ((f32[8,8,128]{2,1,0:T(8,128)}), f32[8,8,128]{2,1,0:T(8,128)S(1)}, u32[]{:S(2)}, u32[]{:S(2)}) async-start(f32[8,8,128]{2,1,0:T(8,128)} %total.1), calls=%async_computation.5 | async-start | bytes 65536 | tf_op jit(solution)/shard_map/all_to_all | solution.py:448
  (42 other events, 382.2 us)

commit v5 on v4

--- a/solution.py
+++ b/solution.py
@@ -29,13 +29,13 @@
     return lax.optimization_barrier((value, other))[0]
 
 
-def params(mib=56):
+def params(mib):
     return pltpu.CompilerParams(vmem_limit_bytes=mib * MIB)
 
 
 SMEM = pl.BlockSpec(memory_space=pltpu.SMEM)
 VMEM = pl.BlockSpec(memory_space=pltpu.VMEM)
-HBM = pl.BlockSpec(memory_space=pltpu.HBM)
+HBM = pl.BlockSpec(memory_space=pl.ANY)
 
 
 def part_kernel(x_ref, x_other_ref, gate_ref, up_ref, theirs_ref, width_ref, gains_ref, target_ref, out_ref, gain_ref):
@@ -72,7 +72,7 @@
             jax.ShapeDtypeStruct((16, 2 * lanes + 3, 8, 128), F32),
             jax.ShapeDtypeStruct(gains.shape, F32),
         ],
-        compiler_params=params(),
+        compiler_params=params(56),
         name="part",
     )(x, x_other, gate, up, theirs, widths, gains, targets)
 
@@ -114,7 +114,7 @@
         out_specs=VMEM,
         out_shape=jax.ShapeDtypeStruct((8, lanes + 6, 8, 128), F32),
         scratch_shapes=[pltpu.VMEM(part.shape, F32), pltpu.SemaphoreType.DMA((16,))],
-        compiler_params=params(),
+        compiler_params=params(8),
         name="sum_x",
     )(part)
 
@@ -152,7 +152,7 @@
             jax.ShapeDtypeStruct((2, 16, 256), F32),
             jax.ShapeDtypeStruct((8, 4, 8, 128), F32),
         ],
-        compiler_params=params(),
+        compiler_params=params(6),
         name="raw",
     )(mine, other)
 
@@ -178,7 +178,7 @@
         out_specs=[VMEM] * 2,
         out_shape=[jax.ShapeDtypeStruct((4, 16, lanes * 128), F32)] * 2,
         scratch_shapes=[pltpu.VMEM((2, 16, lanes, 8, 128), F32)],
-        compiler_params=params(),
+        compiler_params=params(8),
         name="extract",
     )(*raws, *others)
 
@@ -251,7 +251,7 @@
             pltpu.SemaphoreType.DMA((8,)),
             pltpu.SemaphoreType.DMA((8,)),
         ],
-        compiler_params=params(),
+        compiler_params=params(56),
         cost_estimate=pl.CostEstimate(flops=2 * 512 * 8 * width * 256, bytes_accessed=6 * MIB, transcendentals=0),
         name="output",
     )(*raws, *others, *gains, *mine, *theirs, target)
@@ -278,7 +278,7 @@
         in_specs=[VMEM] * 21,
         out_specs=VMEM,
         out_shape=jax.ShapeDtypeStruct((16, 8, width), F32),
-        compiler_params=params(),
+        compiler_params=params(56),
         cost_estimate=pl.CostEstimate(flops=2 * 512 * 8 * width * 256, bytes_accessed=6 * MIB, transcendentals=0),
         name="back",
     )(res, *owns, *mine, *theirs)
@@ -302,7 +302,7 @@
         in_specs=[VMEM],
         out_specs=VMEM,
         out_shape=jax.ShapeDtypeStruct((8, 8, 128), F32),
-        compiler_params=params(),
+        compiler_params=params(6),
         name="total",
     )(part)
 
@@ -319,7 +319,7 @@
         in_specs=[VMEM] * 2,
         out_specs=[VMEM] * 4,
         out_shape=[jax.ShapeDtypeStruct((2,) + near.shape[1:], F32)] * 4,
-        compiler_params=params(),
+        compiler_params=params(6),
         name="pair",
     )(near, far)
 
@@ -345,7 +345,7 @@
         out_specs=VMEM,
         out_shape=jax.ShapeDtypeStruct((width, 256), BF16),
         scratch_shapes=[pltpu.VMEM((256, width), BF16)],
-        compiler_params=params(),
+        compiler_params=params(8),
         name="hidden",
     )(gain, *mine, *others)
 
@@ -392,7 +392,7 @@
         out_specs=pl.BlockSpec((1, width, some * feats), lambda s: (0, 0, s)),
         out_shape=jax.ShapeDtypeStruct((1, width, blocks * feats), BF16),
         scratch_shapes=[pltpu.VMEM((4, pieces, rows, feats), BF16), pltpu.SemaphoreType.DMA((blocks // some, 8))],
-        compiler_params=params(),
+        compiler_params=params(22),
         cost_estimate=pl.CostEstimate(
             flops=40 * 8 * rows * width * blocks * feats, bytes_accessed=10 * MIB, transcendentals=0
         ),

time: 178 us -> 173 us (0.972)
  waiting for transfers between devices: 45.8 us -> 54.9 us
  Pallas kernels: 36.4 us -> 27.9 us
  local copies, waits for them, and re-layouts: 7.02 us -> 2.06 us
    unnamed x93 -> x65, local copies, waits for them, and re-layouts: 7.02 us -> 2.06 us
    ppermute x39, waiting for transfers between devices: 35.4 us -> 39.9 us  [swap(): return lax.ppermute(value, axis, [(i, i ^ mask) for i in range(SIZE[axis])])]
    all_to_all x1, waiting for transfers between devices: 2.37 us -> 5.04 us  [local(): sums = lax.all_to_all(sums, ('zl', 'x'), 0, 0, tiled=True)]
    pallas_call x1, Pallas kernels: 2.22 us -> 0.19 us  [hidden_call(): pl.pallas_call(hidden_kernel, in_specs=[VMEM] * 9, out_specs=VMEM, out_sh...]
    pallas_call x1, Pallas kernels: 2.33 us -> 0.32 us  [extract_call(): pl.pallas_call(extract_kernel, in_specs=[VMEM] * 8, out_specs=[VMEM] * 2,...]
    all_to_all x1, waiting for transfers between devices: 4.14 us -> 6.04 us  [local(): lax.all_to_all(after(res, far), ('zh', 'zl', 'x'), 0, 0, tiled=True)]
    pallas_call x1, Pallas kernels: 1.9 us -> 0.03 us  [raw_call(): pl.pallas_call(raw_kernel, in_specs=[VMEM, VMEM], out_specs=[VMEM] * 3, o...]
    pallas_call x1, Pallas kernels: 1.84 us -> 0.03 us  [pair_call(): pl.pallas_call(pair_kernel, in_specs=[VMEM] * 2, out_specs=[VMEM] * 4, ou...]
  transfers between devices with their start and end apart: 44 -> 44, of which waited for: 21 -> 21; matrix products, arithmetic and copies ran while one was open for 0% -> 0% of each run, Pallas kernels for 17% -> 13%
where the time goes in v5:
time: 173 us; the launch traced here: 172 us
  starting transfers between devices  75 us (43%)
  waiting for transfers between devices  54.9 us (32%)
  Pallas kernels  27.9 us (16%)
  blocking collectives  8.9 us (5%)
  local copies, waits for them, and re-layouts  2.06 us (1%)
  between operations  1.73 us (1%)
    ppermute x39, waiting for transfers between devices, swap(): return lax.ppermute(value, axis, [(i, i ^ mask) for i in range(SIZE[axis])])  39.9 us
    ppermute x39, starting transfers between devices, swap(): return lax.ppermute(value, axis, [(i, i ^ mask) for i in range(SIZE[axis])])  39.7 us
    pallas_call x1, Pallas kernels, output_call(): pl.pallas_call(output_kernel, in_specs=[HBM] * 28 + [VMEM], out_specs=[VM...  9 us
    all_to_all x1, blocking collectives, local(): raw = lax.all_to_all(raw, 'zl', 0, 0, tiled=True)  8.9 us
    all_to_all x1, starting transfers between devices, local(): part = lax.all_to_all(part, ('zh', 'zl'), 0, 0, tiled=True)  8.48 us
    all_to_all x1, starting transfers between devices, local(): lax.all_to_all(after(res, far), ('zh', 'zl', 'x'), 0, 0, tiled=True)  8.41 us
    all_to_all x1, starting transfers between devices, local(): part = lax.all_to_all(part, ('x', 'y'), 0, 0, tiled=True)  7.61 us
    pallas_call x1, Pallas kernels, grad_call(): pl.pallas_call(functools.partial(grad_kernel, scale), grid=(blocks // som...  6.75 us
  transfers between devices with their start and end apart: 44, of which 21 were waited for; matrix products, arithmetic and copies ran while one was open for 0% of the time, Pallas kernels for 13%

profile of v5, /device:TPU:2, one launch (start us, length us, event | category | flops | bytes accessed | tf_op | source)
XLA Modules:
  0.0 172.1 jit_solution(247877691984964468)
XLA Ops:
  0.6 1.0 broadcast_select_fusion
  4.1 0.7 copy-done.11
  4.8 2.6 %part.1 = (f32[16,17,8,128]{3,2,1,0:T(8,128)}, f32[1,896]{1,0:T(1,128)}) custom-call(bf16[128,256]{1,0:T(8,128)(2,1)} %x_ref.1, bf16[128,256]{1,0:T(8,128)(2,1)} %copy-done.12, bf16[128,896]{1,0:T(8,128)(2,1)} %gate_ref.1, bf16[128,896]{1,0:T(8,128)(2,1)} %up_ref.1, bf16[128,896]{1,0:T(8,128)(2,1)} %copy-done.11, s32[1]{0:T(128)} %copy.11.width_ref, ...), custom_call_target="tpu_custom_call" | custom-call | tf_op jit(solution)/shard_map/part/pallas_call | solution.py:67
  7.4 7.6 %all-to-all-start = ((f32[16,17,8,128]{3,2,1,0:T(8,128)}), f32[16,17,8,128]{3,2,1,0:T(8,128)S(1)}, u32[]{:S(2)}, u32[]{:S(2)}) async-start(f32[16,17,8,128]{3,2,1,0:T(8,128)} %get-tuple-element.54), calls=%async_computation | async-start | bytes 2228224 | tf_op jit(solution)/shard_map/all_to_all | solution.py:414
  15.0 7.3 %collective-permute-start.2 = (bf16[896,128]{1,0:T(8,128)(2,1)S(1)}, bf16[896,128]{1,0:T(8,128)(2,1)S(1)}, u32[]{:S(2)}, u32[]{:S(2)}) collective-permute-start(bf16[896,128]{1,0:T(8,128)(2,1)S(1)} %copy-done.13), channel_id=1, source_target_pairs={{0,4},{4,0},{1,5},{5,1},{2,6},{6,2},{3,7},{7,3},{8,12},{12,8},{9,1... | collective-permute-start | bytes 688136 | tf_op jit(solution)/shard_map/ppermute | solution.py:21
  22.3 6.5 %collective-permute-done.2.refs_16_.refs_9_ = bf16[896,128]{1,0:T(8,128)(2,1)S(1)} collective-permute-done((bf16[896,128]{1,0:T(8,128)(2,1)S(1)}, bf16[896,128]{1,0:T(8,128)(2,1)S(1)}, u32[]{:S(2)}, u32[]{:S(2)}) %collective-permute-start.2) | collective-permute-done | bytes 229408 | tf_op jit(solution)/shard_map/ppermute | solution.py:21
  28.8 2.3 %all-to-all-done.part_ref = f32[16,17,8,128]{3,2,1,0:T(8,128)S(1)} async-done(((f32[16,17,8,128]{3,2,1,0:T(8,128)}), f32[16,17,8,128]{3,2,1,0:T(8,128)S(1)}, u32[]{:S(2)}, u32[]{:S(2)}) %all-to-all-start) | async-done | bytes 1114144 | tf_op jit(solution)/shard_map/all_to_all | solution.py:414
  31.2 2.5 %sum_x.1 = f32[8,13,8,128]{3,2,1,0:T(8,128)} custom-call(f32[16,17,8,128]{3,2,1,0:T(8,128)S(1)} %all-to-all-done.part_ref), custom_call_target="tpu_custom_call" | custom-call | tf_op jit(solution)/shard_map/sum_x/pallas_call | solution.py:111
  33.7 8.5 %all-to-all-start.1 = ((f32[8,13,8,128]{3,2,1,0:T(8,128)}), f32[8,13,8,128]{3,2,1,0:T(8,128)S(1)}, u32[]{:S(2)}, u32[]{:S(2)}) async-start(f32[8,13,8,128]{3,2,1,0:T(8,128)} %sum_x.1), calls=%async_computation.1 | async-start | bytes 851968 | tf_op jit(solution)/shard_map/all_to_all | solution.py:418
  42.1 2.1 %collective-permute-start.5 = (bf16[896,128]{1,0:T(8,128)(2,1)S(1)}, bf16[896,128]{1,0:T(8,128)(2,1)S(1)}, u32[]{:S(2)}, u32[]{:S(2)}) collective-permute-start(bf16[896,128]{1,0:T(8,128)(2,1)S(1)} %copy-done.13), channel_id=1, source_target_pairs={{0,3},{1,2},{2,1},{3,0},{4,7},{5,6},{6,5},{7,4},{8,11},{9,10},{10,... | collective-permute-start | bytes 688136 | tf_op jit(solution)/shard_map/ppermute | solution.py:21
  44.3 0.9 collective-permute-start.4
  45.1 1.1 collective-permute-start.3
  46.2 7.7 %collective-permute-done.5.refs_15_.refs_8_ = bf16[896,128]{1,0:T(8,128)(2,1)S(1)} collective-permute-done((bf16[896,128]{1,0:T(8,128)(2,1)S(1)}, bf16[896,128]{1,0:T(8,128)(2,1)S(1)}, u32[]{:S(2)}, u32[]{:S(2)}) %collective-permute-start.5) | collective-permute-done | bytes 229408 | tf_op jit(solution)/shard_map/ppermute | solution.py:21
  54.6 1.6 all-to-all-done.1.mine_ref
  56.2 1.8 %collective-permute-done.6.other_ref = f32[8,13,8,128]{3,2,1,0:T(8,128)S(1)} collective-permute-done((f32[8,13,8,128]{3,2,1,0:T(8,128)S(1)}, f32[8,13,8,128]{3,2,1,0:T(8,128)S(1)}, u32[]{:S(2)}, u32[]{:S(2)}) %collective-permute-start.6) | collective-permute-done | bytes 426016 | tf_op jit(solution)/shard_map/ppermute | solution.py:21
  59.1 2.2 %collective-permute-start.13 = (bf16[896,128]{1,0:T(8,128)(2,1)S(1)}, bf16[896,128]{1,0:T(8,128)(2,1)S(1)}, u32[]{:S(2)}, u32[]{:S(2)}) collective-permute-start(bf16[896,128]{1,0:T(8,128)(2,1)S(1)} %collective-permute-done.2.refs_16_.refs_9_), channel_id=1, source_target_pairs={{0,3},{1,2},{2,1},{3,0},{4,7},{5,6},{6,5},{7,4},{8,11},{9,10},{10,... | collective-permute-start | bytes 688136 | tf_op jit(solution)/shard_map/ppermute | solution.py:21
  61.3 0.9 collective-permute-start.12
  62.2 1.0 collective-permute-start.11
  63.2 8.9 %all_to_all.30.refs_0_ = f32[4,7,8,128]{3,2,1,0:T(8,128)S(1)} all-to-all(f32[4,7,8,128]{3,2,1,0:T(8,128)S(1)} %get-tuple-element.59), channel_id=1, replica_groups=mesh['zl'=4,'x'=4,'core'=2,'zh'=2,'y'=4] {'zl'}, dimensions={0} | all-to-all | bytes 229376 | tf_op jit(solution)/shard_map/all_to_all | solution.py:423
  72.1 0.7 collective-permute-done.13.refs_19_.refs_12_
  73.5 1.3 collective-permute-start.16
  74.8 2.6 %collective-permute-start.15 = (f32[4,7,8,128]{3,2,1,0:T(8,128)S(1)}, f32[4,7,8,128]{3,2,1,0:T(8,128)S(1)}, u32[]{:S(2)}, u32[]{:S(2)}) collective-permute-start(f32[4,7,8,128]{3,2,1,0:T(8,128)S(1)} %all_to_all.30.refs_0_), channel_id=1, source_target_pairs={{0,32},{16,48},{32,0},{48,16},{1,33},{17,49},{33,1},{49,17},{2,34}... | collective-permute-start | bytes 344072 | tf_op jit(solution)/shard_map/ppermute | solution.py:21
  77.6 2.2 %collective-permute-start.23 = (f32[8,4,8,128]{3,2,1,0:T(8,128)S(1)}, f32[8,4,8,128]{3,2,1,0:T(8,128)S(1)}, u32[]{:S(2)}, u32[]{:S(2)}) collective-permute-start(f32[8,4,8,128]{3,2,1,0:T(8,128)S(1)} %get-tuple-element.77.refs_8_), channel_id=1, source_target_pairs={{0,3},{1,2},{2,1},{3,0},{4,7},{5,6},{6,5},{7,4},{8,11},{9,10},{10,... | collective-permute-start | bytes 393224 | tf_op jit(solution)/shard_map/ppermute | solution.py:21
  79.8 1.2 collective-permute-start.22
  81.0 1.2 collective-permute-done.15.refs_2_
  82.2 1.1 collective-permute-done.14.refs_1_
  83.4 3.4 %collective-permute-done.23.refs_11_ = f32[8,4,8,128]{3,2,1,0:T(8,128)S(1)} collective-permute-done((f32[8,4,8,128]{3,2,1,0:T(8,128)S(1)}, f32[8,4,8,128]{3,2,1,0:T(8,128)S(1)}, u32[]{:S(2)}, u32[]{:S(2)}) %collective-permute-start.23) | collective-permute-done | bytes 131104 | tf_op jit(solution)/shard_map/ppermute | solution.py:21
  88.2 5.1 %collective-permute-done.21.refs_9_ = f32[8,4,8,128]{3,2,1,0:T(8,128)S(1)} collective-permute-done((f32[8,4,8,128]{3,2,1,0:T(8,128)S(1)}, f32[8,4,8,128]{3,2,1,0:T(8,128)S(1)}, u32[]{:S(2)}, u32[]{:S(2)}) %collective-permute-start.21) | collective-permute-done | bytes 131104 | tf_op jit(solution)/shard_map/ppermute | solution.py:21
  93.3 4.1 %collective-permute-start.28 = (f32[4,16,896]{2,1,0:T(8,128)S(1)}, f32[4,16,896]{2,1,0:T(8,128)S(1)}, u32[]{:S(2)}, u32[]{:S(2)}) collective-permute-start(f32[4,16,896]{2,1,0:T(8,128)S(1)} %get-tuple-element.84), channel_id=1, source_target_pairs={{0,4},{4,0},{1,5},{5,1},{2,6},{6,2},{3,7},{7,3},{8,12},{12,8},{9,1... | collective-permute-start | bytes 688136 | tf_op jit(solution)/shard_map/ppermute | solution.py:21
  98.4 9.0 %output.1 = (bf16[32,32,256]{2,1,0:T(8,128)(2,1)}, f32[2,2,16,896]{3,2,1,0:T(8,128)}, f32[2,2,16,896]{3,2,1,0:T(8,128)}, f32[2,2,16,896]{3,2,1,0:T(8,128)}, f32[2,2,16,896]{3,2,1,0:T(8,128)}) custom-call(f32[4,7,8,128]{3,2,1,0:T(8,128)} %copy-done, f32[4,7,8,128]{3,2,1,0:T(8,128)} %copy-done.4, f32[4,7,8,128]{3,2,1,0:T(8,128)} %copy-done.3, ...), custom_call_target="tpu_custom_call" | custom-call | flops 1879048192 | bytes 6291456 | tf_op jit(solution)/shard_map/output/pallas_call | solution.py:237
  107.4 1.6 collective-permute-done.28.far_ref
  109.0 8.4 %all-to-all-start.3 = ((bf16[32,32,256]{2,1,0:T(8,128)(2,1)}), bf16[32,32,256]{2,1,0:T(8,128)(2,1)S(1)}, u32[]{:S(2)}, u32[]{:S(2)}) async-start(bf16[32,32,256]{2,1,0:T(8,128)(2,1)} %get-tuple-element.96.refs_0_), calls=%async_computation.3 | async-start | bytes 1048576 | tf_op jit(solution)/shard_map/all_to_all | solution.py:439
  117.4 0.7 collective-permute-start.29
  118.1 3.1 %collective-permute-start.30 = (f32[2,16,896]{2,1,0:T(8,128)S(1)}, f32[2,16,896]{2,1,0:T(8,128)S(1)}, u32[]{:S(2)}, u32[]{:S(2)}) collective-permute-start(f32[2,16,896]{2,1,0:T(8,128)S(1)} %get-tuple-element.89), channel_id=1, source_target_pairs={{0,2},{1,3},{2,0},{3,1},{4,6},{5,7},{6,4},{7,5},{8,10},{9,11},{10,... | collective-permute-start | bytes 344072 | tf_op jit(solution)/shard_map/ppermute | solution.py:21
  121.2 1.0 collective-permute-start.31
  122.2 5.9 %back.1 = f32[16,8,896]{2,1,0:T(8,128)} custom-call(bf16[32,32,256]{2,1,0:T(8,128)(2,1)} %get-tuple-element.96.refs_0_, f32[2,2,16,896]{3,2,1,0:T(8,128)} %get-tuple-element.92.refs_1_, f32[2,2,16,896]{3,2,1,0:T(8,128)} %get-tuple-element.93.refs_2_, f32[2,2,16,896]{3,2,1,0:T(8,128)} %get-tuple-element.94.refs_3_, ...), custom_call_target="tpu_custom_call" | custom-call | flops 1879048192 | bytes 6291456 | tf_op jit(solution)/shard_map/back/pallas_call | solution.py:276
  128.1 6.0 %all-to-all-done.3.refs_0_ = bf16[32,32,256]{2,1,0:T(8,128)(2,1)S(1)} async-done(((bf16[32,32,256]{2,1,0:T(8,128)(2,1)}), bf16[32,32,256]{2,1,0:T(8,128)(2,1)S(1)}, u32[]{:S(2)}, u32[]{:S(2)}) %all-to-all-start.3) | async-done | bytes 524320 | tf_op jit(solution)/shard_map/all_to_all | solution.py:439
  134.1 4.8 %all-to-all-start.4 = ((f32[16,8,896]{2,1,0:T(8,128)}), f32[16,8,896]{2,1,0:T(8,128)S(1)}, u32[]{:S(2)}, u32[]{:S(2)}) async-start(f32[16,8,896]{2,1,0:T(8,128)} %back.1), calls=%async_computation.4 | async-start | bytes 917504 | tf_op jit(solution)/shard_map/all_to_all | solution.py:446
  139.0 2.2 %collective-permute-start.38 = (bf16[32,32,256]{2,1,0:T(8,128)(2,1)S(1)}, bf16[32,32,256]{2,1,0:T(8,128)(2,1)S(1)}, u32[]{:S(2)}, u32[]{:S(2)}) collective-permute-start(bf16[32,32,256]{2,1,0:T(8,128)(2,1)S(1)} %all-to-all-done.3.refs_0_), channel_id=1, source_target_pairs={{0,3},{1,2},{2,1},{3,0},{4,7},{5,6},{6,5},{7,4},{8,11},{9,10},{10,... | collective-permute-start | bytes 1572872 | tf_op jit(solution)/shard_map/ppermute | solution.py:21
  141.9 1.2 collective-permute-start.36
  143.6 0.8 collective-permute-done.32.refs_4_
  144.9 0.8 collective-permute-done.34.refs_6_
  146.1 5.0 %all-to-all-done.4.part_ref = f32[16,8,896]{2,1,0:T(8,128)S(1)} async-done(((f32[16,8,896]{2,1,0:T(8,128)}), f32[16,8,896]{2,1,0:T(8,128)S(1)}, u32[]{:S(2)}, u32[]{:S(2)}) %all-to-all-start.4) | async-done | bytes 458784 | tf_op jit(solution)/shard_map/all_to_all | solution.py:446
  151.1 0.6 total.1
  151.8 6.0 %all-to-all-start.5 = ((f32[8,8,128]{2,1,0:T(8,128)}), f32[8,8,128]{2,1,0:T(8,128)S(1)}, u32[]{:S(2)}, u32[]{:S(2)}) async-start(f32[8,8,128]{2,1,0:T(8,128)} %total.1), calls=%async_computation.5 | async-start | bytes 65536 | tf_op jit(solution)/shard_map/all_to_all | solution.py:448
  157.7 6.2 %collective-permute-done.38.refs_3_ = bf16[32,32,256]{2,1,0:T(8,128)(2,1)S(1)} collective-permute-done((bf16[32,32,256]{2,1,0:T(8,128)(2,1)S(1)}, bf16[32,32,256]{2,1,0:T(8,128)(2,1)S(1)}, u32[]{:S(2)}, u32[]{:S(2)}) %collective-permute-start.38) | collective-permute-done | bytes 524320 | tf_op jit(solution)/shard_map/ppermute | solution.py:21
  163.9 0.8 collective-permute-done.36.refs_1_
  164.7 6.8 %grad.1 = bf16[1,896,4096]{2,1,0:T(8,128)(2,1)} custom-call(bf16[896,256]{1,0:T(8,128)(2,1)S(1)} %hidden.1.hidden_ref, bf16[32,32,256]{2,1,0:T(8,128)(2,1)S(1)} %all-to-all-done.3.refs_0_, bf16[32,32,256]{2,1,0:T(8,128)(2,1)} %collective-permute-done.36.refs_1_, bf16[32,32,256]{2,1,0:T(8,128)(2,1)S(1)} %collective-permute-done.37.refs_2_, ...), custom_call_target="tpu_custom_call" | custom-call | flops 37580963840 | bytes 10485760 | tf_op jit(solution)/shard_map/grad/pallas_call | solution.py:388
  (119 shorter events, 9.3 us)
Async XLA Ops:
  1.6 1.9 %collective-permute-start.1 = (bf16[128,896]{1,0:T(8,128)(2,1)S(1)}, bf16[128,896]{1,0:T(8,128)(2,1)S(1)}, u32[]{:S(2)}, u32[]{:S(2)}) collective-permute-start(bf16[128,896]{1,0:T(8,128)(2,1)S(1)} %broadcast_select_fusion), channel_id=1, source_target_pairs={{0,8},{8,0},{1,9},{9,1},{2,10},{10,2},{3,11},{11,3},{4,12},{12,4},... | collective-permute-start | bytes 688136 | tf_op jit(solution)/shard_map/ppermute | solution.py:21
  1.7 1.8 %collective-permute-start = (bf16[128,256]{1,0:T(8,128)(2,1)}, bf16[128,256]{1,0:T(8,128)(2,1)S(1)}, u32[]{:S(2)}, u32[]{:S(2)}) collective-permute-start(bf16[128,256]{1,0:T(8,128)(2,1)} %x_ref.1), channel_id=1, source_target_pairs={{0,8},{8,0},{1,9},{9,1},{2,10},{10,2},{3,11},{11,3},{4,12},{12,4},... | collective-permute-start | bytes 196616 | tf_op jit(solution)/shard_map/ppermute | solution.py:21
  7.4 23.8 %all-to-all-start = ((f32[16,17,8,128]{3,2,1,0:T(8,128)}), f32[16,17,8,128]{3,2,1,0:T(8,128)S(1)}, u32[]{:S(2)}, u32[]{:S(2)}) async-start(f32[16,17,8,128]{3,2,1,0:T(8,128)} %get-tuple-element.54), calls=%async_computation | async-start | bytes 2228224 | tf_op jit(solution)/shard_map/all_to_all | solution.py:414
  15.0 13.8 %collective-permute-start.2 = (bf16[896,128]{1,0:T(8,128)(2,1)S(1)}, bf16[896,128]{1,0:T(8,128)(2,1)S(1)}, u32[]{:S(2)}, u32[]{:S(2)}) collective-permute-start(bf16[896,128]{1,0:T(8,128)(2,1)S(1)} %copy-done.13), channel_id=1, source_target_pairs={{0,4},{4,0},{1,5},{5,1},{2,6},{6,2},{3,7},{7,3},{8,12},{12,8},{9,1... | collective-permute-start | bytes 688136 | tf_op jit(solution)/shard_map/ppermute | solution.py:21
  28.8 58.0 %copy-start.14 = (bf16[896,128]{1,0:T(8,128)(2,1)}, bf16[896,128]{1,0:T(8,128)(2,1)S(1)}, u32[]{:S(2)}) copy-start(bf16[896,128]{1,0:T(8,128)(2,1)S(1)} %collective-permute-done.2.refs_16_.refs_9_) | copy-start | bytes 688132
  33.7 22.5 %all-to-all-start.1 = ((f32[8,13,8,128]{3,2,1,0:T(8,128)}), f32[8,13,8,128]{3,2,1,0:T(8,128)S(1)}, u32[]{:S(2)}, u32[]{:S(2)}) async-start(f32[8,13,8,128]{3,2,1,0:T(8,128)} %sum_x.1), calls=%async_computation.1 | async-start | bytes 851968 | tf_op jit(solution)/shard_map/all_to_all | solution.py:418
  42.1 11.8 %collective-permute-start.5 = (bf16[896,128]{1,0:T(8,128)(2,1)S(1)}, bf16[896,128]{1,0:T(8,128)(2,1)S(1)}, u32[]{:S(2)}, u32[]{:S(2)}) collective-permute-start(bf16[896,128]{1,0:T(8,128)(2,1)S(1)} %copy-done.13), channel_id=1, source_target_pairs={{0,3},{1,2},{2,1},{3,0},{4,7},{5,6},{6,5},{7,4},{8,11},{9,10},{10,... | collective-permute-start | bytes 688136 | tf_op jit(solution)/shard_map/ppermute | solution.py:21
  44.3 9.7 %collective-permute-start.4 = (bf16[896,128]{1,0:T(8,128)(2,1)S(1)}, bf16[896,128]{1,0:T(8,128)(2,1)S(1)}, u32[]{:S(2)}, u32[]{:S(2)}) collective-permute-start(bf16[896,128]{1,0:T(8,128)(2,1)S(1)} %copy-done.13), channel_id=1, source_target_pairs={{0,2},{1,3},{2,0},{3,1},{4,6},{5,7},{6,4},{7,5},{8,10},{9,11},{10,... | collective-permute-start | bytes 688136 | tf_op jit(solution)/shard_map/ppermute | solution.py:21
  45.1 9.4 %collective-permute-start.3 = (bf16[896,128]{1,0:T(8,128)(2,1)S(1)}, bf16[896,128]{1,0:T(8,128)(2,1)S(1)}, u32[]{:S(2)}, u32[]{:S(2)}) collective-permute-start(bf16[896,128]{1,0:T(8,128)(2,1)S(1)} %copy-done.13), channel_id=1, source_target_pairs={{0,1},{1,0},{2,3},{3,2},{4,5},{5,4},{6,7},{7,6},{8,9},{9,8},{10,11... | collective-permute-start | bytes 688136 | tf_op jit(solution)/shard_map/ppermute | solution.py:21
  54.0 43.6 %copy-start.15 = (bf16[896,128]{1,0:T(8,128)(2,1)}, bf16[896,128]{1,0:T(8,128)(2,1)S(1)}, u32[]{:S(2)}) copy-start(bf16[896,128]{1,0:T(8,128)(2,1)S(1)} %collective-permute-done.5.refs_15_.refs_8_) | copy-start | bytes 688132
  54.0 43.6 %copy-start.16 = (bf16[896,128]{1,0:T(8,128)(2,1)}, bf16[896,128]{1,0:T(8,128)(2,1)S(1)}, u32[]{:S(2)}) copy-start(bf16[896,128]{1,0:T(8,128)(2,1)S(1)} %collective-permute-done.4.refs_14_.refs_7_) | copy-start | bytes 688132
  54.6 43.0 %copy-start.17 = (bf16[896,128]{1,0:T(8,128)(2,1)}, bf16[896,128]{1,0:T(8,128)(2,1)S(1)}, u32[]{:S(2)}) copy-start(bf16[896,128]{1,0:T(8,128)(2,1)S(1)} %collective-permute-done.3.refs_13_.refs_6_) | copy-start | bytes 688132
  56.2 1.8 %collective-permute-start.6 = (f32[8,13,8,128]{3,2,1,0:T(8,128)S(1)}, f32[8,13,8,128]{3,2,1,0:T(8,128)S(1)}, u32[]{:S(2)}, u32[]{:S(2)}) collective-permute-start(f32[8,13,8,128]{3,2,1,0:T(8,128)S(1)} %all-to-all-done.1.mine_ref), channel_id=1, source_target_pairs={{0,8},{8,0},{1,9},{9,1},{2,10},{10,2},{3,11},{11,3},{4,12},{12,4},... | collective-permute-start | bytes 1277960 | tf_op jit(solution)/shard_map/ppermute | solution.py:21
  58.0 3.4 %collective-permute-start.7 = (bf16[896,128]{1,0:T(8,128)(2,1)S(1)}, bf16[896,128]{1,0:T(8,128)(2,1)S(1)}, u32[]{:S(2)}, u32[]{:S(2)}) collective-permute-start(bf16[896,128]{1,0:T(8,128)(2,1)S(1)} %copy-done.13), channel_id=1, source_target_pairs={{0,8},{8,0},{1,9},{9,1},{2,10},{10,2},{3,11},{11,3},{4,12},{12,4},... | collective-permute-start | bytes 688136 | tf_op jit(solution)/shard_map/ppermute | solution.py:21
  58.2 4.0 %collective-permute-start.8 = (bf16[896,128]{1,0:T(8,128)(2,1)S(1)}, bf16[896,128]{1,0:T(8,128)(2,1)S(1)}, u32[]{:S(2)}, u32[]{:S(2)}) collective-permute-start(bf16[896,128]{1,0:T(8,128)(2,1)S(1)} %collective-permute-done.3.refs_13_.refs_6_), channel_id=1, source_target_pairs={{0,8},{8,0},{1,9},{9,1},{2,10},{10,2},{3,11},{11,3},{4,12},{12,4},... | collective-permute-start | bytes 688136 | tf_op jit(solution)/shard_map/ppermute | solution.py:21
  58.6 13.5 %collective-permute-start.9 = (bf16[896,128]{1,0:T(8,128)(2,1)S(1)}, bf16[896,128]{1,0:T(8,128)(2,1)S(1)}, u32[]{:S(2)}, u32[]{:S(2)}) collective-permute-start(bf16[896,128]{1,0:T(8,128)(2,1)S(1)} %collective-permute-done.4.refs_14_.refs_7_), channel_id=1, source_target_pairs={{0,8},{8,0},{1,9},{9,1},{2,10},{10,2},{3,11},{11,3},{4,12},{12,4},... | collective-permute-start | bytes 688136 | tf_op jit(solution)/shard_map/ppermute | solution.py:21
  58.7 13.4 %collective-permute-start.10 = (bf16[896,128]{1,0:T(8,128)(2,1)S(1)}, bf16[896,128]{1,0:T(8,128)(2,1)S(1)}, u32[]{:S(2)}, u32[]{:S(2)}) collective-permute-start(bf16[896,128]{1,0:T(8,128)(2,1)S(1)} %collective-permute-done.5.refs_15_.refs_8_), channel_id=1, source_target_pairs={{0,8},{8,0},{1,9},{9,1},{2,10},{10,2},{3,11},{11,3},{4,12},{12,4},... | collective-permute-start | bytes 688136 | tf_op jit(solution)/shard_map/ppermute | solution.py:21
  59.1 13.8 %collective-permute-start.13 = (bf16[896,128]{1,0:T(8,128)(2,1)S(1)}, bf16[896,128]{1,0:T(8,128)(2,1)S(1)}, u32[]{:S(2)}, u32[]{:S(2)}) collective-permute-start(bf16[896,128]{1,0:T(8,128)(2,1)S(1)} %collective-permute-done.2.refs_16_.refs_9_), channel_id=1, source_target_pairs={{0,3},{1,2},{2,1},{3,0},{4,7},{5,6},{6,5},{7,4},{8,11},{9,10},{10,... | collective-permute-start | bytes 688136 | tf_op jit(solution)/shard_map/ppermute | solution.py:21
  61.3 11.5 %collective-permute-start.12 = (bf16[896,128]{1,0:T(8,128)(2,1)S(1)}, bf16[896,128]{1,0:T(8,128)(2,1)S(1)}, u32[]{:S(2)}, u32[]{:S(2)}) collective-permute-start(bf16[896,128]{1,0:T(8,128)(2,1)S(1)} %collective-permute-done.2.refs_16_.refs_9_), channel_id=1, source_target_pairs={{0,2},{1,3},{2,0},{3,1},{4,6},{5,7},{6,4},{7,5},{8,10},{9,11},{10,... | collective-permute-start | bytes 688136 | tf_op jit(solution)/shard_map/ppermute | solution.py:21
  62.2 11.3 %collective-permute-start.11 = (bf16[896,128]{1,0:T(8,128)(2,1)S(1)}, bf16[896,128]{1,0:T(8,128)(2,1)S(1)}, u32[]{:S(2)}, u32[]{:S(2)}) collective-permute-start(bf16[896,128]{1,0:T(8,128)(2,1)S(1)} %collective-permute-done.2.refs_16_.refs_9_), channel_id=1, source_target_pairs={{0,1},{1,0},{2,3},{3,2},{4,5},{5,4},{6,7},{7,6},{8,9},{9,8},{10,11... | collective-permute-start | bytes 688136 | tf_op jit(solution)/shard_map/ppermute | solution.py:21
  73.5 6.3 %collective-permute-start.17 = (f32[4,7,8,128]{3,2,1,0:T(8,128)S(1)}, f32[4,7,8,128]{3,2,1,0:T(8,128)S(1)}, u32[]{:S(2)}, u32[]{:S(2)}) collective-permute-start(f32[4,7,8,128]{3,2,1,0:T(8,128)S(1)} %all_to_all.30.refs_0_), channel_id=1, source_target_pairs={{0,8},{8,0},{1,9},{9,1},{2,10},{10,2},{3,11},{11,3},{4,12},{12,4},... | collective-permute-start | bytes 344072 | tf_op jit(solution)/shard_map/ppermute | solution.py:21
  73.5 7.5 %collective-permute-start.16 = (f32[4,7,8,128]{3,2,1,0:T(8,128)S(1)}, f32[4,7,8,128]{3,2,1,0:T(8,128)S(1)}, u32[]{:S(2)}, u32[]{:S(2)}) collective-permute-start(f32[4,7,8,128]{3,2,1,0:T(8,128)S(1)} %all_to_all.30.refs_0_), channel_id=1, source_target_pairs={{0,48},{16,32},{32,16},{48,0},{1,49},{17,33},{33,17},{49,1},{2,50}... | collective-permute-start | bytes 344072 | tf_op jit(solution)/shard_map/ppermute | solution.py:21
  74.8 7.5 %collective-permute-start.15 = (f32[4,7,8,128]{3,2,1,0:T(8,128)S(1)}, f32[4,7,8,128]{3,2,1,0:T(8,128)S(1)}, u32[]{:S(2)}, u32[]{:S(2)}) collective-permute-start(f32[4,7,8,128]{3,2,1,0:T(8,128)S(1)} %all_to_all.30.refs_0_), channel_id=1, source_target_pairs={{0,32},{16,48},{32,0},{48,16},{1,33},{17,49},{33,1},{49,17},{2,34}... | collective-permute-start | bytes 344072 | tf_op jit(solution)/shard_map/ppermute | solution.py:21
  77.4 6.0 %collective-permute-start.14 = (f32[4,7,8,128]{3,2,1,0:T(8,128)S(1)}, f32[4,7,8,128]{3,2,1,0:T(8,128)S(1)}, u32[]{:S(2)}, u32[]{:S(2)}) collective-permute-start(f32[4,7,8,128]{3,2,1,0:T(8,128)S(1)} %all_to_all.30.refs_0_), channel_id=1, source_target_pairs={{0,16},{16,0},{32,48},{48,32},{1,17},{17,1},{33,49},{49,33},{2,18}... | collective-permute-start | bytes 344072 | tf_op jit(solution)/shard_map/ppermute | solution.py:21
  77.6 9.2 %collective-permute-start.23 = (f32[8,4,8,128]{3,2,1,0:T(8,128)S(1)}, f32[8,4,8,128]{3,2,1,0:T(8,128)S(1)}, u32[]{:S(2)}, u32[]{:S(2)}) collective-permute-start(f32[8,4,8,128]{3,2,1,0:T(8,128)S(1)} %get-tuple-element.77.refs_8_), channel_id=1, source_target_pairs={{0,3},{1,2},{2,1},{3,0},{4,7},{5,6},{6,5},{7,4},{8,11},{9,10},{10,... | collective-permute-start | bytes 393224 | tf_op jit(solution)/shard_map/ppermute | solution.py:21
  79.8 6.9 %collective-permute-start.22 = (f32[8,4,8,128]{3,2,1,0:T(8,128)S(1)}, f32[8,4,8,128]{3,2,1,0:T(8,128)S(1)}, u32[]{:S(2)}, u32[]{:S(2)}) collective-permute-start(f32[8,4,8,128]{3,2,1,0:T(8,128)S(1)} %get-tuple-element.77.refs_8_), channel_id=1, source_target_pairs={{0,2},{1,3},{2,0},{3,1},{4,6},{5,7},{6,4},{7,5},{8,10},{9,11},{10,... | collective-permute-start | bytes 393224 | tf_op jit(solution)/shard_map/ppermute | solution.py:21
  81.0 6.3 %collective-permute-start.20 = (f32[4,7,8,128]{3,2,1,0:T(8,128)S(1)}, f32[4,7,8,128]{3,2,1,0:T(8,128)S(1)}, u32[]{:S(2)}, u32[]{:S(2)}) collective-permute-start(f32[4,7,8,128]{3,2,1,0:T(8,128)S(1)} %collective-permute-done.16.refs_3_), channel_id=1, source_target_pairs={{0,8},{8,0},{1,9},{9,1},{2,10},{10,2},{3,11},{11,3},{4,12},{12,4},... | collective-permute-start | bytes 344072 | tf_op jit(solution)/shard_map/ppermute | solution.py:21
  82.2 5.2 %collective-permute-start.19 = (f32[4,7,8,128]{3,2,1,0:T(8,128)S(1)}, f32[4,7,8,128]{3,2,1,0:T(8,128)S(1)}, u32[]{:S(2)}, u32[]{:S(2)}) collective-permute-start(f32[4,7,8,128]{3,2,1,0:T(8,128)S(1)} %collective-permute-done.15.refs_2_), channel_id=1, source_target_pairs={{0,8},{8,0},{1,9},{9,1},{2,10},{10,2},{3,11},{11,3},{4,12},{12,4},... | collective-permute-start | bytes 344072 | tf_op jit(solution)/shard_map/ppermute | solution.py:21
  83.4 4.5 %collective-permute-start.18 = (f32[4,7,8,128]{3,2,1,0:T(8,128)S(1)}, f32[4,7,8,128]{3,2,1,0:T(8,128)S(1)}, u32[]{:S(2)}, u32[]{:S(2)}) collective-permute-start(f32[4,7,8,128]{3,2,1,0:T(8,128)S(1)} %collective-permute-done.14.refs_1_), channel_id=1, source_target_pairs={{0,8},{8,0},{1,9},{9,1},{2,10},{10,2},{3,11},{11,3},{4,12},{12,4},... | collective-permute-start | bytes 344072 | tf_op jit(solution)/shard_map/ppermute | solution.py:21
  86.8 10.7 %collective-permute-start.24 = (bf16[896,128]{1,0:T(8,128)(2,1)S(1)}, bf16[896,128]{1,0:T(8,128)(2,1)S(1)}, u32[]{:S(2)}, u32[]{:S(2)}) collective-permute-start(bf16[896,128]{1,0:T(8,128)(2,1)S(1)} %collective-permute-done.2.refs_16_.refs_9_), channel_id=1, source_target_pairs={{0,8},{8,0},{1,9},{9,1},{2,10},{10,2},{3,11},{11,3},{4,12},{12,4},... | collective-permute-start | bytes 688136 | tf_op jit(solution)/shard_map/ppermute | solution.py:21
  86.8 10.7 %collective-permute-start.25 = (bf16[896,128]{1,0:T(8,128)(2,1)S(1)}, bf16[896,128]{1,0:T(8,128)(2,1)S(1)}, u32[]{:S(2)}, u32[]{:S(2)}) collective-permute-start(bf16[896,128]{1,0:T(8,128)(2,1)S(1)} %collective-permute-done.11.refs_17_.refs_10_), channel_id=1, source_target_pairs={{0,8},{8,0},{1,9},{9,1},{2,10},{10,2},{3,11},{11,3},{4,12},{12,4},... | collective-permute-start | bytes 688136 | tf_op jit(solution)/shard_map/ppermute | solution.py:21
  87.3 10.2 %collective-permute-start.26 = (bf16[896,128]{1,0:T(8,128)(2,1)S(1)}, bf16[896,128]{1,0:T(8,128)(2,1)S(1)}, u32[]{:S(2)}, u32[]{:S(2)}) collective-permute-start(bf16[896,128]{1,0:T(8,128)(2,1)S(1)} %collective-permute-done.12.refs_18_.refs_11_), channel_id=1, source_target_pairs={{0,8},{8,0},{1,9},{9,1},{2,10},{10,2},{3,11},{11,3},{4,12},{12,4},... | collective-permute-start | bytes 688136 | tf_op jit(solution)/shard_map/ppermute | solution.py:21
  87.4 10.1 %collective-permute-start.27 = (bf16[896,128]{1,0:T(8,128)(2,1)S(1)}, bf16[896,128]{1,0:T(8,128)(2,1)S(1)}, u32[]{:S(2)}, u32[]{:S(2)}) collective-permute-start(bf16[896,128]{1,0:T(8,128)(2,1)S(1)} %collective-permute-done.13.refs_19_.refs_12_), channel_id=1, source_target_pairs={{0,8},{8,0},{1,9},{9,1},{2,10},{10,2},{3,11},{11,3},{4,12},{12,4},... | collective-permute-start | bytes 688136 | tf_op jit(solution)/shard_map/ppermute | solution.py:21
  87.8 5.5 %collective-permute-start.21 = (f32[8,4,8,128]{3,2,1,0:T(8,128)S(1)}, f32[8,4,8,128]{3,2,1,0:T(8,128)S(1)}, u32[]{:S(2)}, u32[]{:S(2)}) collective-permute-start(f32[8,4,8,128]{3,2,1,0:T(8,128)S(1)} %get-tuple-element.77.refs_8_), channel_id=1, source_target_pairs={{0,1},{1,0},{2,3},{3,2},{4,5},{5,4},{6,7},{7,6},{8,9},{9,8},{10,11... | collective-permute-start | bytes 393224 | tf_op jit(solution)/shard_map/ppermute | solution.py:21
  93.3 15.6 %collective-permute-start.28 = (f32[4,16,896]{2,1,0:T(8,128)S(1)}, f32[4,16,896]{2,1,0:T(8,128)S(1)}, u32[]{:S(2)}, u32[]{:S(2)}) collective-permute-start(f32[4,16,896]{2,1,0:T(8,128)S(1)} %get-tuple-element.84), channel_id=1, source_target_pairs={{0,4},{4,0},{1,5},{5,1},{2,6},{6,2},{3,7},{7,3},{8,12},{12,8},{9,1... | collective-permute-start | bytes 688136 | tf_op jit(solution)/shard_map/ppermute | solution.py:21
  109.0 25.2 %all-to-all-start.3 = ((bf16[32,32,256]{2,1,0:T(8,128)(2,1)}), bf16[32,32,256]{2,1,0:T(8,128)(2,1)S(1)}, u32[]{:S(2)}, u32[]{:S(2)}) async-start(bf16[32,32,256]{2,1,0:T(8,128)(2,1)} %get-tuple-element.96.refs_0_), calls=%async_computation.3 | async-start | bytes 1048576 | tf_op jit(solution)/shard_map/all_to_all | solution.py:439
  117.4 10.6 %collective-permute-start.29 = (f32[2,16,896]{2,1,0:T(8,128)S(1)}, f32[2,16,896]{2,1,0:T(8,128)S(1)}, u32[]{:S(2)}, u32[]{:S(2)}) collective-permute-start(f32[2,16,896]{2,1,0:T(8,128)S(1)} %get-tuple-element.88), channel_id=1, source_target_pairs={{0,1},{1,0},{2,3},{3,2},{4,5},{5,4},{6,7},{7,6},{8,9},{9,8},{10,11... | collective-permute-start | bytes 344072 | tf_op jit(solution)/shard_map/ppermute | solution.py:21
  118.1 10.0 %collective-permute-start.30 = (f32[2,16,896]{2,1,0:T(8,128)S(1)}, f32[2,16,896]{2,1,0:T(8,128)S(1)}, u32[]{:S(2)}, u32[]{:S(2)}) collective-permute-start(f32[2,16,896]{2,1,0:T(8,128)S(1)} %get-tuple-element.89), channel_id=1, source_target_pairs={{0,2},{1,3},{2,0},{3,1},{4,6},{5,7},{6,4},{7,5},{8,10},{9,11},{10,... | collective-permute-start | bytes 344072 | tf_op jit(solution)/shard_map/ppermute | solution.py:21
  121.2 6.9 %collective-permute-start.31 = (f32[2,16,896]{2,1,0:T(8,128)S(1)}, f32[2,16,896]{2,1,0:T(8,128)S(1)}, u32[]{:S(2)}, u32[]{:S(2)}) collective-permute-start(f32[2,16,896]{2,1,0:T(8,128)S(1)} %get-tuple-element.90), channel_id=1, source_target_pairs={{0,3},{1,2},{2,1},{3,0},{4,7},{5,6},{6,5},{7,4},{8,11},{9,10},{10,... | collective-permute-start | bytes 344072 | tf_op jit(solution)/shard_map/ppermute | solution.py:21
  134.1 17.0 %all-to-all-start.4 = ((f32[16,8,896]{2,1,0:T(8,128)}), f32[16,8,896]{2,1,0:T(8,128)S(1)}, u32[]{:S(2)}, u32[]{:S(2)}) async-start(f32[16,8,896]{2,1,0:T(8,128)} %back.1), calls=%async_computation.4 | async-start | bytes 917504 | tf_op jit(solution)/shard_map/all_to_all | solution.py:446
  139.0 24.9 %collective-permute-start.38 = (bf16[32,32,256]{2,1,0:T(8,128)(2,1)S(1)}, bf16[32,32,256]{2,1,0:T(8,128)(2,1)S(1)}, u32[]{:S(2)}, u32[]{:S(2)}) collective-permute-start(bf16[32,32,256]{2,1,0:T(8,128)(2,1)S(1)} %all-to-all-done.3.refs_0_), channel_id=1, source_target_pairs={{0,3},{1,2},{2,1},{3,0},{4,7},{5,6},{6,5},{7,4},{8,11},{9,10},{10,... | collective-permute-start | bytes 1572872 | tf_op jit(solution)/shard_map/ppermute | solution.py:21
  141.2 22.7 %collective-permute-start.37 = (bf16[32,32,256]{2,1,0:T(8,128)(2,1)S(1)}, bf16[32,32,256]{2,1,0:T(8,128)(2,1)S(1)}, u32[]{:S(2)}, u32[]{:S(2)}) collective-permute-start(bf16[32,32,256]{2,1,0:T(8,128)(2,1)S(1)} %all-to-all-done.3.refs_0_), channel_id=1, source_target_pairs={{0,2},{1,3},{2,0},{3,1},{4,6},{5,7},{6,4},{7,5},{8,10},{9,11},{10,... | collective-permute-start | bytes 1572872 | tf_op jit(solution)/shard_map/ppermute | solution.py:21
  141.9 22.9 %collective-permute-start.36 = (bf16[32,32,256]{2,1,0:T(8,128)(2,1)S(1)}, bf16[32,32,256]{2,1,0:T(8,128)(2,1)}, u32[]{:S(2)}, u32[]{:S(2)}) collective-permute-start(bf16[32,32,256]{2,1,0:T(8,128)(2,1)S(1)} %all-to-all-done.3.refs_0_), channel_id=1, source_target_pairs={{0,1},{1,0},{2,3},{3,2},{4,5},{5,4},{6,7},{7,6},{8,9},{9,8},{10,11... | collective-permute-start | bytes 1572872 | tf_op jit(solution)/shard_map/ppermute | solution.py:21
  143.1 1.3 collective-permute-start.32
  143.1 1.5 collective-permute-start.33
  144.4 1.3 collective-permute-start.34
  144.6 1.3 collective-permute-start.35
  151.8 19.7 %all-to-all-start.5 = ((f32[8,8,128]{2,1,0:T(8,128)}), f32[8,8,128]{2,1,0:T(8,128)S(1)}, u32[]{:S(2)}, u32[]{:S(2)}) async-start(f32[8,8,128]{2,1,0:T(8,128)} %total.1), calls=%async_computation.5 | async-start | bytes 65536 | tf_op jit(solution)/shard_map/all_to_all | solution.py:448
  (28 other events, 457.7 us)
